TPU v7x, 768 devices: a whole 4x8x12 slice. The times are simulated.
768 devices in a mesh: etp: 8 (over y), ep: 96 (over z, x, core).
Axes of the slice: x: 4, y: 8, z: 12, core: 2. Of those that a mesh axis runs over, the one named last changes fastest.
Arguments:
- tokens: bfloat16 [1536, 4096], P('ep', 'etp'), may hold values from -6 to 6
- routes: int32 [1536, 8], P('ep'), may hold values from 0 to 95, all different within a row; in each aligned block of 16 rows (0 to 15, 16 to 31, ...) at most 2 rows name the same one
- route_weight: float32 [1536, 8], P('ep'), may hold values from 0.1 to 1
- grad_out: bfloat16 [1536, 4096], P('ep', 'etp'), may hold values from -6 to 6
- w_gate: bfloat16 [96, 4096, 1536], P('ep', None, 'etp'), may hold values from -0.09375 to 0.09375
- w_up: bfloat16 [96, 4096, 1536], P('ep', None, 'etp'), may hold values from -0.09375 to 0.09375
- w_down: bfloat16 [96, 1536, 4096], P('ep', 'etp'), may hold values from -0.15625 to 0.15625
Outputs:
- mixed: bfloat16 [1536, 4096], P('ep', 'etp')
- grad_tokens: bfloat16 [1536, 4096], P('ep', 'etp')
Inputs may be any that keep to these rules, and one draw needn't show every extreme that they name: `routes`: each row names 8 different experts. Among the rows of one index of ep, no expert is named more than 2 times, a bound that some block reaches.
All inputs are finite; a program needn't handle non-finite values.
Results may differ from a plain program's by a relative error of at most 0.0064.
Values may be sent and summed in bfloat16 or wider, within the bound.
No kernel may reach another device: no remote copies, remote signals or barrier semaphores. Data moves between devices by JAX's collectives and lax.ppermute only.
A program may use at most 64 MiB of HBM per device.

v0:
```python
import jax
import jax.numpy as jnp
from jax import lax
from jax.sharding import PartitionSpec as P


def contract_first(left, right):
    return lax.dot_general(
        left, right, (((0,), (0,)), ((), ())), preferred_element_type=jnp.float32
    )


def contract_last(left, right):
    return lax.dot_general(
        left, right, (((1,), (1,)), ((), ())), preferred_element_type=jnp.float32
    )


def on_device(tokens, routes, route_weight, grad_out, w_gate, w_up, w_down):
    owners = lax.axis_size("ep")
    tok_rows, local_width = tokens.shape
    top_count = routes.shape[1]
    capacity = min(tok_rows, max(2, (3 * tok_rows * top_count + 2 * owners - 1) // (2 * owners)))
    slot_count = owners * capacity
    chosen = routes.reshape(-1)
    onehot = (chosen[:, None] == jnp.arange(owners, dtype=jnp.int32)[None, :]).astype(jnp.int32)
    earlier = jnp.cumsum(onehot, axis=0) - onehot
    within = jnp.sum(earlier * onehot, axis=1)
    target = chosen * capacity + within
    select = (jnp.arange(slot_count, dtype=jnp.int32)[:, None] == target[None, :]).astype(
        jnp.bfloat16
    )
    token_pairs = jnp.repeat(tokens, top_count, axis=0)
    weight_pairs = route_weight.reshape(-1)
    grad_pairs = (
        weight_pairs[:, None] * jnp.repeat(grad_out, top_count, axis=0).astype(jnp.float32)
    ).astype(jnp.bfloat16)
    token_buffer = jnp.dot(select, token_pairs, preferred_element_type=jnp.float32).astype(
        jnp.bfloat16
    )
    grad_buffer = jnp.dot(select, grad_pairs, preferred_element_type=jnp.float32).astype(
        jnp.bfloat16
    )
    token_buffer = token_buffer.reshape(owners, capacity, local_width)
    grad_buffer = grad_buffer.reshape(owners, capacity, local_width)
    token_recv, grad_recv = (
        lax.all_to_all(token_buffer, "ep", split_axis=0, concat_axis=0, tiled=True),
        lax.all_to_all(grad_buffer, "ep", split_axis=0, concat_axis=0, tiled=True),
    )
    token_recv = token_recv.reshape(slot_count, local_width)
    grad_recv = grad_recv.reshape(slot_count, local_width)
    token_slots, grad_slots = (
        lax.all_gather(token_recv, "etp", axis=1, tiled=True),
        lax.all_gather(grad_recv, "etp", axis=1, tiled=True),
    )
    gate_weight = w_gate[0]
    up_weight = w_up[0]
    down_weight = w_down[0]
    gate_pre = jnp.dot(token_slots, gate_weight, preferred_element_type=jnp.float32)
    up_pre = jnp.dot(token_slots, up_weight, preferred_element_type=jnp.float32)
    squash = jax.nn.sigmoid(gate_pre)
    active = gate_pre * squash
    hidden = (active * up_pre).astype(jnp.bfloat16)
    hidden_grad = contract_last(grad_slots, down_weight)
    up_grad = (hidden_grad * active).astype(jnp.bfloat16)
    gate_grad = (hidden_grad * up_pre * squash * (1.0 + gate_pre * (1.0 - squash))).astype(
        jnp.bfloat16
    )
    out_part = jnp.dot(hidden, down_weight, preferred_element_type=jnp.float32)
    input_part = contract_last(gate_grad, gate_weight) + contract_last(up_grad, up_weight)
    out_local, input_local = (
        lax.psum_scatter(out_part, "etp", scatter_dimension=1, tiled=True),
        lax.psum_scatter(input_part, "etp", scatter_dimension=1, tiled=True),
    )
    out_send = out_local.astype(jnp.bfloat16).reshape(owners, capacity, local_width)
    input_send = input_local.astype(jnp.bfloat16).reshape(owners, capacity, local_width)
    out_back, input_back = (
        lax.all_to_all(out_send, "ep", split_axis=0, concat_axis=0, tiled=True),
        lax.all_to_all(input_send, "ep", split_axis=0, concat_axis=0, tiled=True),
    )
    out_rows = contract_first(select, out_back.reshape(slot_count, local_width))
    input_rows = contract_first(select, input_back.reshape(slot_count, local_width))
    out_rows = out_rows.reshape(tok_rows, top_count, local_width)
    input_rows = input_rows.reshape(tok_rows, top_count, local_width)
    mixed = jnp.sum(route_weight[:, :, None] * out_rows, axis=1).astype(jnp.bfloat16)
    grad_tokens = jnp.sum(input_rows, axis=1).astype(jnp.bfloat16)
    return (mixed, grad_tokens)


def solution(mesh):
    in_specs = (
        P("ep", "etp"),
        P("ep", None),
        P("ep", None),
        P("ep", "etp"),
        P("ep", None, "etp"),
        P("ep", None, "etp"),
        P("ep", "etp", None),
    )
    out_specs = (P("ep", "etp"), P("ep", "etp"))
    return jax.shard_map(
        on_device, mesh=mesh, in_specs=in_specs, out_specs=out_specs, check_vma=False
    )
```

profile of v0, /device:TPU:1, one launch (start us, length us, event | category | flops | bytes accessed | tf_op | source)
XLA Modules:
  0.0 280.3 jit_solution(4056784469805328214)
XLA Ops:
  7.2 0.0 copy-start
  7.2 0.0 all-gather.3.cloned.1.call-start
  7.2 0.9 copy.13
  8.1 0.1 reshape.87
  8.2 0.1 fusion.25
  8.3 0.2 reduce_window_sum.11
  8.5 0.2 select_reduce_fusion
  8.7 0.9 convolution_convert_fusion.1
  9.6 0.1 reshape.89
  9.7 36.3 %all_to_all.20 = bf16[96,2,512]{2,1,0:T(2,128)(2,1)S(1)} all-to-all(bf16[96,2,512]{2,1,0:T(2,128)(2,1)S(1)} %reshape.89), channel_id=1, replica_groups=mesh['etp'=8,'ep'=96] {'ep'}, dimensions={0} | all-to-all | bytes 393216 | tf_op jit(solution)/shard_map/all_to_all | solution.py:47
  46.0 0.8 reshape.90
  46.8 0.0 all-gather.3.cloned.1.call-update
  46.8 0.0 all-gather.5.cloned.1.call-start
  46.9 0.1 copy.12
  46.9 0.1 mul.59
  47.0 0.3 convolution_convert_fusion
  47.3 0.1 reshape.93
  47.4 21.6 %all_to_all.21 = bf16[96,2,512]{2,1,0:T(2,128)(2,1)S(1)} all-to-all(bf16[96,2,512]{2,1,0:T(2,128)(2,1)S(1)} %reshape.93), channel_id=1, replica_groups=mesh['etp'=8,'ep'=96] {'ep'}, dimensions={0} | all-to-all | bytes 393216 | tf_op jit(solution)/shard_map/all_to_all | solution.py:48
  69.0 0.8 reshape.94
  69.7 0.0 all-gather.5.cloned.1.call-update
  69.8 0.0 copy-start.2
  69.8 0.0 reduce-scatter.3.cloned.1.call-start
  69.8 11.1 %all-gather.3.cloned.1.call-done = bf16[192,4096]{1,0:T(8,128)(2,1)} async-done(((bf16[192,512]{1,0:T(8,128)(2,1)}), bf16[192,4096]{1,0:T(8,128)(2,1)}) %all-gather.3.cloned.1.call-update) | async-done | bytes 1572880 | tf_op jit(solution)/shard_map/all_gather | solution.py:53
  80.9 2.6 fusion.5
  83.5 0.6 fusion.9
  84.1 2.2 fusion.2
  86.3 0.0 reduce-scatter.3.cloned.1.call-update
  86.4 0.0 reduce-scatter.5.cloned.1.call-start
  86.4 41.2 %all-gather.5.cloned.1.call-done = bf16[192,4096]{1,0:T(8,128)(2,1)} async-done(((bf16[192,512]{1,0:T(8,128)(2,1)}), bf16[192,4096]{1,0:T(8,128)(2,1)}) %all-gather.5.cloned.1.call-update) | async-done | bytes 1572880 | tf_op jit(solution)/shard_map/all_gather | solution.py:54
  127.6 2.0 fusion
  129.6 0.0 copy-start.3
  129.6 0.6 fusion.7
  130.2 0.8 copy-done.3
  131.0 2.3 convolution_add_fusion
  133.3 0.0 reduce-scatter.5.cloned.1.call-update
  133.3 49.4 %reduce-scatter.3.cloned.1.call-done = f32[192,512]{1,0:T(8,128)} async-done(((f32[192,4096]{1,0:T(8,128)}), f32[192,512]{1,0:T(8,128)}) %reduce-scatter.3.cloned.1.call-update) | async-done | bytes 393232 | tf_op jit(solution)/shard_map/reduce_scatter | solution.py:72
  182.7 1.0 convert_element_type.44
  183.7 0.8 reshape.91
  184.5 17.1 %all-to-all-start.1 = ((bf16[96,2,512]{2,1,0:T(2,128)(2,1)}), bf16[96,2,512]{2,1,0:T(2,128)(2,1)S(1)}, u32[]{:S(2)}, u32[]{:S(2)}) async-start(bf16[96,2,512]{2,1,0:T(2,128)(2,1)} %reshape.91), calls=%async_computation.2 | async-start | bytes 393216 | tf_op jit(solution)/shard_map/all_to_all | solution.py:78
  201.6 35.8 %reduce-scatter.5.cloned.1.call-done = f32[192,512]{1,0:T(8,128)} async-done(((f32[192,4096]{1,0:T(8,128)}), f32[192,512]{1,0:T(8,128)}) %reduce-scatter.5.cloned.1.call-update) | async-done | bytes 393232 | tf_op jit(solution)/shard_map/reduce_scatter | solution.py:73
  237.5 1.0 convert_element_type.52
  238.5 0.8 reshape.95
  239.2 17.1 %all-to-all-start.3 = ((bf16[96,2,512]{2,1,0:T(2,128)(2,1)}), bf16[96,2,512]{2,1,0:T(2,128)(2,1)S(1)}, u32[]{:S(2)}, u32[]{:S(2)}) async-start(bf16[96,2,512]{2,1,0:T(2,128)(2,1)} %reshape.95), calls=%async_computation.5 | async-start | bytes 393216 | tf_op jit(solution)/shard_map/all_to_all | solution.py:79
  256.3 0.1 reshape.97
  256.4 0.9 fusion.11
  257.3 15.6 %all-to-all-done.3 = bf16[96,2,512]{2,1,0:T(2,128)(2,1)S(1)} async-done(((bf16[96,2,512]{2,1,0:T(2,128)(2,1)}), bf16[96,2,512]{2,1,0:T(2,128)(2,1)S(1)}, u32[]{:S(2)}, u32[]{:S(2)}) %all-to-all-start.3) | async-done | bytes 196640 | tf_op jit(solution)/shard_map/all_to_all | solution.py:79
  272.8 0.1 reshape.98
  272.9 0.9 convolution_reduce_fusion
  (11 shorter events, 0.0 us)
Async XLA Ops:
  7.2 76.9 %copy-start = (bf16[1,192,4096]{2,1,0:T(8,128)(2,1)S(1)}, bf16[1,192,4096]{2,1,0:T(8,128)(2,1)}, u32[]{:S(2)}) copy-start(bf16[1,192,4096]{2,1,0:T(8,128)(2,1)} %param.13) | copy-start | bytes 4718596
  7.2 39.7 %copy-start.5 = (f32[16,8]{0,1:T(8,128)S(1)}, f32[16,8]{0,1:T(8,128)}, u32[]{:S(2)}) copy-start(f32[16,8]{0,1:T(8,128)} %param.9) | copy-start | bytes 1540
  7.2 39.8 %copy-start.4 = (bf16[16,512]{1,0:T(8,128)(2,1)S(1)}, bf16[16,512]{1,0:T(8,128)(2,1)}, u32[]{:S(2)}) copy-start(bf16[16,512]{1,0:T(8,128)(2,1)} %param.10) | copy-start | bytes 49156
  7.2 73.7 %all-gather.3.cloned.1.call-start = ((), (), s32[]{:S(2)}) async-start(), calls=%async_computation.6 | async-start | bytes 1769472 | tf_op jit(solution)/shard_map/all_gather | solution.py:53
  46.8 80.8 %all-gather.5.cloned.1.call-start = ((), (), s32[]{:S(2)}) async-start(), calls=%async_computation.8 | async-start | bytes 1769472 | tf_op jit(solution)/shard_map/all_gather | solution.py:54
  69.8 13.7 %copy-start.2 = (bf16[1,4096,192]{1,2,0:T(8,128)(2,1)S(1)}, bf16[1,4096,192]{1,2,0:T(8,128)(2,1)}, u32[]{:S(2)}) copy-start(bf16[1,4096,192]{1,2,0:T(8,128)(2,1)} %param.11) | copy-start | bytes 4718596
  69.8 113.0 %reduce-scatter.3.cloned.1.call-start = ((), (), s32[]{:S(2)}) async-start(), calls=%async_computation.7 | async-start | bytes 3538944 | tf_op jit(solution)/shard_map/reduce_scatter | solution.py:72
  80.9 2.6 copy-start.1
  86.4 151.1 %reduce-scatter.5.cloned.1.call-start = ((), (), s32[]{:S(2)}) async-start(), calls=%async_computation.9 | async-start | bytes 3538944 | tf_op jit(solution)/shard_map/reduce_scatter | solution.py:73
  129.6 1.4 copy-start.3
  184.5 54.7 %all-to-all-start.1 = ((bf16[96,2,512]{2,1,0:T(2,128)(2,1)}), bf16[96,2,512]{2,1,0:T(2,128)(2,1)S(1)}, u32[]{:S(2)}, u32[]{:S(2)}) async-start(bf16[96,2,512]{2,1,0:T(2,128)(2,1)} %reshape.91), calls=%async_computation.2 | async-start | bytes 393216 | tf_op jit(solution)/shard_map/all_to_all | solution.py:78
  239.2 33.6 %all-to-all-start.3 = ((bf16[96,2,512]{2,1,0:T(2,128)(2,1)}), bf16[96,2,512]{2,1,0:T(2,128)(2,1)S(1)}, u32[]{:S(2)}, u32[]{:S(2)}) async-start(bf16[96,2,512]{2,1,0:T(2,128)(2,1)} %reshape.95), calls=%async_computation.5 | async-start | bytes 393216 | tf_op jit(solution)/shard_map/all_to_all | solution.py:79
Sparse Core Ops, SparseCore 0:
  46.9 33.9 all-gather.2
  83.3 44.2 all-gather.4
  130.7 51.9 reduce-scatter.2
  185.7 51.6 reduce-scatter.4
where the time goes:
time: 281 us; the launch traced here: 280 us
  waiting for transfers between devices  153 us (54%)
  blocking collectives  57.9 us (21%)
  starting transfers between devices  34.3 us (12%)
  between operations  14 us (5%)
  matrix products  13.2 us (5%)
  local copies, waits for them, and re-layouts  5.3 us (2%)
    reduce_scatter x1, waiting for transfers between devices, on_device(): lax.psum_scatter(out_part, 'etp', scatter_dimension=1, tiled=True)  49.4 us
    all_gather x1, waiting for transfers between devices, on_device(): lax.all_gather(grad_recv, 'etp', axis=1, tiled=True)  41.2 us
    all_to_all x1, blocking collectives, on_device(): lax.all_to_all(token_buffer, 'ep', split_axis=0, concat_axis=0, tiled=True)  36.3 us
    reduce_scatter x1, waiting for transfers between devices, on_device(): lax.psum_scatter(input_part, 'etp', scatter_dimension=1, tiled=True)  35.8 us
    all_to_all x1, blocking collectives, on_device(): lax.all_to_all(grad_buffer, 'ep', split_axis=0, concat_axis=0, tiled=True)  21.6 us
    all_to_all x1, starting transfers between devices, on_device(): lax.all_to_all(out_send, 'ep', split_axis=0, concat_axis=0, tiled=True)  17.1 us
    all_to_all x1, starting transfers between devices, on_device(): lax.all_to_all(input_send, 'ep', split_axis=0, concat_axis=0, tiled=True)  17.1 us
    all_to_all x1, waiting for transfers between devices, on_device(): lax.all_to_all(input_send, 'ep', split_axis=0, concat_axis=0, tiled=True)  15.6 us
  transfers between devices with their start and end apart: 6, of which 5 were waited for; matrix products, arithmetic and copies ran while one was open for 6% of the time, Pallas kernels for 0%

commit v1 on v0

v1 whole, which is shorter than its diff:
```python
import jax
import jax.numpy as jnp
from jax import lax
from jax.sharding import PartitionSpec as P

bf16 = jnp.bfloat16
f32 = jnp.float32


def contract_last(left, right):
    return lax.dot_general(left, right, (((1,), (1,)), ((), ())), preferred_element_type=f32)


def on_device(tokens, routes, route_weight, grad_out, w_gate, w_up, w_down):
    owners = lax.axis_size("ep")
    tok_rows, local_width = tokens.shape
    top_count = routes.shape[1]
    capacity = min(tok_rows, max(2, (3 * tok_rows * top_count + 2 * owners - 1) // (2 * owners)))
    slots = owners * capacity
    chosen = routes.reshape(-1)
    onehot = (chosen[:, None] == jnp.arange(owners, dtype=jnp.int32)[None, :]).astype(jnp.int32)
    earlier = jnp.cumsum(onehot, axis=0) - onehot
    within = jnp.sum(earlier * onehot, axis=1)
    target = chosen * (2 * capacity) + within
    rows = jnp.arange(2 * slots, dtype=jnp.int32)
    pick_token = (rows[:, None] == target[None, :]).astype(bf16)
    pick_grad = (rows[:, None] == target[None, :] + capacity).astype(bf16)
    token_pairs = jnp.repeat(tokens, top_count, axis=0)
    grad_pairs = (
        route_weight.reshape(-1)[:, None] * jnp.repeat(grad_out, top_count, axis=0).astype(f32)
    ).astype(bf16)
    send = jnp.dot(
        jnp.concatenate([pick_token, pick_grad], axis=1),
        jnp.concatenate([token_pairs, grad_pairs], axis=0),
        preferred_element_type=f32,
    ).astype(bf16)
    recv = lax.all_to_all(
        send.reshape(owners, 2 * capacity, local_width), "ep", split_axis=0, concat_axis=0, tiled=True
    ).reshape(2 * slots, local_width)
    place = jnp.arange(2 * slots, dtype=jnp.int32)
    kind, slot = place // slots, place % slots
    source = (slot // capacity) * (2 * capacity) + kind * capacity + slot % capacity
    sort = (source[:, None] == rows[None, :]).astype(bf16)
    sorted_rows = jnp.dot(sort, recv, preferred_element_type=f32).astype(bf16)
    full = lax.all_gather(sorted_rows, "etp", axis=1, tiled=True)
    token_slots, grad_slots = full[:slots], full[slots:]
    gate_weight, up_weight, down_weight = w_gate[0], w_up[0], w_down[0]
    gate_pre = jnp.dot(token_slots, gate_weight, preferred_element_type=f32)
    up_pre = jnp.dot(token_slots, up_weight, preferred_element_type=f32)
    squash = jax.nn.sigmoid(gate_pre)
    active = gate_pre * squash
    hidden = (active * up_pre).astype(bf16)
    hidden_grad = contract_last(grad_slots, down_weight)
    up_grad = (hidden_grad * active).astype(bf16)
    gate_grad = (hidden_grad * up_pre * squash * (1.0 + gate_pre * (1.0 - squash))).astype(bf16)
    out_part = jnp.dot(hidden, down_weight, preferred_element_type=f32)
    input_part = contract_last(gate_grad, gate_weight) + contract_last(up_grad, up_weight)
    part = jnp.concatenate([out_part.astype(bf16), input_part.astype(bf16)], axis=0)
    local = lax.psum_scatter(part, "etp", scatter_dimension=1, tiled=True)
    unsorted = lax.dot_general(
        sort, local, (((0,), (0,)), ((), ())), preferred_element_type=f32
    ).astype(bf16)
    back = lax.all_to_all(
        unsorted.reshape(owners, 2 * capacity, local_width), "ep", split_axis=0, concat_axis=0, tiled=True
    ).reshape(2 * slots, local_width)
    first = (((0,), (0,)), ((), ()))
    out_rows = lax.dot_general(pick_token, back, first, preferred_element_type=f32)
    input_rows = lax.dot_general(pick_grad, back, first, preferred_element_type=f32)
    out_rows = out_rows.reshape(tok_rows, top_count, local_width)
    input_rows = input_rows.reshape(tok_rows, top_count, local_width)
    mixed = jnp.sum(route_weight[:, :, None] * out_rows, axis=1).astype(bf16)
    grad_tokens = jnp.sum(input_rows, axis=1).astype(bf16)
    return (mixed, grad_tokens)


def solution(mesh):
    in_specs = (
        P("ep", "etp"),
        P("ep", None),
        P("ep", None),
        P("ep", "etp"),
        P("ep", None, "etp"),
        P("ep", None, "etp"),
        P("ep", "etp", None),
    )
    out_specs = (P("ep", "etp"), P("ep", "etp"))
    return jax.shard_map(
        on_device, mesh=mesh, in_specs=in_specs, out_specs=out_specs, check_vma=False
    )
```

time: 281 us -> 208 us (0.74)
  waiting for transfers between devices: 153 us -> 114 us
  blocking collectives: 57.9 us -> 38.3 us
  starting transfers between devices: 34.3 us -> 20.1 us
    reduce_scatter x2 -> x1, waiting for transfers between devices: 85.2 us -> 48.9 us  [on_device(): local = lax.psum_scatter(part, 'etp', scatter_dimension=1, tiled=True)]
    all_to_all x2 -> x1, blocking collectives: 57.9 us -> 38.3 us  [on_device(): lax.all_to_all(unsorted.reshape(owners, 2 * capacity, local_width), 'ep',...]
    all_to_all x2 -> x1, starting transfers between devices: 34.2 us -> 20 us  [on_device(): lax.all_to_all(send.reshape(owners, 2 * capacity, local_width), 'ep', spl...]
    all_gather x2 -> x1, waiting for transfers between devices: 52.2 us -> 43.6 us  [on_device(): full = lax.all_gather(sorted_rows, 'etp', axis=1, tiled=True)]
    all_to_all x2 -> x1, waiting for transfers between devices: 15.6 us -> 21.4 us  [on_device(): lax.all_to_all(send.reshape(owners, 2 * capacity, local_width), 'ep', spl...]
    dot_general x3, matrix products: 4.85 us -> 1.81 us  [contract_last(): lax.dot_general(left, right, (((1,), (1,)), ((), ())), preferred_element_...]
    dot_general x7 -> x8, matrix products: 8.35 us -> 9.79 us  [the longest x1 2.46 us: on_device(): gate_pre = jnp.dot(token_slots, gate_weight, preferred_element_type=f32)]
  transfers between devices with their start and end apart: 6 -> 3, of which waited for: 5 -> 3; matrix products, arithmetic and copies ran while one was open for 6% -> 0% of each run, Pallas kernels for 0% -> 0%
where the time goes in v1:
time: 208 us; the launch traced here: 207 us
  waiting for transfers between devices  114 us (55%)
  blocking collectives  38.3 us (18%)
  starting transfers between devices  20.1 us (10%)
  between operations  14.2 us (7%)
  matrix products  11.6 us (6%)
  local copies, waits for them, and re-layouts  5.78 us (3%)
  other arithmetic  3.35 us (2%)
    reduce_scatter x1, waiting for transfers between devices, on_device(): local = lax.psum_scatter(part, 'etp', scatter_dimension=1, tiled=True)  48.9 us
    all_gather x1, waiting for transfers between devices, on_device(): full = lax.all_gather(sorted_rows, 'etp', axis=1, tiled=True)  43.6 us
    all_to_all x1, blocking collectives, on_device(): lax.all_to_all(unsorted.reshape(owners, 2 * capacity, local_width), 'ep',...  38.3 us
    all_to_all x1, waiting for transfers between devices, on_device(): lax.all_to_all(send.reshape(owners, 2 * capacity, local_width), 'ep', spl...  21.4 us
    all_to_all x1, starting transfers between devices, on_device(): lax.all_to_all(send.reshape(owners, 2 * capacity, local_width), 'ep', spl...  20 us
  transfers between devices with their start and end apart: 3, of which 3 were waited for; matrix products, arithmetic and copies ran while one was open for 0% of the time, Pallas kernels for 0%

profile of v1, /device:TPU:1, one launch (start us, length us, event | category | flops | bytes accessed | tf_op | source)
XLA Modules:
  0.0 207.2 jit_solution(14663788232850854531)
XLA Ops:
  7.2 0.0 copy-start
  7.2 0.9 copy.13
  8.1 0.1 reshape.141
  8.1 0.1 fusion.32
  8.2 0.2 reduce_window_sum.11
  8.4 0.2 select_reduce_fusion
  8.6 0.8 copy.12
  9.4 0.1 mul.84
  9.5 0.7 convert_element_type.47
  10.2 0.7 broadcast_bitcast_fusion
  10.9 0.1 iota_compare_fusion.4
  11.0 0.1 fusion.23
  11.1 0.3 convolution_convert_fusion.3
  11.4 0.8 reshape.143
  12.2 20.0 %all-to-all-start = ((bf16[96,4,512]{2,1,0:T(4,128)(2,1)}), bf16[96,4,512]{2,1,0:T(4,128)(2,1)S(1)}, u32[]{:S(2)}, u32[]{:S(2)}) async-start(bf16[96,4,512]{2,1,0:T(4,128)(2,1)} %reshape.143), calls=%async_computation | async-start | bytes 786432 | tf_op jit(solution)/shard_map/all_to_all | solution.py:37
  32.2 0.0 all-gather.2.cloned.1.call-start
  32.3 21.4 %all-to-all-done = bf16[96,4,512]{2,1,0:T(4,128)(2,1)S(1)} async-done(((bf16[96,4,512]{2,1,0:T(4,128)(2,1)}), bf16[96,4,512]{2,1,0:T(4,128)(2,1)S(1)}, u32[]{:S(2)}, u32[]{:S(2)}) %all-to-all-start) | async-done | bytes 393248 | tf_op jit(solution)/shard_map/all_to_all | solution.py:37
  53.7 0.1 reshape.144
  53.8 1.2 convolution_convert_fusion.2
  54.9 0.0 all-gather.2.cloned.1.call-update
  55.0 0.0 copy-start.1
  55.0 0.0 reduce-scatter.2.cloned.1.call-start
  55.0 43.6 %all-gather.2.cloned.1.call-done = bf16[384,4096]{1,0:T(8,128)(2,1)} async-done(((bf16[384,512]{1,0:T(8,128)(2,1)}), bf16[384,4096]{1,0:T(8,128)(2,1)}) %all-gather.2.cloned.1.call-update) | async-done | bytes 3145744 | tf_op jit(solution)/shard_map/all_gather | solution.py:45
  98.6 2.5 %fusion.10 = f32[192,192]{1,0:T(8,128)S(1)} fusion(bf16[1,4096,192]{1,2,0:T(8,128)(2,1)} %param.11, bf16[384,4096]{1,0:T(8,128)(2,1)} %all-gather.2.cloned.1.call-done), kind=kOutput, calls=%fused_computation.13 | convolution fusion | flops 301989888 | bytes 3293184 | tf_op jit(solution)/shard_map/dot_general | solution.py:48
  101.1 0.0 copy-done.1
  101.1 2.0 fusion.6
  103.1 0.0 copy-done
  103.1 0.0 copy-start.3
  103.1 0.6 convolution_convert_fusion
  103.7 1.3 copy-done.3
  105.0 0.0 copy-start.2
  105.0 0.6 fusion.1
  105.6 0.8 copy-done.2
  106.4 0.6 fusion.8
  107.0 0.6 fusion
  107.6 2.0 pad_maximum_fusion
  109.7 0.0 reduce-scatter.2.cloned.1.call-update
  109.7 48.9 %reduce-scatter.2.cloned.1.call-done = bf16[384,512]{1,0:T(8,128)(2,1)} async-done(((bf16[384,4096]{1,0:T(8,128)(2,1)}), bf16[384,512]{1,0:T(8,128)(2,1)}) %reduce-scatter.2.cloned.1.call-update) | async-done | bytes 393232 | tf_op jit(solution)/shard_map/reduce_scatter | solution.py:59
  158.5 1.5 convolution_convert_fusion.1
  160.0 0.1 reshape.145
  160.1 38.3 %all_to_all.10 = bf16[96,4,512]{2,1,0:T(4,128)(2,1)S(1)} all-to-all(bf16[96,4,512]{2,1,0:T(4,128)(2,1)S(1)} %reshape.145), channel_id=1, replica_groups=mesh['etp'=8,'ep'=96] {'ep'}, dimensions={0} | all-to-all | bytes 786432 | tf_op jit(solution)/shard_map/all_to_all | solution.py:63
  198.4 0.1 reshape.147
  198.5 0.9 convolution_reduce_fusion
  199.4 0.9 fusion.14
  (2 shorter events, 0.0 us)
Async XLA Ops:
  7.2 95.9 %copy-start = (bf16[1,192,4096]{2,1,0:T(8,128)(2,1)S(1)}, bf16[1,192,4096]{2,1,0:T(8,128)(2,1)}, u32[]{:S(2)}) copy-start(bf16[1,192,4096]{2,1,0:T(8,128)(2,1)} %param.13) | copy-start | bytes 4718596
  12.2 41.5 %all-to-all-start = ((bf16[96,4,512]{2,1,0:T(4,128)(2,1)}), bf16[96,4,512]{2,1,0:T(4,128)(2,1)S(1)}, u32[]{:S(2)}, u32[]{:S(2)}) async-start(bf16[96,4,512]{2,1,0:T(4,128)(2,1)} %reshape.143), calls=%async_computation | async-start | bytes 786432 | tf_op jit(solution)/shard_map/all_to_all | solution.py:37
  32.2 66.4 %all-gather.2.cloned.1.call-start = ((), (), s32[]{:S(2)}) async-start(), calls=%async_computation.3 | async-start | bytes 3538944 | tf_op jit(solution)/shard_map/all_gather | solution.py:45
  55.0 46.1 %copy-start.1 = (bf16[1,4096,192]{1,2,0:T(8,128)(2,1)S(1)}, bf16[1,4096,192]{1,2,0:T(8,128)(2,1)}, u32[]{:S(2)}) copy-start(bf16[1,4096,192]{1,2,0:T(8,128)(2,1)} %param.12) | copy-start | bytes 4718596
  55.0 103.6 %reduce-scatter.2.cloned.1.call-start = ((), (), s32[]{:S(2)}) async-start(), calls=%async_computation.4 | async-start | bytes 3538944 | tf_op jit(solution)/shard_map/reduce_scatter | solution.py:59
  103.1 1.9 copy-start.3
  105.0 1.4 copy-start.2
Sparse Core Ops, SparseCore 0:
  55.1 43.4 all-gather.1
  109.8 48.6 reduce-scatter.1

commit v2 on v1

--- a/solution.py
+++ b/solution.py
@@ -1,18 +1,114 @@
 import jax
 import jax.numpy as jnp
 from jax import lax
+from jax.experimental import pallas as pl
+from jax.experimental.pallas import tpu as pltpu
 from jax.sharding import PartitionSpec as P
 
 bf16 = jnp.bfloat16
 f32 = jnp.float32
+VMEM = pl.BlockSpec(memory_space=pltpu.VMEM)
+VMEM_LIMIT = 28 * 1024 * 1024
 
 
-def contract_last(left, right):
+def dot_last(left, right):
     return lax.dot_general(left, right, (((1,), (1,)), ((), ())), preferred_element_type=f32)
 
 
+def dot(left, right):
+    return lax.dot_general(left, right, (((1,), (0,)), ((), ())), preferred_element_type=f32)
+
+
+def exchange(value, step):
+    size, owners = lax.axis_size("etp"), lax.axis_size("ep")
+    pairs = []
+    for y in range(size):
+        for j in range(owners):
+            sign = 1 if (y + j + step) % 2 == 0 else -1
+            pairs.append((y * owners + j, (y + sign) % size * owners + j))
+    return lax.ppermute(value, ("etp", "ep"), pairs)
+
+
+def gather_step(held, step):
+    if step == 0:
+        return [jnp.stack([held[0], exchange(held[0], 0)])]
+    return held + [exchange(held[-1], step)]
+
+
+def columns_of(steps, width):
+    size = 2 * steps
+    y = lax.axis_index("etp")
+    sign = 1 - 2 * lax.rem(y + lax.axis_index("ep"), 2)
+    out = []
+    for k in range(steps):
+        turn = sign if k % 2 == 0 else -sign
+        blocks = [lax.rem(y + turn * (k + b) + 2 * size, size) for b in (0, 1)]
+        out.append([pl.ds(pl.multiple_of(block * width, width), width) for block in blocks])
+    return out
+
+
+def forward_kernel(steps, *refs):
+    held, (gate_w, up_w, down_w) = refs[:steps], refs[steps : steps + 3]
+    gate_ref, up_ref = refs[steps + 3 : steps + 5]
+    parts = refs[steps + 5 :]
+    columns = columns_of(steps, held[0].shape[2])
+    gate = up = None
+    for k in range(steps):
+        for b in (0, 1):
+            rows = held[k][b]
+            gate_now = dot_last(rows, gate_w[:, columns[k][b]])
+            up_now = dot_last(rows, up_w[:, columns[k][b]])
+            gate = gate_now if gate is None else gate + gate_now
+            up = up_now if up is None else up + up_now
+    gate_ref[...] = gate
+    up_ref[...] = up
+    hidden = (gate * jax.nn.sigmoid(gate) * up).astype(bf16)
+    for k in reversed(range(steps)):
+        for b in (0, 1):
+            parts[k][b] = dot(hidden, down_w[:, columns[k][b]]).astype(parts[k].dtype)
+
+
+def backward_kernel(steps, *refs):
+    held, (gate_w, up_w, down_w) = refs[:steps], refs[steps : steps + 3]
+    gate_ref, up_ref = refs[steps + 3 : steps + 5]
+    parts = refs[steps + 5 :]
+    columns = columns_of(steps, held[0].shape[2])
+    hidden_grad = None
+    for k in range(steps):
+        for b in (0, 1):
+            now = dot_last(held[k][b], down_w[:, columns[k][b]])
+            hidden_grad = now if hidden_grad is None else hidden_grad + now
+    gate, up = gate_ref[...], up_ref[...]
+    squash = jax.nn.sigmoid(gate)
+    up_grad = (hidden_grad * (gate * squash)).astype(bf16)
+    gate_grad = (hidden_grad * up * squash * (1.0 + gate * (1.0 - squash))).astype(bf16)
+    for k in reversed(range(steps)):
+        for b in (0, 1):
+            part = dot(gate_grad, gate_w[:, columns[k][b]]) + dot(up_grad, up_w[:, columns[k][b]])
+            parts[k][b] = part.astype(parts[k].dtype)
+
+
+def call(kernel, steps, operands, extra_shapes, pair_shape, flops):
+    shapes = extra_shapes + [
+        jax.ShapeDtypeStruct(pair_shape, f32 if k < steps - 1 else bf16) for k in range(steps)
+    ]
+    return pl.pallas_call(
+        lambda *refs: kernel(steps, *refs),
+        out_shape=shapes,
+        in_specs=[VMEM] * len(operands),
+        out_specs=[VMEM] * len(shapes),
+        compiler_params=pltpu.CompilerParams(vmem_limit_bytes=VMEM_LIMIT),
+        cost_estimate=pl.CostEstimate(flops=flops, bytes_accessed=9 << 20, transcendentals=0),
+    )(*operands)
+
+
+def sum_step(parts, arrived, step):
+    received = exchange(arrived, step)
+    return (parts[step - 1] + received.astype(f32)).astype(bf16)
+
+
 def on_device(tokens, routes, route_weight, grad_out, w_gate, w_up, w_down):
-    owners = lax.axis_size("ep")
+    owners, steps = lax.axis_size("ep"), lax.axis_size("etp") // 2
     tok_rows, local_width = tokens.shape
     top_count = routes.shape[1]
     capacity = min(tok_rows, max(2, (3 * tok_rows * top_count + 2 * owners - 1) // (2 * owners)))
@@ -41,22 +137,30 @@
     kind, slot = place // slots, place % slots
     source = (slot // capacity) * (2 * capacity) + kind * capacity + slot % capacity
     sort = (source[:, None] == rows[None, :]).astype(bf16)
-    sorted_rows = jnp.dot(sort, recv, preferred_element_type=f32).astype(bf16)
-    full = lax.all_gather(sorted_rows, "etp", axis=1, tiled=True)
-    token_slots, grad_slots = full[:slots], full[slots:]
-    gate_weight, up_weight, down_weight = w_gate[0], w_up[0], w_down[0]
-    gate_pre = jnp.dot(token_slots, gate_weight, preferred_element_type=f32)
-    up_pre = jnp.dot(token_slots, up_weight, preferred_element_type=f32)
-    squash = jax.nn.sigmoid(gate_pre)
-    active = gate_pre * squash
-    hidden = (active * up_pre).astype(bf16)
-    hidden_grad = contract_last(grad_slots, down_weight)
-    up_grad = (hidden_grad * active).astype(bf16)
-    gate_grad = (hidden_grad * up_pre * squash * (1.0 + gate_pre * (1.0 - squash))).astype(bf16)
-    out_part = jnp.dot(hidden, down_weight, preferred_element_type=f32)
-    input_part = contract_last(gate_grad, gate_weight) + contract_last(up_grad, up_weight)
-    part = jnp.concatenate([out_part.astype(bf16), input_part.astype(bf16)], axis=0)
-    local = lax.psum_scatter(part, "etp", scatter_dimension=1, tiled=True)
+    token_held = [jnp.dot(sort[:slots], recv, preferred_element_type=f32).astype(bf16)]
+    grad_held = [jnp.dot(sort[slots:], recv, preferred_element_type=f32).astype(bf16)]
+    for step in range(steps):
+        token_held = gather_step(token_held, step)
+        grad_held = gather_step(grad_held, step)
+    gate_weight, up_weight, down_weight = w_gate[0].T, w_up[0].T, w_down[0]
+    weights = [gate_weight, up_weight, down_weight]
+    hidden_width, width = down_weight.shape
+    square = jax.ShapeDtypeStruct((slots, hidden_width), f32)
+    pair_shape = (2, slots, local_width)
+    flops = 2 * slots * hidden_width * width
+    gate, up, *out_parts = call(
+        forward_kernel, steps, token_held + weights, [square, square], pair_shape, 3 * flops
+    )
+    input_parts = call(
+        backward_kernel, steps, grad_held + weights + [gate, up], [], pair_shape, 3 * flops
+    )
+    out_sum, input_sum = out_parts[-1], input_parts[-1]
+    for step in reversed(range(1, steps)):
+        out_sum = sum_step(out_parts, out_sum, step)
+        input_sum = sum_step(input_parts, input_sum, step)
+    out_local = (out_sum[0].astype(f32) + exchange(out_sum[1], 0).astype(f32)).astype(bf16)
+    input_local = (input_sum[0].astype(f32) + exchange(input_sum[1], 0).astype(f32)).astype(bf16)
+    local = jnp.concatenate([out_local, input_local], axis=0)
     unsorted = lax.dot_general(
         sort, local, (((0,), (0,)), ((), ())), preferred_element_type=f32
     ).astype(bf16)

time: 208 us -> 191 us (0.918)
  starting transfers between devices: 20.1 us -> 69.7 us
  waiting for transfers between devices: 114 us -> 64.8 us
  between operations: 14.2 us -> 1.07 us
  matrix products: 11.6 us -> 4.8 us
  Pallas kernels: 0 us -> 3.84 us
    ppermute x0 -> x16, starting transfers between devices: none -> 49.4 us  [exchange(): return lax.ppermute(value, ('etp', 'ep'), pairs)]
    reduce_scatter x1 -> x0, waiting for transfers between devices: 48.9 us -> none  [on_device(): local = lax.psum_scatter(part, 'etp', scatter_dimension=1, tiled=True)]
    ppermute x0 -> x16, waiting for transfers between devices: none -> 45 us  [exchange(): return lax.ppermute(value, ('etp', 'ep'), pairs)]
    all_gather x1 -> x0, waiting for transfers between devices: 43.6 us -> none  [on_device(): full = lax.all_gather(sorted_rows, 'etp', axis=1, tiled=True)]
    dot_general x7 -> x2, matrix products: 8.01 us -> 2.21 us  [the longest x1 1.16 us: on_device(): jnp.dot(sort[:slots], recv, preferred_element_type=f32).astype(bf16)]
    pallas_call x0 -> x2, Pallas kernels: none -> 3.84 us  [call(): pl.pallas_call(lambda *refs: kernel(steps, *refs), out_shape=shapes, in_s...]
  transfers between devices with their start and end apart: 3 -> 17, of which waited for: 3 -> 14; matrix products, arithmetic and copies ran while one was open for 0% -> 1% of each run, Pallas kernels for 0% -> 2%
where the time goes in v2:
time: 191 us; the launch traced here: 190 us
  starting transfers between devices  69.7 us (36%)
  waiting for transfers between devices  64.8 us (34%)
  blocking collectives  38.1 us (20%)
  matrix products  4.8 us (3%)
  local copies, waits for them, and re-layouts  4.61 us (2%)
  Pallas kernels  3.84 us (2%)
  other arithmetic  3.03 us (2%)
    ppermute x16, starting transfers between devices, exchange(): return lax.ppermute(value, ('etp', 'ep'), pairs)  49.4 us
    ppermute x16, waiting for transfers between devices, exchange(): return lax.ppermute(value, ('etp', 'ep'), pairs)  45 us
    all_to_all x1, blocking collectives, on_device(): lax.all_to_all(unsorted.reshape(owners, 2 * capacity, local_width), 'ep',...  38.1 us
    all_to_all x1, starting transfers between devices, on_device(): lax.all_to_all(send.reshape(owners, 2 * capacity, local_width), 'ep', spl...  20.3 us
    all_to_all x1, waiting for transfers between devices, on_device(): lax.all_to_all(send.reshape(owners, 2 * capacity, local_width), 'ep', spl...  19.8 us
    pallas_call x2, Pallas kernels, call(): pl.pallas_call(lambda *refs: kernel(steps, *refs), out_shape=shapes, in_s...  3.84 us
  transfers between devices with their start and end apart: 17, of which 14 were waited for; matrix products, arithmetic and copies ran while one was open for 1% of the time, Pallas kernels for 2%

profile of v2, /device:TPU:1, one launch (start us, length us, event | category | flops | bytes accessed | tf_op | source)
XLA Modules:
  0.0 190.0 jit_solution(1039830138476410688)
XLA Ops:
  0.6 0.8 copy.13
  1.6 0.2 reduce_window_sum.11
  2.0 0.8 copy.12
  2.8 0.7 convert_element_type.95
  3.8 0.3 convolution_convert_fusion.1
  4.1 0.8 reshape.147
  4.9 20.3 %all-to-all-start = ((bf16[96,4,512]{2,1,0:T(4,128)(2,1)}), bf16[96,4,512]{2,1,0:T(4,128)(2,1)}, u32[]{:S(2)}, u32[]{:S(2)}) async-start(bf16[96,4,512]{2,1,0:T(4,128)(2,1)} %reshape.147), calls=%async_computation | async-start | bytes 786432 | tf_op jit(solution)/shard_map/all_to_all | solution.py:133
  25.3 0.6 copy-done.6
  25.9 0.8 iota_compare_fusion
  26.7 19.8 %all-to-all-done = bf16[96,4,512]{2,1,0:T(4,128)(2,1)} async-done(((bf16[96,4,512]{2,1,0:T(4,128)(2,1)}), bf16[96,4,512]{2,1,0:T(4,128)(2,1)}, u32[]{:S(2)}, u32[]{:S(2)}) %all-to-all-start) | async-done | bytes 393248 | tf_op jit(solution)/shard_map/all_to_all | solution.py:133
  46.5 1.2 reshape.148
  47.7 1.2 convolution_convert_fusion.3
  48.9 5.1 %collective-permute-start = (bf16[192,512]{1,0:T(8,128)(2,1)S(1)}, bf16[192,512]{1,0:T(8,128)(2,1)S(1)}, u32[]{:S(2)}, u32[]{:S(2)}) collective-permute-start(bf16[192,512]{1,0:T(8,128)(2,1)S(1)} %convolution_convert_fusion.3), channel_id=1, source_target_pairs={{0,96},{1,673},{2,98},{3,675},{4,100},{5,677},{6,102},{7,679},{8,1... | collective-permute-start | bytes 589832 | tf_op jit(solution)/shard_map/ppermute | solution.py:29
  54.0 3.0 %collective-permute-done = bf16[192,512]{1,0:T(8,128)(2,1)S(1)} collective-permute-done((bf16[192,512]{1,0:T(8,128)(2,1)S(1)}, bf16[192,512]{1,0:T(8,128)(2,1)S(1)}, u32[]{:S(2)}, u32[]{:S(2)}) %collective-permute-start) | collective-permute-done | bytes 196640 | tf_op jit(solution)/shard_map/ppermute | solution.py:29
  57.1 1.9 %collective-permute-start.1 = (bf16[2,192,512]{2,1,0:T(8,128)(2,1)S(1)}, bf16[2,192,512]{2,1,0:T(8,128)(2,1)S(1)}, u32[]{:S(2)}, u32[]{:S(2)}) collective-permute-start(bf16[2,192,512]{2,1,0:T(8,128)(2,1)S(1)} %pad_maximum_fusion.refs_0_), channel_id=1, source_target_pairs={{0,672},{1,97},{2,674},{3,99},{4,676},{5,101},{6,678},{7,103},{8,6... | collective-permute-start | bytes 1179656 | tf_op jit(solution)/shard_map/ppermute | solution.py:29
  59.0 1.0 convolution_convert_fusion.2
  60.1 4.7 %collective-permute-start.8 = (bf16[192,512]{1,0:T(8,128)(2,1)S(1)}, bf16[192,512]{1,0:T(8,128)(2,1)S(1)}, u32[]{:S(2)}, u32[]{:S(2)}) collective-permute-start(bf16[192,512]{1,0:T(8,128)(2,1)S(1)} %convolution_convert_fusion.2), channel_id=1, source_target_pairs={{0,96},{1,673},{2,98},{3,675},{4,100},{5,677},{6,102},{7,679},{8,1... | collective-permute-start | bytes 589832 | tf_op jit(solution)/shard_map/ppermute | solution.py:29
  64.8 5.5 %collective-permute-done.8 = bf16[192,512]{1,0:T(8,128)(2,1)S(1)} collective-permute-done((bf16[192,512]{1,0:T(8,128)(2,1)S(1)}, bf16[192,512]{1,0:T(8,128)(2,1)S(1)}, u32[]{:S(2)}, u32[]{:S(2)}) %collective-permute-start.8) | collective-permute-done | bytes 196640 | tf_op jit(solution)/shard_map/ppermute | solution.py:29
  70.3 2.3 %collective-permute-start.9 = (bf16[2,192,512]{2,1,0:T(8,128)(2,1)S(1)}, bf16[2,192,512]{2,1,0:T(8,128)(2,1)S(1)}, u32[]{:S(2)}, u32[]{:S(2)}) collective-permute-start(bf16[2,192,512]{2,1,0:T(8,128)(2,1)S(1)} %pad_maximum_fusion.1.refs_0_), channel_id=1, source_target_pairs={{0,672},{1,97},{2,674},{3,99},{4,676},{5,101},{6,678},{7,103},{8,6... | collective-permute-start | bytes 1179656 | tf_op jit(solution)/shard_map/ppermute | solution.py:29
  72.7 4.6 %collective-permute-start.2 = (bf16[2,192,512]{2,1,0:T(8,128)(2,1)S(1)}, bf16[2,192,512]{2,1,0:T(8,128)(2,1)S(1)}, u32[]{:S(2)}, u32[]{:S(2)}) collective-permute-start(bf16[2,192,512]{2,1,0:T(8,128)(2,1)S(1)} %collective-permute-done.1.refs_1_), channel_id=1, source_target_pairs={{0,96},{1,673},{2,98},{3,675},{4,100},{5,677},{6,102},{7,679},{8,1... | collective-permute-start | bytes 1179656 | tf_op jit(solution)/shard_map/ppermute | solution.py:29
  77.2 1.9 %collective-permute-done.9.refs_1_ = bf16[2,192,512]{2,1,0:T(8,128)(2,1)S(1)} collective-permute-done((bf16[2,192,512]{2,1,0:T(8,128)(2,1)S(1)}, bf16[2,192,512]{2,1,0:T(8,128)(2,1)S(1)}, u32[]{:S(2)}, u32[]{:S(2)}) %collective-permute-start.9) | collective-permute-done | bytes 393248 | tf_op jit(solution)/shard_map/ppermute | solution.py:29
  79.2 4.5 %collective-permute-start.10 = (bf16[2,192,512]{2,1,0:T(8,128)(2,1)S(1)}, bf16[2,192,512]{2,1,0:T(8,128)(2,1)S(1)}, u32[]{:S(2)}, u32[]{:S(2)}) collective-permute-start(bf16[2,192,512]{2,1,0:T(8,128)(2,1)S(1)} %collective-permute-done.9.refs_1_), channel_id=1, source_target_pairs={{0,96},{1,673},{2,98},{3,675},{4,100},{5,677},{6,102},{7,679},{8,1... | collective-permute-start | bytes 1179656 | tf_op jit(solution)/shard_map/ppermute | solution.py:29
  83.7 2.9 %collective-permute-done.2.refs_2_ = bf16[2,192,512]{2,1,0:T(8,128)(2,1)S(1)} collective-permute-done((bf16[2,192,512]{2,1,0:T(8,128)(2,1)S(1)}, bf16[2,192,512]{2,1,0:T(8,128)(2,1)S(1)}, u32[]{:S(2)}, u32[]{:S(2)}) %collective-permute-start.2) | collective-permute-done | bytes 393248 | tf_op jit(solution)/shard_map/ppermute | solution.py:29
  86.6 1.9 %collective-permute-start.3 = (bf16[2,192,512]{2,1,0:T(8,128)(2,1)S(1)}, bf16[2,192,512]{2,1,0:T(8,128)(2,1)S(1)}, u32[]{:S(2)}, u32[]{:S(2)}) collective-permute-start(bf16[2,192,512]{2,1,0:T(8,128)(2,1)S(1)} %collective-permute-done.2.refs_2_), channel_id=1, source_target_pairs={{0,672},{1,97},{2,674},{3,99},{4,676},{5,101},{6,678},{7,103},{8,6... | collective-permute-start | bytes 1179656 | tf_op jit(solution)/shard_map/ppermute | solution.py:29
  88.5 2.1 %collective-permute-done.10.refs_2_ = bf16[2,192,512]{2,1,0:T(8,128)(2,1)S(1)} collective-permute-done((bf16[2,192,512]{2,1,0:T(8,128)(2,1)S(1)}, bf16[2,192,512]{2,1,0:T(8,128)(2,1)S(1)}, u32[]{:S(2)}, u32[]{:S(2)}) %collective-permute-start.10) | collective-permute-done | bytes 393248 | tf_op jit(solution)/shard_map/ppermute | solution.py:29
  90.7 1.9 %collective-permute-start.11 = (bf16[2,192,512]{2,1,0:T(8,128)(2,1)S(1)}, bf16[2,192,512]{2,1,0:T(8,128)(2,1)S(1)}, u32[]{:S(2)}, u32[]{:S(2)}) collective-permute-start(bf16[2,192,512]{2,1,0:T(8,128)(2,1)S(1)} %collective-permute-done.10.refs_2_), channel_id=1, source_target_pairs={{0,672},{1,97},{2,674},{3,99},{4,676},{5,101},{6,678},{7,103},{8,6... | collective-permute-start | bytes 1179656 | tf_op jit(solution)/shard_map/ppermute | solution.py:29
  92.6 6.2 %collective-permute-done.3.refs_3_ = bf16[2,192,512]{2,1,0:T(8,128)(2,1)S(1)} collective-permute-done((bf16[2,192,512]{2,1,0:T(8,128)(2,1)S(1)}, bf16[2,192,512]{2,1,0:T(8,128)(2,1)S(1)}, u32[]{:S(2)}, u32[]{:S(2)}) %collective-permute-start.3) | collective-permute-done | bytes 393248 | tf_op jit(solution)/shard_map/ppermute | solution.py:29
  98.8 1.5 shard_map.86
  100.3 2.2 %collective-permute-start.4 = (bf16[2,192,512]{2,1,0:T(8,128)(2,1)S(1)}, bf16[2,192,512]{2,1,0:T(8,128)(2,1)S(1)}, u32[]{:S(2)}, u32[]{:S(2)}) collective-permute-start(bf16[2,192,512]{2,1,0:T(8,128)(2,1)S(1)} %get-tuple-element.15), channel_id=1, source_target_pairs={{0,672},{1,97},{2,674},{3,99},{4,676},{5,101},{6,678},{7,103},{8,6... | collective-permute-start | bytes 1179656 | tf_op jit(solution)/shard_map/ppermute | solution.py:29
  102.6 1.0 collective-permute-done.11.refs_3_
  103.6 2.3 %shard_map.87 = (f32[2,192,512]{2,1,0:T(8,128)S(1)}, f32[2,192,512]{2,1,0:T(8,128)S(1)}, f32[2,192,512]{2,1,0:T(8,128)S(1)}, bf16[2,192,512]{2,1,0:T(8,128)(2,1)S(1)}) custom-call(bf16[2,192,512]{2,1,0:T(8,128)(2,1)S(1)} %pad_maximum_fusion.1.refs_0_, bf16[2,192,512]{2,1,0:T(8,128)(2,1)S(1)} %collective-permute-done.9.refs_1_, ...), custom_call_target="tpu_custom_call" | custom-call | flops 905969664 | bytes 9437184 | tf_op jit(solution)/shard_map/pallas_call | solution.py:95
  105.9 2.1 %collective-permute-start.12 = (bf16[2,192,512]{2,1,0:T(8,128)(2,1)S(1)}, bf16[2,192,512]{2,1,0:T(8,128)(2,1)S(1)}, u32[]{:S(2)}, u32[]{:S(2)}) collective-permute-start(bf16[2,192,512]{2,1,0:T(8,128)(2,1)S(1)} %get-tuple-element.21), channel_id=1, source_target_pairs={{0,672},{1,97},{2,674},{3,99},{4,676},{5,101},{6,678},{7,103},{8,6... | collective-permute-start | bytes 1179656 | tf_op jit(solution)/shard_map/ppermute | solution.py:29
  108.0 1.2 collective-permute-done.4
  109.3 2.7 %collective-permute-start.5 = (bf16[2,192,512]{2,1,0:T(8,128)(2,1)S(1)}, bf16[2,192,512]{2,1,0:T(8,128)(2,1)S(1)}, u32[]{:S(2)}, u32[]{:S(2)}) collective-permute-start(bf16[2,192,512]{2,1,0:T(8,128)(2,1)S(1)} %add_convert_fusion.5), channel_id=1, source_target_pairs={{0,96},{1,673},{2,98},{3,675},{4,100},{5,677},{6,102},{7,679},{8,1... | collective-permute-start | bytes 1179656 | tf_op jit(solution)/shard_map/ppermute | solution.py:29
  112.0 2.7 %collective-permute-done.12 = bf16[2,192,512]{2,1,0:T(8,128)(2,1)S(1)} collective-permute-done((bf16[2,192,512]{2,1,0:T(8,128)(2,1)S(1)}, bf16[2,192,512]{2,1,0:T(8,128)(2,1)S(1)}, u32[]{:S(2)}, u32[]{:S(2)}) %collective-permute-start.12) | collective-permute-done | bytes 393248 | tf_op jit(solution)/shard_map/ppermute | solution.py:29
  114.8 2.0 %collective-permute-start.13 = (bf16[2,192,512]{2,1,0:T(8,128)(2,1)S(1)}, bf16[2,192,512]{2,1,0:T(8,128)(2,1)S(1)}, u32[]{:S(2)}, u32[]{:S(2)}) collective-permute-start(bf16[2,192,512]{2,1,0:T(8,128)(2,1)S(1)} %add_convert_fusion.2), channel_id=1, source_target_pairs={{0,96},{1,673},{2,98},{3,675},{4,100},{5,677},{6,102},{7,679},{8,1... | collective-permute-start | bytes 1179656 | tf_op jit(solution)/shard_map/ppermute | solution.py:29
  116.9 3.6 %collective-permute-done.5 = bf16[2,192,512]{2,1,0:T(8,128)(2,1)S(1)} collective-permute-done((bf16[2,192,512]{2,1,0:T(8,128)(2,1)S(1)}, bf16[2,192,512]{2,1,0:T(8,128)(2,1)S(1)}, u32[]{:S(2)}, u32[]{:S(2)}) %collective-permute-start.5) | collective-permute-done | bytes 393248 | tf_op jit(solution)/shard_map/ppermute | solution.py:29
  120.6 3.1 %collective-permute-start.6 = (bf16[2,192,512]{2,1,0:T(8,128)(2,1)S(1)}, bf16[2,192,512]{2,1,0:T(8,128)(2,1)S(1)}, u32[]{:S(2)}, u32[]{:S(2)}) collective-permute-start(bf16[2,192,512]{2,1,0:T(8,128)(2,1)S(1)} %add_convert_fusion.4), channel_id=1, source_target_pairs={{0,672},{1,97},{2,674},{3,99},{4,676},{5,101},{6,678},{7,103},{8,6... | collective-permute-start | bytes 1179656 | tf_op jit(solution)/shard_map/ppermute | solution.py:29
  123.6 4.8 %collective-permute-done.13 = bf16[2,192,512]{2,1,0:T(8,128)(2,1)S(1)} collective-permute-done((bf16[2,192,512]{2,1,0:T(8,128)(2,1)S(1)}, bf16[2,192,512]{2,1,0:T(8,128)(2,1)S(1)}, u32[]{:S(2)}, u32[]{:S(2)}) %collective-permute-start.13) | collective-permute-done | bytes 393248 | tf_op jit(solution)/shard_map/ppermute | solution.py:29
  128.6 1.9 %collective-permute-start.14 = (bf16[2,192,512]{2,1,0:T(8,128)(2,1)S(1)}, bf16[2,192,512]{2,1,0:T(8,128)(2,1)S(1)}, u32[]{:S(2)}, u32[]{:S(2)}) collective-permute-start(bf16[2,192,512]{2,1,0:T(8,128)(2,1)S(1)} %add_convert_fusion.1), channel_id=1, source_target_pairs={{0,672},{1,97},{2,674},{3,99},{4,676},{5,101},{6,678},{7,103},{8,6... | collective-permute-start | bytes 1179656 | tf_op jit(solution)/shard_map/ppermute | solution.py:29
  130.7 4.7 %collective-permute-start.7 = (bf16[192,512]{1,0:T(8,128)(2,1)S(1)}, bf16[192,512]{1,0:T(8,128)(2,1)S(1)}, u32[]{:S(2)}, u32[]{:S(2)}) collective-permute-start(bf16[192,512]{1,0:T(8,128)(2,1)S(1)} %slice_bitcast_fusion.2), channel_id=1, source_target_pairs={{0,96},{1,673},{2,98},{3,675},{4,100},{5,677},{6,102},{7,679},{8,1... | collective-permute-start | bytes 589832 | tf_op jit(solution)/shard_map/ppermute | solution.py:29
  135.3 5.4 %collective-permute-done.14 = bf16[2,192,512]{2,1,0:T(8,128)(2,1)S(1)} collective-permute-done((bf16[2,192,512]{2,1,0:T(8,128)(2,1)S(1)}, bf16[2,192,512]{2,1,0:T(8,128)(2,1)S(1)}, u32[]{:S(2)}, u32[]{:S(2)}) %collective-permute-start.14) | collective-permute-done | bytes 393248 | tf_op jit(solution)/shard_map/ppermute | solution.py:29
  140.9 3.7 %collective-permute-start.15 = (bf16[192,512]{1,0:T(8,128)(2,1)S(1)}, bf16[192,512]{1,0:T(8,128)(2,1)S(1)}, u32[]{:S(2)}, u32[]{:S(2)}) collective-permute-start(bf16[192,512]{1,0:T(8,128)(2,1)S(1)} %slice_bitcast_fusion), channel_id=1, source_target_pairs={{0,96},{1,673},{2,98},{3,675},{4,100},{5,677},{6,102},{7,679},{8,1... | collective-permute-start | bytes 589832 | tf_op jit(solution)/shard_map/ppermute | solution.py:29
  144.7 4.5 %collective-permute-done.15 = bf16[192,512]{1,0:T(8,128)(2,1)S(1)} collective-permute-done((bf16[192,512]{1,0:T(8,128)(2,1)S(1)}, bf16[192,512]{1,0:T(8,128)(2,1)S(1)}, u32[]{:S(2)}, u32[]{:S(2)}) %collective-permute-start.15) | collective-permute-done | bytes 196640 | tf_op jit(solution)/shard_map/ppermute | solution.py:29
  149.3 0.5 convolution_convert_fusion
  149.9 38.1 %all_to_all.10 = bf16[96,4,512]{2,1,0:T(4,128)(2,1)S(1)} all-to-all(bf16[96,4,512]{2,1,0:T(4,128)(2,1)S(1)} %reshape.149), channel_id=1, replica_groups=mesh['etp'=8,'ep'=96] {'ep'}, dimensions={0} | all-to-all | bytes 786432 | tf_op jit(solution)/shard_map/all_to_all | solution.py:167
  188.1 0.9 convolution_reduce_fusion
  189.0 0.9 fusion
  (49 shorter events, 1.8 us)
Async XLA Ops:
  0.6 2.9 %copy-start = (bf16[16,512]{1,0:T(8,128)(2,1)S(1)}, bf16[16,512]{1,0:T(8,128)(2,1)}, u32[]{:S(2)}) copy-start(bf16[16,512]{1,0:T(8,128)(2,1)} %param.7) | copy-start | bytes 49156
  2.0 1.8 copy-start.8
  2.0 1.8 copy-start.10
  2.7 1.0 copy-start.4
  4.0 94.8 %copy-start.3 = (bf16[1,192,4096]{2,1,0:T(8,128)(2,1)S(1)}, bf16[1,192,4096]{2,1,0:T(8,128)(2,1)}, u32[]{:S(2)}) copy-start(bf16[1,192,4096]{2,1,0:T(8,128)(2,1)} %param.13) | copy-start | bytes 4718596
  4.9 41.6 %all-to-all-start = ((bf16[96,4,512]{2,1,0:T(4,128)(2,1)}), bf16[96,4,512]{2,1,0:T(4,128)(2,1)}, u32[]{:S(2)}, u32[]{:S(2)}) async-start(bf16[96,4,512]{2,1,0:T(4,128)(2,1)} %reshape.147), calls=%async_computation | async-start | bytes 786432 | tf_op jit(solution)/shard_map/all_to_all | solution.py:133
  25.3 0.6 copy-start.6
  46.5 52.3 %copy-start.2 = (bf16[1,4096,192]{1,2,0:T(8,128)(2,1)S(1)}, bf16[1,4096,192]{1,2,0:T(8,128)(2,1)}, u32[]{:S(2)}) copy-start(bf16[1,4096,192]{1,2,0:T(8,128)(2,1)} %param.12) | copy-start | bytes 4718596
  47.7 51.1 %copy-start.1 = (bf16[1,4096,192]{1,2,0:T(8,128)(2,1)S(1)}, bf16[1,4096,192]{1,2,0:T(8,128)(2,1)}, u32[]{:S(2)}) copy-start(bf16[1,4096,192]{1,2,0:T(8,128)(2,1)} %param.11) | copy-start | bytes 4718596
  48.9 8.2 %collective-permute-start = (bf16[192,512]{1,0:T(8,128)(2,1)S(1)}, bf16[192,512]{1,0:T(8,128)(2,1)S(1)}, u32[]{:S(2)}, u32[]{:S(2)}) collective-permute-start(bf16[192,512]{1,0:T(8,128)(2,1)S(1)} %convolution_convert_fusion.3), channel_id=1, source_target_pairs={{0,96},{1,673},{2,98},{3,675},{4,100},{5,677},{6,102},{7,679},{8,1... | collective-permute-start | bytes 589832 | tf_op jit(solution)/shard_map/ppermute | solution.py:29
  57.1 15.6 %collective-permute-start.1 = (bf16[2,192,512]{2,1,0:T(8,128)(2,1)S(1)}, bf16[2,192,512]{2,1,0:T(8,128)(2,1)S(1)}, u32[]{:S(2)}, u32[]{:S(2)}) collective-permute-start(bf16[2,192,512]{2,1,0:T(8,128)(2,1)S(1)} %pad_maximum_fusion.refs_0_), channel_id=1, source_target_pairs={{0,672},{1,97},{2,674},{3,99},{4,676},{5,101},{6,678},{7,103},{8,6... | collective-permute-start | bytes 1179656 | tf_op jit(solution)/shard_map/ppermute | solution.py:29
  60.1 10.2 %collective-permute-start.8 = (bf16[192,512]{1,0:T(8,128)(2,1)S(1)}, bf16[192,512]{1,0:T(8,128)(2,1)S(1)}, u32[]{:S(2)}, u32[]{:S(2)}) collective-permute-start(bf16[192,512]{1,0:T(8,128)(2,1)S(1)} %convolution_convert_fusion.2), channel_id=1, source_target_pairs={{0,96},{1,673},{2,98},{3,675},{4,100},{5,677},{6,102},{7,679},{8,1... | collective-permute-start | bytes 589832 | tf_op jit(solution)/shard_map/ppermute | solution.py:29
  70.3 8.8 %collective-permute-start.9 = (bf16[2,192,512]{2,1,0:T(8,128)(2,1)S(1)}, bf16[2,192,512]{2,1,0:T(8,128)(2,1)S(1)}, u32[]{:S(2)}, u32[]{:S(2)}) collective-permute-start(bf16[2,192,512]{2,1,0:T(8,128)(2,1)S(1)} %pad_maximum_fusion.1.refs_0_), channel_id=1, source_target_pairs={{0,672},{1,97},{2,674},{3,99},{4,676},{5,101},{6,678},{7,103},{8,6... | collective-permute-start | bytes 1179656 | tf_op jit(solution)/shard_map/ppermute | solution.py:29
  72.7 14.0 %collective-permute-start.2 = (bf16[2,192,512]{2,1,0:T(8,128)(2,1)S(1)}, bf16[2,192,512]{2,1,0:T(8,128)(2,1)S(1)}, u32[]{:S(2)}, u32[]{:S(2)}) collective-permute-start(bf16[2,192,512]{2,1,0:T(8,128)(2,1)S(1)} %collective-permute-done.1.refs_1_), channel_id=1, source_target_pairs={{0,96},{1,673},{2,98},{3,675},{4,100},{5,677},{6,102},{7,679},{8,1... | collective-permute-start | bytes 1179656 | tf_op jit(solution)/shard_map/ppermute | solution.py:29
  79.2 11.5 %collective-permute-start.10 = (bf16[2,192,512]{2,1,0:T(8,128)(2,1)S(1)}, bf16[2,192,512]{2,1,0:T(8,128)(2,1)S(1)}, u32[]{:S(2)}, u32[]{:S(2)}) collective-permute-start(bf16[2,192,512]{2,1,0:T(8,128)(2,1)S(1)} %collective-permute-done.9.refs_1_), channel_id=1, source_target_pairs={{0,96},{1,673},{2,98},{3,675},{4,100},{5,677},{6,102},{7,679},{8,1... | collective-permute-start | bytes 1179656 | tf_op jit(solution)/shard_map/ppermute | solution.py:29
  86.6 12.2 %collective-permute-start.3 = (bf16[2,192,512]{2,1,0:T(8,128)(2,1)S(1)}, bf16[2,192,512]{2,1,0:T(8,128)(2,1)S(1)}, u32[]{:S(2)}, u32[]{:S(2)}) collective-permute-start(bf16[2,192,512]{2,1,0:T(8,128)(2,1)S(1)} %collective-permute-done.2.refs_2_), channel_id=1, source_target_pairs={{0,672},{1,97},{2,674},{3,99},{4,676},{5,101},{6,678},{7,103},{8,6... | collective-permute-start | bytes 1179656 | tf_op jit(solution)/shard_map/ppermute | solution.py:29
  90.7 12.9 %collective-permute-start.11 = (bf16[2,192,512]{2,1,0:T(8,128)(2,1)S(1)}, bf16[2,192,512]{2,1,0:T(8,128)(2,1)S(1)}, u32[]{:S(2)}, u32[]{:S(2)}) collective-permute-start(bf16[2,192,512]{2,1,0:T(8,128)(2,1)S(1)} %collective-permute-done.10.refs_2_), channel_id=1, source_target_pairs={{0,672},{1,97},{2,674},{3,99},{4,676},{5,101},{6,678},{7,103},{8,6... | collective-permute-start | bytes 1179656 | tf_op jit(solution)/shard_map/ppermute | solution.py:29
  100.3 8.8 %collective-permute-start.4 = (bf16[2,192,512]{2,1,0:T(8,128)(2,1)S(1)}, bf16[2,192,512]{2,1,0:T(8,128)(2,1)S(1)}, u32[]{:S(2)}, u32[]{:S(2)}) collective-permute-start(bf16[2,192,512]{2,1,0:T(8,128)(2,1)S(1)} %get-tuple-element.15), channel_id=1, source_target_pairs={{0,672},{1,97},{2,674},{3,99},{4,676},{5,101},{6,678},{7,103},{8,6... | collective-permute-start | bytes 1179656 | tf_op jit(solution)/shard_map/ppermute | solution.py:29
  105.9 8.8 %collective-permute-start.12 = (bf16[2,192,512]{2,1,0:T(8,128)(2,1)S(1)}, bf16[2,192,512]{2,1,0:T(8,128)(2,1)S(1)}, u32[]{:S(2)}, u32[]{:S(2)}) collective-permute-start(bf16[2,192,512]{2,1,0:T(8,128)(2,1)S(1)} %get-tuple-element.21), channel_id=1, source_target_pairs={{0,672},{1,97},{2,674},{3,99},{4,676},{5,101},{6,678},{7,103},{8,6... | collective-permute-start | bytes 1179656 | tf_op jit(solution)/shard_map/ppermute | solution.py:29
  109.3 11.2 %collective-permute-start.5 = (bf16[2,192,512]{2,1,0:T(8,128)(2,1)S(1)}, bf16[2,192,512]{2,1,0:T(8,128)(2,1)S(1)}, u32[]{:S(2)}, u32[]{:S(2)}) collective-permute-start(bf16[2,192,512]{2,1,0:T(8,128)(2,1)S(1)} %add_convert_fusion.5), channel_id=1, source_target_pairs={{0,96},{1,673},{2,98},{3,675},{4,100},{5,677},{6,102},{7,679},{8,1... | collective-permute-start | bytes 1179656 | tf_op jit(solution)/shard_map/ppermute | solution.py:29
  114.8 13.6 %collective-permute-start.13 = (bf16[2,192,512]{2,1,0:T(8,128)(2,1)S(1)}, bf16[2,192,512]{2,1,0:T(8,128)(2,1)S(1)}, u32[]{:S(2)}, u32[]{:S(2)}) collective-permute-start(bf16[2,192,512]{2,1,0:T(8,128)(2,1)S(1)} %add_convert_fusion.2), channel_id=1, source_target_pairs={{0,96},{1,673},{2,98},{3,675},{4,100},{5,677},{6,102},{7,679},{8,1... | collective-permute-start | bytes 1179656 | tf_op jit(solution)/shard_map/ppermute | solution.py:29
  120.6 10.0 %collective-permute-start.6 = (bf16[2,192,512]{2,1,0:T(8,128)(2,1)S(1)}, bf16[2,192,512]{2,1,0:T(8,128)(2,1)S(1)}, u32[]{:S(2)}, u32[]{:S(2)}) collective-permute-start(bf16[2,192,512]{2,1,0:T(8,128)(2,1)S(1)} %add_convert_fusion.4), channel_id=1, source_target_pairs={{0,672},{1,97},{2,674},{3,99},{4,676},{5,101},{6,678},{7,103},{8,6... | collective-permute-start | bytes 1179656 | tf_op jit(solution)/shard_map/ppermute | solution.py:29
  128.6 12.2 %collective-permute-start.14 = (bf16[2,192,512]{2,1,0:T(8,128)(2,1)S(1)}, bf16[2,192,512]{2,1,0:T(8,128)(2,1)S(1)}, u32[]{:S(2)}, u32[]{:S(2)}) collective-permute-start(bf16[2,192,512]{2,1,0:T(8,128)(2,1)S(1)} %add_convert_fusion.1), channel_id=1, source_target_pairs={{0,672},{1,97},{2,674},{3,99},{4,676},{5,101},{6,678},{7,103},{8,6... | collective-permute-start | bytes 1179656 | tf_op jit(solution)/shard_map/ppermute | solution.py:29
  130.7 14.0 %collective-permute-start.7 = (bf16[192,512]{1,0:T(8,128)(2,1)S(1)}, bf16[192,512]{1,0:T(8,128)(2,1)S(1)}, u32[]{:S(2)}, u32[]{:S(2)}) collective-permute-start(bf16[192,512]{1,0:T(8,128)(2,1)S(1)} %slice_bitcast_fusion.2), channel_id=1, source_target_pairs={{0,96},{1,673},{2,98},{3,675},{4,100},{5,677},{6,102},{7,679},{8,1... | collective-permute-start | bytes 589832 | tf_op jit(solution)/shard_map/ppermute | solution.py:29
  140.8 8.5 %copy-start.7 = (s32[384]{0:T(512)S(1)}, s32[384]{0:T(512)}, u32[]{:S(2)}) copy-start(s32[384]{0:T(512)} %copy-done.6) | copy-start | bytes 4612
  140.9 8.3 %collective-permute-start.15 = (bf16[192,512]{1,0:T(8,128)(2,1)S(1)}, bf16[192,512]{1,0:T(8,128)(2,1)S(1)}, u32[]{:S(2)}, u32[]{:S(2)}) collective-permute-start(bf16[192,512]{1,0:T(8,128)(2,1)S(1)} %slice_bitcast_fusion), channel_id=1, source_target_pairs={{0,96},{1,673},{2,98},{3,675},{4,100},{5,677},{6,102},{7,679},{8,1... | collective-permute-start | bytes 589832 | tf_op jit(solution)/shard_map/ppermute | solution.py:29
  149.3 38.8 %copy-start.11 = (s32[128]{0:T(128)S(1)}, s32[128]{0:T(128)}, u32[]{:S(2)}) copy-start(s32[128]{0:T(128)} %copy-done.10) | copy-start | bytes 1540
  149.8 39.2 %copy-start.5 = (f32[16,8]{1,0:T(8,128)S(1)}, f32[16,8]{1,0:T(8,128)}, u32[]{:S(2)}) copy-start(f32[16,8]{1,0:T(8,128)} %copy-done.4) | copy-start | bytes 1540
  149.8 39.2 %copy-start.9 = (s32[128]{0:T(128)S(1)}, s32[128]{0:T(128)}, u32[]{:S(2)}) copy-start(s32[128]{0:T(128)} %copy-done.8) | copy-start | bytes 1540

commit v3 on v2

--- a/solution.py
+++ b/solution.py
@@ -19,26 +19,94 @@
     return lax.dot_general(left, right, (((1,), (0,)), ((), ())), preferred_element_type=f32)
 
 
-def exchange(value, step):
+def split3(value):
+    high = value.astype(bf16)
+    rest = value - high.astype(f32)
+    middle = rest.astype(bf16)
+    return high, middle, (rest - middle.astype(f32)).astype(bf16)
+
+
+def dot_first(left, right):
+    return lax.dot_general(left, right, (((0,), (0,)), ((), ())), preferred_element_type=f32)
+
+
+def travel_row(slot, kind, capacity):
+    return lax.div(slot, capacity) * (2 * capacity) + kind * capacity + lax.rem(slot, capacity)
+
+
+def picks(capacity, routes, weight, rows):
+    shape = (rows, routes.shape[1])
+    row = lax.broadcasted_iota(jnp.int32, shape, 0)
+    owner = lax.div(row, 2 * capacity)
+    named = jnp.zeros(shape, f32)
+    scale = jnp.zeros(shape, f32)
+    for k in range(routes.shape[0]):
+        hit = routes[k : k + 1, :] == owner
+        named = jnp.where(hit, 1.0, named)
+        scale = jnp.where(hit, weight[k : k + 1, :], scale)
+    square = (shape[1], shape[1])
+    before = lax.broadcasted_iota(jnp.int32, square, 0) < lax.broadcasted_iota(jnp.int32, square, 1)
+    earlier = dot(named.astype(bf16), before.astype(f32).astype(bf16))
+    here = earlier == lax.rem(row, capacity).astype(f32)
+    gradient = lax.rem(row, 2 * capacity) >= capacity
+    return jnp.where(here, named, 0.0), jnp.where(here, scale, 0.0), gradient
+
+
+def dispatch_kernel(capacity, routes, weight, tokens, grads, send):
+    pick, weighted, gradient = picks(capacity, routes, weight, send.shape[0])
+    out = dot(jnp.where(gradient, 0.0, pick).astype(bf16), tokens[...])
+    for part in split3(jnp.where(gradient, weighted, 0.0)):
+        out = out + dot(part, grads[...])
+    send[...] = out.astype(bf16)
+
+
+def sort_kernel(capacity, recv, token_rows, grad_rows):
+    rows = recv.shape[0]
+    for kind, out in ((0, token_rows), (1, grad_rows)):
+        shape = (rows // 2, rows)
+        source = travel_row(lax.broadcasted_iota(jnp.int32, shape, 0), kind, capacity)
+        place = (source == lax.broadcasted_iota(jnp.int32, shape, 1)).astype(f32).astype(bf16)
+        out[...] = dot(place, recv[...]).astype(bf16)
+
+
+def unsort_kernel(capacity, out_sum, out_last, input_sum, input_last, unsorted):
+    rows = unsorted.shape[0]
+    total = None
+    for kind, held, last in ((0, out_sum, out_last), (1, input_sum, input_last)):
+        local = (held[0].astype(f32) + last[...].astype(f32)).astype(bf16)
+        shape = (rows, rows // 2)
+        target = travel_row(lax.broadcasted_iota(jnp.int32, shape, 1), kind, capacity)
+        place = (target == lax.broadcasted_iota(jnp.int32, shape, 0)).astype(f32).astype(bf16)
+        now = dot(place, local)
+        total = now if total is None else total + now
+    unsorted[...] = total.astype(bf16)
+
+
+def combine_kernel(capacity, routes, weight, back, mixed, grad_tokens):
+    pick, weighted, gradient = picks(capacity, routes, weight, back.shape[0])
+    rows = back[...]
+    out = None
+    for part in split3(jnp.where(gradient, 0.0, weighted)):
+        now = dot_first(part, rows)
+        out = now if out is None else out + now
+    mixed[...] = out.astype(bf16)
+    grad_tokens[...] = dot_first(jnp.where(gradient, pick, 0.0).astype(bf16), rows).astype(bf16)
+
+
+def exchange(value, step, chain):
     size, owners = lax.axis_size("etp"), lax.axis_size("ep")
     pairs = []
     for y in range(size):
         for j in range(owners):
-            sign = 1 if (y + j + step) % 2 == 0 else -1
+            sign = 1 if (y + j + step + chain) % 2 == 0 else -1
             pairs.append((y * owners + j, (y + sign) % size * owners + j))
     return lax.ppermute(value, ("etp", "ep"), pairs)
 
 
-def gather_step(held, step):
-    if step == 0:
-        return [jnp.stack([held[0], exchange(held[0], 0)])]
-    return held + [exchange(held[-1], step)]
-
-
-def columns_of(steps, width):
+def columns_of(steps, width, chain):
     size = 2 * steps
     y = lax.axis_index("etp")
-    sign = 1 - 2 * lax.rem(y + lax.axis_index("ep"), 2)
+    sign = 1 - 2 * lax.rem(y + lax.axis_index("ep") + chain, 2)
     out = []
     for k in range(steps):
         turn = sign if k % 2 == 0 else -sign
@@ -51,7 +119,7 @@
     held, (gate_w, up_w, down_w) = refs[:steps], refs[steps : steps + 3]
     gate_ref, up_ref = refs[steps + 3 : steps + 5]
     parts = refs[steps + 5 :]
-    columns = columns_of(steps, held[0].shape[2])
+    columns = columns_of(steps, held[0].shape[2], 0)
     gate = up = None
     for k in range(steps):
         for b in (0, 1):
@@ -72,7 +140,7 @@
     held, (gate_w, up_w, down_w) = refs[:steps], refs[steps : steps + 3]
     gate_ref, up_ref = refs[steps + 3 : steps + 5]
     parts = refs[steps + 5 :]
-    columns = columns_of(steps, held[0].shape[2])
+    columns = columns_of(steps, held[0].shape[2], 1)
     hidden_grad = None
     for k in range(steps):
         for b in (0, 1):
@@ -102,8 +170,8 @@
     )(*operands)
 
 
-def sum_step(parts, arrived, step):
-    received = exchange(arrived, step)
+def sum_step(parts, arrived, step, chain):
+    received = exchange(arrived, step, chain)
     return (parts[step - 1] + received.astype(f32)).astype(bf16)
 
 
@@ -113,35 +181,31 @@
     top_count = routes.shape[1]
     capacity = min(tok_rows, max(2, (3 * tok_rows * top_count + 2 * owners - 1) // (2 * owners)))
     slots = owners * capacity
-    chosen = routes.reshape(-1)
-    onehot = (chosen[:, None] == jnp.arange(owners, dtype=jnp.int32)[None, :]).astype(jnp.int32)
-    earlier = jnp.cumsum(onehot, axis=0) - onehot
-    within = jnp.sum(earlier * onehot, axis=1)
-    target = chosen * (2 * capacity) + within
-    rows = jnp.arange(2 * slots, dtype=jnp.int32)
-    pick_token = (rows[:, None] == target[None, :]).astype(bf16)
-    pick_grad = (rows[:, None] == target[None, :] + capacity).astype(bf16)
-    token_pairs = jnp.repeat(tokens, top_count, axis=0)
-    grad_pairs = (
-        route_weight.reshape(-1)[:, None] * jnp.repeat(grad_out, top_count, axis=0).astype(f32)
-    ).astype(bf16)
-    send = jnp.dot(
-        jnp.concatenate([pick_token, pick_grad], axis=1),
-        jnp.concatenate([token_pairs, grad_pairs], axis=0),
-        preferred_element_type=f32,
-    ).astype(bf16)
+    rows = 2 * slots
+    send = pl.pallas_call(
+        lambda *refs: dispatch_kernel(capacity, *refs),
+        out_shape=jax.ShapeDtypeStruct((rows, local_width), bf16),
+        compiler_params=pltpu.CompilerParams(vmem_limit_bytes=VMEM_LIMIT),
+    )(routes.T, route_weight.T, tokens, grad_out)
     recv = lax.all_to_all(
         send.reshape(owners, 2 * capacity, local_width), "ep", split_axis=0, concat_axis=0, tiled=True
-    ).reshape(2 * slots, local_width)
-    place = jnp.arange(2 * slots, dtype=jnp.int32)
-    kind, slot = place // slots, place % slots
-    source = (slot // capacity) * (2 * capacity) + kind * capacity + slot % capacity
-    sort = (source[:, None] == rows[None, :]).astype(bf16)
-    token_held = [jnp.dot(sort[:slots], recv, preferred_element_type=f32).astype(bf16)]
-    grad_held = [jnp.dot(sort[slots:], recv, preferred_element_type=f32).astype(bf16)]
-    for step in range(steps):
-        token_held = gather_step(token_held, step)
-        grad_held = gather_step(grad_held, step)
+    ).reshape(rows, local_width)
+    half = jax.ShapeDtypeStruct((slots, local_width), bf16)
+    token_rows, grad_rows = pl.pallas_call(
+        lambda *refs: sort_kernel(capacity, *refs),
+        out_shape=[half, half],
+        in_specs=[VMEM],
+        out_specs=[VMEM] * 2,
+        compiler_params=pltpu.CompilerParams(vmem_limit_bytes=VMEM_LIMIT),
+    )(recv)
+    token_next, grad_next = lax.optimization_barrier(
+        (exchange(token_rows, 0, 0), exchange(grad_rows, 0, 1))
+    )
+    token_held = [jnp.stack([token_rows, token_next])]
+    grad_held = [jnp.stack([grad_rows, grad_next])]
+    for step in range(1, steps):
+        token_held.append(exchange(token_held[-1], step, 0))
+        grad_held.append(exchange(grad_held[-1], step, 1))
     gate_weight, up_weight, down_weight = w_gate[0].T, w_up[0].T, w_down[0]
     weights = [gate_weight, up_weight, down_weight]
     hidden_width, width = down_weight.shape
@@ -156,24 +220,26 @@
     )
     out_sum, input_sum = out_parts[-1], input_parts[-1]
     for step in reversed(range(1, steps)):
-        out_sum = sum_step(out_parts, out_sum, step)
-        input_sum = sum_step(input_parts, input_sum, step)
-    out_local = (out_sum[0].astype(f32) + exchange(out_sum[1], 0).astype(f32)).astype(bf16)
-    input_local = (input_sum[0].astype(f32) + exchange(input_sum[1], 0).astype(f32)).astype(bf16)
-    local = jnp.concatenate([out_local, input_local], axis=0)
-    unsorted = lax.dot_general(
-        sort, local, (((0,), (0,)), ((), ())), preferred_element_type=f32
-    ).astype(bf16)
+        out_sum = sum_step(out_parts, out_sum, step, 0)
+        input_sum = sum_step(input_parts, input_sum, step, 1)
+    unsorted = pl.pallas_call(
+        lambda *refs: unsort_kernel(capacity, *refs),
+        out_shape=jax.ShapeDtypeStruct((rows, local_width), bf16),
+        in_specs=[VMEM] * 4,
+        out_specs=VMEM,
+        compiler_params=pltpu.CompilerParams(vmem_limit_bytes=VMEM_LIMIT),
+    )(out_sum, exchange(out_sum[1], 0, 0), input_sum, exchange(input_sum[1], 0, 1))
     back = lax.all_to_all(
         unsorted.reshape(owners, 2 * capacity, local_width), "ep", split_axis=0, concat_axis=0, tiled=True
-    ).reshape(2 * slots, local_width)
-    first = (((0,), (0,)), ((), ()))
-    out_rows = lax.dot_general(pick_token, back, first, preferred_element_type=f32)
-    input_rows = lax.dot_general(pick_grad, back, first, preferred_element_type=f32)
-    out_rows = out_rows.reshape(tok_rows, top_count, local_width)
-    input_rows = input_rows.reshape(tok_rows, top_count, local_width)
-    mixed = jnp.sum(route_weight[:, :, None] * out_rows, axis=1).astype(bf16)
-    grad_tokens = jnp.sum(input_rows, axis=1).astype(bf16)
+    ).reshape(rows, local_width)
+    mine = jax.ShapeDtypeStruct((tok_rows, local_width), bf16)
+    mixed, grad_tokens = pl.pallas_call(
+        lambda *refs: combine_kernel(capacity, *refs),
+        out_shape=[mine, mine],
+        in_specs=[VMEM] * 3,
+        out_specs=[VMEM] * 2,
+        compiler_params=pltpu.CompilerParams(vmem_limit_bytes=VMEM_LIMIT),
+    )(routes.T, route_weight.T, back)
     return (mixed, grad_tokens)
 
 

time: 191 us -> 189 us (0.990)
  blocking collectives: 38.1 us -> 84.2 us
  starting transfers between devices: 69.7 us -> 46.7 us
  waiting for transfers between devices: 64.8 us -> 43.2 us
  matrix products: 4.8 us -> 0 us
  Pallas kernels: 3.84 us -> 6.55 us
  other arithmetic: 3.03 us -> 0.8 us
    all_to_all x0 -> x1, blocking collectives: none -> 41.5 us  [on_device(): lax.all_to_all(send.reshape(owners, 2 * capacity, local_width), 'ep', spl...]
    all_to_all x1 -> x0, starting transfers between devices: 20.3 us -> none  [on_device(): lax.all_to_all(send.reshape(owners, 2 * capacity, local_width), 'ep', spl...]
    all_to_all x1 -> x0, waiting for transfers between devices: 19.8 us -> none  [on_device(): lax.all_to_all(send.reshape(owners, 2 * capacity, local_width), 'ep', spl...]
    dot_general x6 -> x0, matrix products: 4.8 us -> none  [the longest x1 1.16 us: on_device(): jnp.dot(sort[:slots], recv, preferred_element_type=f32).astype(bf16)]
    all_to_all x1, blocking collectives: 38.1 us -> 42.6 us  [on_device(): lax.all_to_all(unsorted.reshape(owners, 2 * capacity, local_width), 'ep',...]
    pallas_call x0 -> x4, Pallas kernels: none -> 2.73 us  [the longest x1 1.23 us: on_device(): pl.pallas_call(lambda *refs: combine_kernel(capacity, *refs), out_shape=[...]
    ppermute x16, starting transfers between devices: 49.4 us -> 46.7 us  [exchange(): return lax.ppermute(value, ('etp', 'ep'), pairs)]
    unnamed x26 -> x18, local copies, waits for them, and re-layouts: 2.15 us -> 4.23 us
  transfers between devices with their start and end apart: 17 -> 16, of which waited for: 14 -> 15; matrix products, arithmetic and copies ran while one was open for 1% -> 0% of each run, Pallas kernels for 2% -> 2%
where the time goes in v3:
time: 189 us; the launch traced here: 188 us
  blocking collectives  84.2 us (45%)
  starting transfers between devices  46.7 us (25%)
  waiting for transfers between devices  43.2 us (23%)
  Pallas kernels  6.55 us (3%)
  local copies, waits for them, and re-layouts  5.76 us (3%)
    ppermute x16, starting transfers between devices, exchange(): return lax.ppermute(value, ('etp', 'ep'), pairs)  46.7 us
    ppermute x16, waiting for transfers between devices, exchange(): return lax.ppermute(value, ('etp', 'ep'), pairs)  43.2 us
    all_to_all x1, blocking collectives, on_device(): lax.all_to_all(unsorted.reshape(owners, 2 * capacity, local_width), 'ep',...  42.6 us
    all_to_all x1, blocking collectives, on_device(): lax.all_to_all(send.reshape(owners, 2 * capacity, local_width), 'ep', spl...  41.5 us
    unnamed x18, local copies, waits for them, and re-layouts  4.23 us
    pallas_call x2, Pallas kernels, call(): pl.pallas_call(lambda *refs: kernel(steps, *refs), out_shape=shapes, in_s...  3.82 us
  transfers between devices with their start and end apart: 16, of which 15 were waited for; matrix products, arithmetic and copies ran while one was open for 0% of the time, Pallas kernels for 2%

profile of v3, /device:TPU:1, one launch (start us, length us, event | category | flops | bytes accessed | tf_op | source)
XLA Modules:
  0.0 188.1 jit_solution(7573871363490807874)
XLA Ops:
  0.6 0.7 copy-done.3
  1.3 0.7 copy-done.5
  2.0 0.7 copy-done.7
  2.7 0.7 copy-done.8
  3.4 0.7 shard_map.86
  4.3 41.5 %all_to_all.10 = bf16[96,4,512]{2,1,0:T(4,128)(2,1)} all-to-all(bf16[96,4,512]{2,1,0:T(4,128)(2,1)S(1)} %reshape.16), channel_id=1, replica_groups=mesh['etp'=8,'ep'=96] {'ep'}, dimensions={0} | all-to-all | bytes 786432 | tf_op jit(solution)/shard_map/all_to_all | solution.py:190
  45.8 1.2 reshape.17.refs_0_
  47.1 0.4 shard_map.87
  47.4 5.1 %collective-permute-start = (bf16[192,512]{1,0:T(8,128)(2,1)S(1)}, bf16[192,512]{1,0:T(8,128)(2,1)S(1)}, u32[]{:S(2)}, u32[]{:S(2)}) collective-permute-start(bf16[192,512]{1,0:T(8,128)(2,1)S(1)} %get-tuple-element.16), channel_id=1, source_target_pairs={{0,96},{1,673},{2,98},{3,675},{4,100},{5,677},{6,102},{7,679},{8,1... | collective-permute-start | bytes 589832 | tf_op jit(solution)/shard_map/ppermute | solution.py:103
  52.5 1.9 %collective-permute-start.1 = (bf16[192,512]{1,0:T(8,128)(2,1)S(1)}, bf16[192,512]{1,0:T(8,128)(2,1)S(1)}, u32[]{:S(2)}, u32[]{:S(2)}) collective-permute-start(bf16[192,512]{1,0:T(8,128)(2,1)S(1)} %get-tuple-element.17), channel_id=1, source_target_pairs={{0,672},{1,97},{2,674},{3,99},{4,676},{5,101},{6,678},{7,103},{8,6... | collective-permute-start | bytes 589832 | tf_op jit(solution)/shard_map/ppermute | solution.py:103
  54.5 1.1 collective-permute-done
  55.6 3.7 %collective-permute-done.1 = bf16[192,512]{1,0:T(8,128)(2,1)S(1)} collective-permute-done((bf16[192,512]{1,0:T(8,128)(2,1)S(1)}, bf16[192,512]{1,0:T(8,128)(2,1)S(1)}, u32[]{:S(2)}, u32[]{:S(2)}) %collective-permute-start.1) | collective-permute-done | bytes 196640 | tf_op jit(solution)/shard_map/ppermute | solution.py:103
  59.3 2.2 %collective-permute-start.2 = (bf16[2,192,512]{2,1,0:T(8,128)(2,1)S(1)}, bf16[2,192,512]{2,1,0:T(8,128)(2,1)S(1)}, u32[]{:S(2)}, u32[]{:S(2)}) collective-permute-start(bf16[2,192,512]{2,1,0:T(8,128)(2,1)S(1)} %pad_maximum_fusion.refs_0_), channel_id=1, source_target_pairs={{0,672},{1,97},{2,674},{3,99},{4,676},{5,101},{6,678},{7,103},{8,6... | collective-permute-start | bytes 1179656 | tf_op jit(solution)/shard_map/ppermute | solution.py:103
  61.5 4.9 %collective-permute-start.9 = (bf16[2,192,512]{2,1,0:T(8,128)(2,1)S(1)}, bf16[2,192,512]{2,1,0:T(8,128)(2,1)S(1)}, u32[]{:S(2)}, u32[]{:S(2)}) collective-permute-start(bf16[2,192,512]{2,1,0:T(8,128)(2,1)S(1)} %pad_maximum_fusion.1.refs_0_), channel_id=1, source_target_pairs={{0,96},{1,673},{2,98},{3,675},{4,100},{5,677},{6,102},{7,679},{8,1... | collective-permute-start | bytes 1179656 | tf_op jit(solution)/shard_map/ppermute | solution.py:103
  66.4 1.7 collective-permute-done.2.refs_1_
  68.1 3.5 %collective-permute-start.3 = (bf16[2,192,512]{2,1,0:T(8,128)(2,1)S(1)}, bf16[2,192,512]{2,1,0:T(8,128)(2,1)S(1)}, u32[]{:S(2)}, u32[]{:S(2)}) collective-permute-start(bf16[2,192,512]{2,1,0:T(8,128)(2,1)S(1)} %collective-permute-done.2.refs_1_), channel_id=1, source_target_pairs={{0,96},{1,673},{2,98},{3,675},{4,100},{5,677},{6,102},{7,679},{8,1... | collective-permute-start | bytes 1179656 | tf_op jit(solution)/shard_map/ppermute | solution.py:103
  71.6 4.3 %collective-permute-done.9.refs_1_ = bf16[2,192,512]{2,1,0:T(8,128)(2,1)S(1)} collective-permute-done((bf16[2,192,512]{2,1,0:T(8,128)(2,1)S(1)}, bf16[2,192,512]{2,1,0:T(8,128)(2,1)S(1)}, u32[]{:S(2)}, u32[]{:S(2)}) %collective-permute-start.9) | collective-permute-done | bytes 393248 | tf_op jit(solution)/shard_map/ppermute | solution.py:103
  75.9 1.9 %collective-permute-start.10 = (bf16[2,192,512]{2,1,0:T(8,128)(2,1)S(1)}, bf16[2,192,512]{2,1,0:T(8,128)(2,1)S(1)}, u32[]{:S(2)}, u32[]{:S(2)}) collective-permute-start(bf16[2,192,512]{2,1,0:T(8,128)(2,1)S(1)} %collective-permute-done.9.refs_1_), channel_id=1, source_target_pairs={{0,672},{1,97},{2,674},{3,99},{4,676},{5,101},{6,678},{7,103},{8,6... | collective-permute-start | bytes 1179656 | tf_op jit(solution)/shard_map/ppermute | solution.py:103
  77.8 2.1 %collective-permute-done.3.refs_2_ = bf16[2,192,512]{2,1,0:T(8,128)(2,1)S(1)} collective-permute-done((bf16[2,192,512]{2,1,0:T(8,128)(2,1)S(1)}, bf16[2,192,512]{2,1,0:T(8,128)(2,1)S(1)}, u32[]{:S(2)}, u32[]{:S(2)}) %collective-permute-start.3) | collective-permute-done | bytes 393248 | tf_op jit(solution)/shard_map/ppermute | solution.py:103
  79.9 1.9 %collective-permute-start.4 = (bf16[2,192,512]{2,1,0:T(8,128)(2,1)S(1)}, bf16[2,192,512]{2,1,0:T(8,128)(2,1)S(1)}, u32[]{:S(2)}, u32[]{:S(2)}) collective-permute-start(bf16[2,192,512]{2,1,0:T(8,128)(2,1)S(1)} %collective-permute-done.3.refs_2_), channel_id=1, source_target_pairs={{0,672},{1,97},{2,674},{3,99},{4,676},{5,101},{6,678},{7,103},{8,6... | collective-permute-start | bytes 1179656 | tf_op jit(solution)/shard_map/ppermute | solution.py:103
  81.8 6.3 %collective-permute-done.10.refs_2_ = bf16[2,192,512]{2,1,0:T(8,128)(2,1)S(1)} collective-permute-done((bf16[2,192,512]{2,1,0:T(8,128)(2,1)S(1)}, bf16[2,192,512]{2,1,0:T(8,128)(2,1)S(1)}, u32[]{:S(2)}, u32[]{:S(2)}) %collective-permute-start.10) | collective-permute-done | bytes 393248 | tf_op jit(solution)/shard_map/ppermute | solution.py:103
  88.1 4.1 %collective-permute-start.11 = (bf16[2,192,512]{2,1,0:T(8,128)(2,1)S(1)}, bf16[2,192,512]{2,1,0:T(8,128)(2,1)S(1)}, u32[]{:S(2)}, u32[]{:S(2)}) collective-permute-start(bf16[2,192,512]{2,1,0:T(8,128)(2,1)S(1)} %collective-permute-done.10.refs_2_), channel_id=1, source_target_pairs={{0,96},{1,673},{2,98},{3,675},{4,100},{5,677},{6,102},{7,679},{8,1... | collective-permute-start | bytes 1179656 | tf_op jit(solution)/shard_map/ppermute | solution.py:103
  92.2 0.6 collective-permute-done.4.refs_3_
  92.8 1.4 copy-done.2
  94.2 1.5 shard_map.88
  95.7 1.9 %collective-permute-start.5 = (bf16[2,192,512]{2,1,0:T(8,128)(2,1)S(1)}, bf16[2,192,512]{2,1,0:T(8,128)(2,1)S(1)}, u32[]{:S(2)}, u32[]{:S(2)}) collective-permute-start(bf16[2,192,512]{2,1,0:T(8,128)(2,1)S(1)} %get-tuple-element.22), channel_id=1, source_target_pairs={{0,672},{1,97},{2,674},{3,99},{4,676},{5,101},{6,678},{7,103},{8,6... | collective-permute-start | bytes 1179656 | tf_op jit(solution)/shard_map/ppermute | solution.py:103
  97.7 1.9 %collective-permute-done.11.refs_3_ = bf16[2,192,512]{2,1,0:T(8,128)(2,1)S(1)} collective-permute-done((bf16[2,192,512]{2,1,0:T(8,128)(2,1)S(1)}, bf16[2,192,512]{2,1,0:T(8,128)(2,1)S(1)}, u32[]{:S(2)}, u32[]{:S(2)}) %collective-permute-start.11) | collective-permute-done | bytes 393248 | tf_op jit(solution)/shard_map/ppermute | solution.py:103
  99.6 2.3 %shard_map.89 = (f32[2,192,512]{2,1,0:T(8,128)S(1)}, f32[2,192,512]{2,1,0:T(8,128)S(1)}, f32[2,192,512]{2,1,0:T(8,128)S(1)}, bf16[2,192,512]{2,1,0:T(8,128)(2,1)S(1)}) custom-call(bf16[2,192,512]{2,1,0:T(8,128)(2,1)S(1)} %pad_maximum_fusion.1.refs_0_, bf16[2,192,512]{2,1,0:T(8,128)(2,1)S(1)} %collective-permute-done.9.refs_1_, ...), custom_call_target="tpu_custom_call" | custom-call | flops 905969664 | bytes 9437184 | tf_op jit(solution)/shard_map/pallas_call | solution.py:163
  101.9 3.4 %collective-permute-start.12 = (bf16[2,192,512]{2,1,0:T(8,128)(2,1)S(1)}, bf16[2,192,512]{2,1,0:T(8,128)(2,1)S(1)}, u32[]{:S(2)}, u32[]{:S(2)}) collective-permute-start(bf16[2,192,512]{2,1,0:T(8,128)(2,1)S(1)} %get-tuple-element.29), channel_id=1, source_target_pairs={{0,96},{1,673},{2,98},{3,675},{4,100},{5,677},{6,102},{7,679},{8,1... | collective-permute-start | bytes 1179656 | tf_op jit(solution)/shard_map/ppermute | solution.py:103
  105.3 3.3 %collective-permute-done.5 = bf16[2,192,512]{2,1,0:T(8,128)(2,1)S(1)} collective-permute-done((bf16[2,192,512]{2,1,0:T(8,128)(2,1)S(1)}, bf16[2,192,512]{2,1,0:T(8,128)(2,1)S(1)}, u32[]{:S(2)}, u32[]{:S(2)}) %collective-permute-start.5) | collective-permute-done | bytes 393248 | tf_op jit(solution)/shard_map/ppermute | solution.py:103
  108.6 0.1 add_convert_fusion.5
  108.8 1.9 %collective-permute-start.6 = (bf16[2,192,512]{2,1,0:T(8,128)(2,1)S(1)}, bf16[2,192,512]{2,1,0:T(8,128)(2,1)S(1)}, u32[]{:S(2)}, u32[]{:S(2)}) collective-permute-start(bf16[2,192,512]{2,1,0:T(8,128)(2,1)S(1)} %add_convert_fusion.5), channel_id=1, source_target_pairs={{0,96},{1,673},{2,98},{3,675},{4,100},{5,677},{6,102},{7,679},{8,1... | collective-permute-start | bytes 1179656 | tf_op jit(solution)/shard_map/ppermute | solution.py:103
  110.7 0.9 collective-permute-done.12
  111.6 0.1 add_convert_fusion.2
  111.7 1.9 %collective-permute-start.13 = (bf16[2,192,512]{2,1,0:T(8,128)(2,1)S(1)}, bf16[2,192,512]{2,1,0:T(8,128)(2,1)S(1)}, u32[]{:S(2)}, u32[]{:S(2)}) collective-permute-start(bf16[2,192,512]{2,1,0:T(8,128)(2,1)S(1)} %add_convert_fusion.2), channel_id=1, source_target_pairs={{0,672},{1,97},{2,674},{3,99},{4,676},{5,101},{6,678},{7,103},{8,6... | collective-permute-start | bytes 1179656 | tf_op jit(solution)/shard_map/ppermute | solution.py:103
  113.7 6.4 %collective-permute-done.6 = bf16[2,192,512]{2,1,0:T(8,128)(2,1)S(1)} collective-permute-done((bf16[2,192,512]{2,1,0:T(8,128)(2,1)S(1)}, bf16[2,192,512]{2,1,0:T(8,128)(2,1)S(1)}, u32[]{:S(2)}, u32[]{:S(2)}) %collective-permute-start.6) | collective-permute-done | bytes 393248 | tf_op jit(solution)/shard_map/ppermute | solution.py:103
  120.2 1.9 %collective-permute-start.7 = (bf16[2,192,512]{2,1,0:T(8,128)(2,1)S(1)}, bf16[2,192,512]{2,1,0:T(8,128)(2,1)S(1)}, u32[]{:S(2)}, u32[]{:S(2)}) collective-permute-start(bf16[2,192,512]{2,1,0:T(8,128)(2,1)S(1)} %add_convert_fusion.4), channel_id=1, source_target_pairs={{0,672},{1,97},{2,674},{3,99},{4,676},{5,101},{6,678},{7,103},{8,6... | collective-permute-start | bytes 1179656 | tf_op jit(solution)/shard_map/ppermute | solution.py:103
  122.1 1.6 collective-permute-done.13
  123.8 4.4 %collective-permute-start.14 = (bf16[2,192,512]{2,1,0:T(8,128)(2,1)S(1)}, bf16[2,192,512]{2,1,0:T(8,128)(2,1)S(1)}, u32[]{:S(2)}, u32[]{:S(2)}) collective-permute-start(bf16[2,192,512]{2,1,0:T(8,128)(2,1)S(1)} %add_convert_fusion.1), channel_id=1, source_target_pairs={{0,96},{1,673},{2,98},{3,675},{4,100},{5,677},{6,102},{7,679},{8,1... | collective-permute-start | bytes 1179656 | tf_op jit(solution)/shard_map/ppermute | solution.py:103
  128.2 5.0 %collective-permute-done.7 = bf16[2,192,512]{2,1,0:T(8,128)(2,1)S(1)} collective-permute-done((bf16[2,192,512]{2,1,0:T(8,128)(2,1)S(1)}, bf16[2,192,512]{2,1,0:T(8,128)(2,1)S(1)}, u32[]{:S(2)}, u32[]{:S(2)}) %collective-permute-start.7) | collective-permute-done | bytes 393248 | tf_op jit(solution)/shard_map/ppermute | solution.py:103
  133.3 3.4 %collective-permute-start.8 = (bf16[192,512]{1,0:T(8,128)(2,1)S(1)}, bf16[192,512]{1,0:T(8,128)(2,1)S(1)}, u32[]{:S(2)}, u32[]{:S(2)}) collective-permute-start(bf16[192,512]{1,0:T(8,128)(2,1)S(1)} %slice_bitcast_fusion.1), channel_id=1, source_target_pairs={{0,96},{1,673},{2,98},{3,675},{4,100},{5,677},{6,102},{7,679},{8,1... | collective-permute-start | bytes 589832 | tf_op jit(solution)/shard_map/ppermute | solution.py:103
  136.7 0.1 add_convert_fusion.refs_2_
  136.9 2.4 %collective-permute-start.15 = (bf16[192,512]{1,0:T(8,128)(2,1)S(1)}, bf16[192,512]{1,0:T(8,128)(2,1)S(1)}, u32[]{:S(2)}, u32[]{:S(2)}) collective-permute-start(bf16[192,512]{1,0:T(8,128)(2,1)S(1)} %slice_bitcast_fusion), channel_id=1, source_target_pairs={{0,672},{1,97},{2,674},{3,99},{4,676},{5,101},{6,678},{7,103},{8,6... | collective-permute-start | bytes 589832 | tf_op jit(solution)/shard_map/ppermute | solution.py:103
  139.3 3.3 %collective-permute-done.8.refs_1_ = bf16[192,512]{1,0:T(8,128)(2,1)S(1)} collective-permute-done((bf16[192,512]{1,0:T(8,128)(2,1)S(1)}, bf16[192,512]{1,0:T(8,128)(2,1)S(1)}, u32[]{:S(2)}, u32[]{:S(2)}) %collective-permute-start.8) | collective-permute-done | bytes 196640 | tf_op jit(solution)/shard_map/ppermute | solution.py:103
  142.6 1.0 collective-permute-done.15.refs_3_
  143.6 0.4 shard_map.90
  144.1 42.6 %all_to_all.11 = bf16[96,4,512]{2,1,0:T(4,128)(2,1)S(1)} all-to-all(bf16[96,4,512]{2,1,0:T(4,128)(2,1)S(1)} %reshape.18), channel_id=1, replica_groups=mesh['etp'=8,'ep'=96] {'ep'}, dimensions={0} | all-to-all | bytes 786432 | tf_op jit(solution)/shard_map/all_to_all | solution.py:232
  186.9 1.2 shard_map.91
  (24 shorter events, 0.8 us)
Async XLA Ops:
  0.6 0.7 copy-start.3
  1.3 0.7 copy-start.5
  2.0 0.7 copy-start.7
  2.7 0.7 copy-start.8
  4.3 88.5 %copy-start.1 = (bf16[1,4096,192]{1,2,0:T(8,128)(2,1)S(1)}, bf16[1,4096,192]{1,2,0:T(8,128)(2,1)}, u32[]{:S(2)}) copy-start(bf16[1,4096,192]{1,2,0:T(8,128)(2,1)} %param.12) | copy-start | bytes 4718596
  45.8 47.0 %copy-start = (bf16[1,4096,192]{1,2,0:T(8,128)(2,1)S(1)}, bf16[1,4096,192]{1,2,0:T(8,128)(2,1)}, u32[]{:S(2)}) copy-start(bf16[1,4096,192]{1,2,0:T(8,128)(2,1)} %param.11) | copy-start | bytes 4718596
  47.4 8.2 %collective-permute-start = (bf16[192,512]{1,0:T(8,128)(2,1)S(1)}, bf16[192,512]{1,0:T(8,128)(2,1)S(1)}, u32[]{:S(2)}, u32[]{:S(2)}) collective-permute-start(bf16[192,512]{1,0:T(8,128)(2,1)S(1)} %get-tuple-element.16), channel_id=1, source_target_pairs={{0,96},{1,673},{2,98},{3,675},{4,100},{5,677},{6,102},{7,679},{8,1... | collective-permute-start | bytes 589832 | tf_op jit(solution)/shard_map/ppermute | solution.py:103
  52.5 6.7 %collective-permute-start.1 = (bf16[192,512]{1,0:T(8,128)(2,1)S(1)}, bf16[192,512]{1,0:T(8,128)(2,1)S(1)}, u32[]{:S(2)}, u32[]{:S(2)}) collective-permute-start(bf16[192,512]{1,0:T(8,128)(2,1)S(1)} %get-tuple-element.17), channel_id=1, source_target_pairs={{0,672},{1,97},{2,674},{3,99},{4,676},{5,101},{6,678},{7,103},{8,6... | collective-permute-start | bytes 589832 | tf_op jit(solution)/shard_map/ppermute | solution.py:103
  59.3 8.8 %collective-permute-start.2 = (bf16[2,192,512]{2,1,0:T(8,128)(2,1)S(1)}, bf16[2,192,512]{2,1,0:T(8,128)(2,1)S(1)}, u32[]{:S(2)}, u32[]{:S(2)}) collective-permute-start(bf16[2,192,512]{2,1,0:T(8,128)(2,1)S(1)} %pad_maximum_fusion.refs_0_), channel_id=1, source_target_pairs={{0,672},{1,97},{2,674},{3,99},{4,676},{5,101},{6,678},{7,103},{8,6... | collective-permute-start | bytes 1179656 | tf_op jit(solution)/shard_map/ppermute | solution.py:103
  61.5 14.4 %collective-permute-start.9 = (bf16[2,192,512]{2,1,0:T(8,128)(2,1)S(1)}, bf16[2,192,512]{2,1,0:T(8,128)(2,1)S(1)}, u32[]{:S(2)}, u32[]{:S(2)}) collective-permute-start(bf16[2,192,512]{2,1,0:T(8,128)(2,1)S(1)} %pad_maximum_fusion.1.refs_0_), channel_id=1, source_target_pairs={{0,96},{1,673},{2,98},{3,675},{4,100},{5,677},{6,102},{7,679},{8,1... | collective-permute-start | bytes 1179656 | tf_op jit(solution)/shard_map/ppermute | solution.py:103
  68.1 11.8 %collective-permute-start.3 = (bf16[2,192,512]{2,1,0:T(8,128)(2,1)S(1)}, bf16[2,192,512]{2,1,0:T(8,128)(2,1)S(1)}, u32[]{:S(2)}, u32[]{:S(2)}) collective-permute-start(bf16[2,192,512]{2,1,0:T(8,128)(2,1)S(1)} %collective-permute-done.2.refs_1_), channel_id=1, source_target_pairs={{0,96},{1,673},{2,98},{3,675},{4,100},{5,677},{6,102},{7,679},{8,1... | collective-permute-start | bytes 1179656 | tf_op jit(solution)/shard_map/ppermute | solution.py:103
  75.9 12.2 %collective-permute-start.10 = (bf16[2,192,512]{2,1,0:T(8,128)(2,1)S(1)}, bf16[2,192,512]{2,1,0:T(8,128)(2,1)S(1)}, u32[]{:S(2)}, u32[]{:S(2)}) collective-permute-start(bf16[2,192,512]{2,1,0:T(8,128)(2,1)S(1)} %collective-permute-done.9.refs_1_), channel_id=1, source_target_pairs={{0,672},{1,97},{2,674},{3,99},{4,676},{5,101},{6,678},{7,103},{8,6... | collective-permute-start | bytes 1179656 | tf_op jit(solution)/shard_map/ppermute | solution.py:103
  79.9 12.9 %collective-permute-start.4 = (bf16[2,192,512]{2,1,0:T(8,128)(2,1)S(1)}, bf16[2,192,512]{2,1,0:T(8,128)(2,1)S(1)}, u32[]{:S(2)}, u32[]{:S(2)}) collective-permute-start(bf16[2,192,512]{2,1,0:T(8,128)(2,1)S(1)} %collective-permute-done.3.refs_2_), channel_id=1, source_target_pairs={{0,672},{1,97},{2,674},{3,99},{4,676},{5,101},{6,678},{7,103},{8,6... | collective-permute-start | bytes 1179656 | tf_op jit(solution)/shard_map/ppermute | solution.py:103
  88.1 11.5 %collective-permute-start.11 = (bf16[2,192,512]{2,1,0:T(8,128)(2,1)S(1)}, bf16[2,192,512]{2,1,0:T(8,128)(2,1)S(1)}, u32[]{:S(2)}, u32[]{:S(2)}) collective-permute-start(bf16[2,192,512]{2,1,0:T(8,128)(2,1)S(1)} %collective-permute-done.10.refs_2_), channel_id=1, source_target_pairs={{0,96},{1,673},{2,98},{3,675},{4,100},{5,677},{6,102},{7,679},{8,1... | collective-permute-start | bytes 1179656 | tf_op jit(solution)/shard_map/ppermute | solution.py:103
  92.8 1.4 copy-start.2
  95.7 12.9 %collective-permute-start.5 = (bf16[2,192,512]{2,1,0:T(8,128)(2,1)S(1)}, bf16[2,192,512]{2,1,0:T(8,128)(2,1)S(1)}, u32[]{:S(2)}, u32[]{:S(2)}) collective-permute-start(bf16[2,192,512]{2,1,0:T(8,128)(2,1)S(1)} %get-tuple-element.22), channel_id=1, source_target_pairs={{0,672},{1,97},{2,674},{3,99},{4,676},{5,101},{6,678},{7,103},{8,6... | collective-permute-start | bytes 1179656 | tf_op jit(solution)/shard_map/ppermute | solution.py:103
  101.9 9.7 %collective-permute-start.12 = (bf16[2,192,512]{2,1,0:T(8,128)(2,1)S(1)}, bf16[2,192,512]{2,1,0:T(8,128)(2,1)S(1)}, u32[]{:S(2)}, u32[]{:S(2)}) collective-permute-start(bf16[2,192,512]{2,1,0:T(8,128)(2,1)S(1)} %get-tuple-element.29), channel_id=1, source_target_pairs={{0,96},{1,673},{2,98},{3,675},{4,100},{5,677},{6,102},{7,679},{8,1... | collective-permute-start | bytes 1179656 | tf_op jit(solution)/shard_map/ppermute | solution.py:103
  108.8 11.3 %collective-permute-start.6 = (bf16[2,192,512]{2,1,0:T(8,128)(2,1)S(1)}, bf16[2,192,512]{2,1,0:T(8,128)(2,1)S(1)}, u32[]{:S(2)}, u32[]{:S(2)}) collective-permute-start(bf16[2,192,512]{2,1,0:T(8,128)(2,1)S(1)} %add_convert_fusion.5), channel_id=1, source_target_pairs={{0,96},{1,673},{2,98},{3,675},{4,100},{5,677},{6,102},{7,679},{8,1... | collective-permute-start | bytes 1179656 | tf_op jit(solution)/shard_map/ppermute | solution.py:103
  111.7 11.9 %collective-permute-start.13 = (bf16[2,192,512]{2,1,0:T(8,128)(2,1)S(1)}, bf16[2,192,512]{2,1,0:T(8,128)(2,1)S(1)}, u32[]{:S(2)}, u32[]{:S(2)}) collective-permute-start(bf16[2,192,512]{2,1,0:T(8,128)(2,1)S(1)} %add_convert_fusion.2), channel_id=1, source_target_pairs={{0,672},{1,97},{2,674},{3,99},{4,676},{5,101},{6,678},{7,103},{8,6... | collective-permute-start | bytes 1179656 | tf_op jit(solution)/shard_map/ppermute | solution.py:103
  120.2 13.0 %collective-permute-start.7 = (bf16[2,192,512]{2,1,0:T(8,128)(2,1)S(1)}, bf16[2,192,512]{2,1,0:T(8,128)(2,1)S(1)}, u32[]{:S(2)}, u32[]{:S(2)}) collective-permute-start(bf16[2,192,512]{2,1,0:T(8,128)(2,1)S(1)} %add_convert_fusion.4), channel_id=1, source_target_pairs={{0,672},{1,97},{2,674},{3,99},{4,676},{5,101},{6,678},{7,103},{8,6... | collective-permute-start | bytes 1179656 | tf_op jit(solution)/shard_map/ppermute | solution.py:103
  123.8 13.0 %collective-permute-start.14 = (bf16[2,192,512]{2,1,0:T(8,128)(2,1)S(1)}, bf16[2,192,512]{2,1,0:T(8,128)(2,1)S(1)}, u32[]{:S(2)}, u32[]{:S(2)}) collective-permute-start(bf16[2,192,512]{2,1,0:T(8,128)(2,1)S(1)} %add_convert_fusion.1), channel_id=1, source_target_pairs={{0,96},{1,673},{2,98},{3,675},{4,100},{5,677},{6,102},{7,679},{8,1... | collective-permute-start | bytes 1179656 | tf_op jit(solution)/shard_map/ppermute | solution.py:103
  133.3 9.3 %collective-permute-start.8 = (bf16[192,512]{1,0:T(8,128)(2,1)S(1)}, bf16[192,512]{1,0:T(8,128)(2,1)S(1)}, u32[]{:S(2)}, u32[]{:S(2)}) collective-permute-start(bf16[192,512]{1,0:T(8,128)(2,1)S(1)} %slice_bitcast_fusion.1), channel_id=1, source_target_pairs={{0,96},{1,673},{2,98},{3,675},{4,100},{5,677},{6,102},{7,679},{8,1... | collective-permute-start | bytes 589832 | tf_op jit(solution)/shard_map/ppermute | solution.py:103
  136.9 50.0 %copy-start.4 = (s32[16,8]{0,1:T(8,128)S(1)}, s32[16,8]{0,1:T(8,128)}, u32[]{:S(2)}) copy-start(s32[16,8]{0,1:T(8,128)} %param.8) | copy-start | bytes 1540
  136.9 50.0 %copy-start.6 = (f32[16,8]{0,1:T(8,128)S(1)}, f32[16,8]{0,1:T(8,128)}, u32[]{:S(2)}) copy-start(f32[16,8]{0,1:T(8,128)} %param.9) | copy-start | bytes 1540
  136.9 6.7 %collective-permute-start.15 = (bf16[192,512]{1,0:T(8,128)(2,1)S(1)}, bf16[192,512]{1,0:T(8,128)(2,1)S(1)}, u32[]{:S(2)}, u32[]{:S(2)}) collective-permute-start(bf16[192,512]{1,0:T(8,128)(2,1)S(1)} %slice_bitcast_fusion), channel_id=1, source_target_pairs={{0,672},{1,97},{2,674},{3,99},{4,676},{5,101},{6,678},{7,103},{8,6... | collective-permute-start | bytes 589832 | tf_op jit(solution)/shard_map/ppermute | solution.py:103

commit v4 on v3

--- a/solution.py
+++ b/solution.py
@@ -8,7 +8,9 @@
 bf16 = jnp.bfloat16
 f32 = jnp.float32
 VMEM = pl.BlockSpec(memory_space=pltpu.VMEM)
-VMEM_LIMIT = 28 * 1024 * 1024
+ANY = pl.BlockSpec(memory_space=pl.ANY)
+VMEM_LIMIT = 12 * 1024 * 1024
+CHUNKS = 4
 
 
 def dot_last(left, right):
@@ -69,11 +71,11 @@
         out[...] = dot(place, recv[...]).astype(bf16)
 
 
-def unsort_kernel(capacity, out_sum, out_last, input_sum, input_last, unsorted):
+def unsort_kernel(capacity, out_sum, out_last, input_local, unsorted):
     rows = unsorted.shape[0]
+    out_local = (out_sum[0].astype(f32) + out_last[...].astype(f32)).astype(bf16)
     total = None
-    for kind, held, last in ((0, out_sum, out_last), (1, input_sum, input_last)):
-        local = (held[0].astype(f32) + last[...].astype(f32)).astype(bf16)
+    for kind, local in ((0, out_local), (1, input_local[...])):
         shape = (rows, rows // 2)
         target = travel_row(lax.broadcasted_iota(jnp.int32, shape, 1), kind, capacity)
         place = (target == lax.broadcasted_iota(jnp.int32, shape, 0)).astype(f32).astype(bf16)
@@ -93,20 +95,20 @@
     grad_tokens[...] = dot_first(jnp.where(gradient, pick, 0.0).astype(bf16), rows).astype(bf16)
 
 
-def exchange(value, step, chain):
+def exchange(value, step):
     size, owners = lax.axis_size("etp"), lax.axis_size("ep")
     pairs = []
     for y in range(size):
         for j in range(owners):
-            sign = 1 if (y + j + step + chain) % 2 == 0 else -1
+            sign = 1 if (y + j + step) % 2 == 0 else -1
             pairs.append((y * owners + j, (y + sign) % size * owners + j))
     return lax.ppermute(value, ("etp", "ep"), pairs)
 
 
-def columns_of(steps, width, chain):
+def columns_of(steps, width):
     size = 2 * steps
     y = lax.axis_index("etp")
-    sign = 1 - 2 * lax.rem(y + lax.axis_index("ep") + chain, 2)
+    sign = 1 - 2 * lax.rem(y + lax.axis_index("ep"), 2)
     out = []
     for k in range(steps):
         turn = sign if k % 2 == 0 else -sign
@@ -119,7 +121,7 @@
     held, (gate_w, up_w, down_w) = refs[:steps], refs[steps : steps + 3]
     gate_ref, up_ref = refs[steps + 3 : steps + 5]
     parts = refs[steps + 5 :]
-    columns = columns_of(steps, held[0].shape[2], 0)
+    columns = columns_of(steps, held[0].shape[2])
     gate = up = None
     for k in range(steps):
         for b in (0, 1):
@@ -136,42 +138,37 @@
             parts[k][b] = dot(hidden, down_w[:, columns[k][b]]).astype(parts[k].dtype)
 
 
-def backward_kernel(steps, *refs):
-    held, (gate_w, up_w, down_w) = refs[:steps], refs[steps : steps + 3]
-    gate_ref, up_ref = refs[steps + 3 : steps + 5]
-    parts = refs[steps + 5 :]
-    columns = columns_of(steps, held[0].shape[2], 1)
+def backward_kernel(rows_hbm, gate_w, up_w, down_w, gate_ref, up_ref, part_hbm, rows, part, in_sem, out_sem):
+    chunk = rows.shape[1] // CHUNKS
+    columns = [slice(c * chunk, (c + 1) * chunk) for c in range(CHUNKS)]
+    arriving = [
+        pltpu.make_async_copy(rows_hbm.at[:, columns[c]], rows.at[:, columns[c]], in_sem.at[c])
+        for c in range(CHUNKS)
+    ]
+    for copy in arriving:
+        copy.start()
     hidden_grad = None
-    for k in range(steps):
-        for b in (0, 1):
-            now = dot_last(held[k][b], down_w[:, columns[k][b]])
-            hidden_grad = now if hidden_grad is None else hidden_grad + now
+    for c in range(CHUNKS):
+        arriving[c].wait()
+        now = dot_last(rows[:, columns[c]], down_w[:, columns[c]])
+        hidden_grad = now if hidden_grad is None else hidden_grad + now
     gate, up = gate_ref[...], up_ref[...]
     squash = jax.nn.sigmoid(gate)
     up_grad = (hidden_grad * (gate * squash)).astype(bf16)
     gate_grad = (hidden_grad * up * squash * (1.0 + gate * (1.0 - squash))).astype(bf16)
-    for k in reversed(range(steps)):
-        for b in (0, 1):
-            part = dot(gate_grad, gate_w[:, columns[k][b]]) + dot(up_grad, up_w[:, columns[k][b]])
-            parts[k][b] = part.astype(parts[k].dtype)
-
-
-def call(kernel, steps, operands, extra_shapes, pair_shape, flops):
-    shapes = extra_shapes + [
-        jax.ShapeDtypeStruct(pair_shape, f32 if k < steps - 1 else bf16) for k in range(steps)
-    ]
-    return pl.pallas_call(
-        lambda *refs: kernel(steps, *refs),
-        out_shape=shapes,
-        in_specs=[VMEM] * len(operands),
-        out_specs=[VMEM] * len(shapes),
-        compiler_params=pltpu.CompilerParams(vmem_limit_bytes=VMEM_LIMIT),
-        cost_estimate=pl.CostEstimate(flops=flops, bytes_accessed=9 << 20, transcendentals=0),
-    )(*operands)
-
-
-def sum_step(parts, arrived, step, chain):
-    received = exchange(arrived, step, chain)
+    leaving = []
+    for c in range(CHUNKS):
+        now = dot(gate_grad, gate_w[:, columns[c]]) + dot(up_grad, up_w[:, columns[c]])
+        part[:, columns[c]] = now.astype(bf16)
+        copy = pltpu.make_async_copy(part.at[:, columns[c]], part_hbm.at[:, columns[c]], out_sem.at[c])
+        copy.start()
+        leaving.append(copy)
+    for copy in leaving:
+        copy.wait()
+
+
+def sum_step(parts, arrived, step):
+    received = exchange(arrived, step)
     return (parts[step - 1] + received.astype(f32)).astype(bf16)
 
 
@@ -198,37 +195,56 @@
         out_specs=[VMEM] * 2,
         compiler_params=pltpu.CompilerParams(vmem_limit_bytes=VMEM_LIMIT),
     )(recv)
-    token_next, grad_next = lax.optimization_barrier(
-        (exchange(token_rows, 0, 0), exchange(grad_rows, 0, 1))
-    )
-    token_held = [jnp.stack([token_rows, token_next])]
-    grad_held = [jnp.stack([grad_rows, grad_next])]
+    grad_full = lax.all_gather(grad_rows, "etp", axis=1, tiled=True)
+    held = [jnp.stack([token_rows, exchange(token_rows, 0)])]
     for step in range(1, steps):
-        token_held.append(exchange(token_held[-1], step, 0))
-        grad_held.append(exchange(grad_held[-1], step, 1))
+        held.append(exchange(held[-1], step))
     gate_weight, up_weight, down_weight = w_gate[0].T, w_up[0].T, w_down[0]
     weights = [gate_weight, up_weight, down_weight]
     hidden_width, width = down_weight.shape
     square = jax.ShapeDtypeStruct((slots, hidden_width), f32)
     pair_shape = (2, slots, local_width)
-    flops = 2 * slots * hidden_width * width
-    gate, up, *out_parts = call(
-        forward_kernel, steps, token_held + weights, [square, square], pair_shape, 3 * flops
+    cost = pl.CostEstimate(
+        flops=6 * slots * hidden_width * width, bytes_accessed=9 << 20, transcendentals=0
     )
-    input_parts = call(
-        backward_kernel, steps, grad_held + weights + [gate, up], [], pair_shape, 3 * flops
-    )
-    out_sum, input_sum = out_parts[-1], input_parts[-1]
+    params = pltpu.CompilerParams(vmem_limit_bytes=VMEM_LIMIT)
+    operands = held + weights
+    shapes = [square, square] + [
+        jax.ShapeDtypeStruct(pair_shape, f32 if k < steps - 1 else bf16) for k in range(steps)
+    ]
+    gate, up, *parts = pl.pallas_call(
+        lambda *refs: forward_kernel(steps, *refs),
+        out_shape=shapes,
+        in_specs=[VMEM] * len(operands),
+        out_specs=[VMEM] * len(shapes),
+        compiler_params=params,
+        cost_estimate=cost,
+    )(*operands)
+    input_part = pl.pallas_call(
+        backward_kernel,
+        out_shape=jax.ShapeDtypeStruct((slots, width), bf16),
+        in_specs=[ANY] + [VMEM] * 5,
+        out_specs=ANY,
+        scratch_shapes=[
+            pltpu.VMEM((slots, width), bf16),
+            pltpu.VMEM((slots, width), bf16),
+            pltpu.SemaphoreType.DMA((CHUNKS,)),
+            pltpu.SemaphoreType.DMA((CHUNKS,)),
+        ],
+        compiler_params=params,
+        cost_estimate=cost,
+    )(grad_full, *weights, gate, up)
+    input_local = lax.psum_scatter(input_part, "etp", scatter_dimension=1, tiled=True)
+    out_sum = parts[-1]
     for step in reversed(range(1, steps)):
-        out_sum = sum_step(out_parts, out_sum, step, 0)
-        input_sum = sum_step(input_parts, input_sum, step, 1)
+        out_sum = sum_step(parts, out_sum, step)
     unsorted = pl.pallas_call(
         lambda *refs: unsort_kernel(capacity, *refs),
         out_shape=jax.ShapeDtypeStruct((rows, local_width), bf16),
-        in_specs=[VMEM] * 4,
+        in_specs=[VMEM] * 3,
         out_specs=VMEM,
-        compiler_params=pltpu.CompilerParams(vmem_limit_bytes=VMEM_LIMIT),
-    )(out_sum, exchange(out_sum[1], 0, 0), input_sum, exchange(input_sum[1], 0, 1))
+        compiler_params=params,
+    )(out_sum, exchange(out_sum[1], 0), input_local)
     back = lax.all_to_all(
         unsorted.reshape(owners, 2 * capacity, local_width), "ep", split_axis=0, concat_axis=0, tiled=True
     ).reshape(rows, local_width)

time: 189 us -> 217 us (1.15)
  waiting for transfers between devices: 43.2 us -> 64.7 us
  starting transfers between devices: 46.7 us -> 28.4 us
  between operations: 0.93 us -> 14.3 us
  local copies, waits for them, and re-layouts: 5.76 us -> 15.1 us
    ppermute x16 -> x8, waiting for transfers between devices: 43.2 us -> 64.6 us  [exchange(): return lax.ppermute(value, ('etp', 'ep'), pairs)]
    ppermute x16 -> x8, starting transfers between devices: 46.7 us -> 28.3 us  [exchange(): return lax.ppermute(value, ('etp', 'ep'), pairs)]
    unnamed x18 -> x44, local copies, waits for them, and re-layouts: 4.23 us -> 13.7 us
  transfers between devices with their start and end apart: 16 -> 10, of which waited for: 15 -> 8; matrix products, arithmetic and copies ran while one was open for 0% -> 1% of each run, Pallas kernels for 2% -> 1%
where the time goes in v4:
time: 217 us; the launch traced here: 215 us
  blocking collectives  83.9 us (39%)
  waiting for transfers between devices  64.7 us (30%)
  starting transfers between devices  28.4 us (13%)
  local copies, waits for them, and re-layouts  15.1 us (7%)
  between operations  14.3 us (7%)
  Pallas kernels  7.7 us (4%)
    ppermute x8, waiting for transfers between devices, exchange(): return lax.ppermute(value, ('etp', 'ep'), pairs)  64.6 us
    all_to_all x1, blocking collectives, on_device(): lax.all_to_all(unsorted.reshape(owners, 2 * capacity, local_width), 'ep',...  42.4 us
    all_to_all x1, blocking collectives, on_device(): lax.all_to_all(send.reshape(owners, 2 * capacity, local_width), 'ep', spl...  41.5 us
    ppermute x8, starting transfers between devices, exchange(): return lax.ppermute(value, ('etp', 'ep'), pairs)  28.3 us
    unnamed x44, local copies, waits for them, and re-layouts  13.7 us
  transfers between devices with their start and end apart: 10, of which 8 were waited for; matrix products, arithmetic and copies ran while one was open for 1% of the time, Pallas kernels for 1%

profile of v4, /device:TPU:1, one launch (start us, length us, event | category | flops | bytes accessed | tf_op | source)
XLA Modules:
  0.0 215.4 jit_solution(6915964715340027416)
XLA Ops:
  7.2 0.7 copy-done.14
  7.9 0.7 copy-done.16
  8.6 0.7 copy-done.18
  9.3 0.7 copy-done.19
  10.0 0.7 shard_map.86
  10.8 0.1 reshape.16
  10.9 41.5 %all_to_all.10 = bf16[96,4,512]{2,1,0:T(4,128)(2,1)} all-to-all(bf16[96,4,512]{2,1,0:T(4,128)(2,1)S(1)} %reshape.16), channel_id=1, replica_groups=mesh['etp'=8,'ep'=96] {'ep'}, dimensions={0} | all-to-all | bytes 786432 | tf_op jit(solution)/shard_map/all_to_all | solution.py:187
  52.4 1.1 reshape.17.refs_0_
  53.5 0.4 shard_map.87
  53.9 0.7 copy-done.12
  54.6 0.7 copy-done.13
  55.3 0.0 reduce-scatter.2.cloned.1.call-start
  55.3 5.1 %collective-permute-start = (bf16[192,512]{1,0:T(8,128)(2,1)}, bf16[192,512]{1,0:T(8,128)(2,1)S(1)}, u32[]{:S(2)}, u32[]{:S(2)}) collective-permute-start(bf16[192,512]{1,0:T(8,128)(2,1)} %copy-done.13), channel_id=1, source_target_pairs={{0,96},{1,673},{2,98},{3,675},{4,100},{5,677},{6,102},{7,679},{8,1... | collective-permute-start | bytes 589832 | tf_op jit(solution)/shard_map/ppermute | solution.py:105
  60.4 3.3 %collective-permute-done = bf16[192,512]{1,0:T(8,128)(2,1)S(1)} collective-permute-done((bf16[192,512]{1,0:T(8,128)(2,1)}, bf16[192,512]{1,0:T(8,128)(2,1)S(1)}, u32[]{:S(2)}, u32[]{:S(2)}) %collective-permute-start) | collective-permute-done | bytes 196640 | tf_op jit(solution)/shard_map/ppermute | solution.py:105
  63.7 1.0 pad_maximum_fusion.refs_0_
  64.7 1.9 collective-permute-start.1
  66.6 11.4 %collective-permute-done.1.refs_1_ = bf16[2,192,512]{2,1,0:T(8,128)(2,1)S(1)} collective-permute-done((bf16[2,192,512]{2,1,0:T(8,128)(2,1)S(1)}, bf16[2,192,512]{2,1,0:T(8,128)(2,1)S(1)}, u32[]{:S(2)}, u32[]{:S(2)}) %collective-permute-start.1) | collective-permute-done | bytes 393248 | tf_op jit(solution)/shard_map/ppermute | solution.py:105
  77.9 5.3 %collective-permute-start.2 = (bf16[2,192,512]{2,1,0:T(8,128)(2,1)S(1)}, bf16[2,192,512]{2,1,0:T(8,128)(2,1)S(1)}, u32[]{:S(2)}, u32[]{:S(2)}) collective-permute-start(bf16[2,192,512]{2,1,0:T(8,128)(2,1)S(1)} %collective-permute-done.1.refs_1_), channel_id=1, source_target_pairs={{0,96},{1,673},{2,98},{3,675},{4,100},{5,677},{6,102},{7,679},{8,1... | collective-permute-start | bytes 1179656 | tf_op jit(solution)/shard_map/ppermute | solution.py:105
  83.2 10.5 %collective-permute-done.2.refs_2_ = bf16[2,192,512]{2,1,0:T(8,128)(2,1)S(1)} collective-permute-done((bf16[2,192,512]{2,1,0:T(8,128)(2,1)S(1)}, bf16[2,192,512]{2,1,0:T(8,128)(2,1)S(1)}, u32[]{:S(2)}, u32[]{:S(2)}) %collective-permute-start.2) | collective-permute-done | bytes 393248 | tf_op jit(solution)/shard_map/ppermute | solution.py:105
  93.8 1.9 collective-permute-start.3
  95.7 6.9 %collective-permute-done.3.refs_3_ = bf16[2,192,512]{2,1,0:T(8,128)(2,1)S(1)} collective-permute-done((bf16[2,192,512]{2,1,0:T(8,128)(2,1)S(1)}, bf16[2,192,512]{2,1,0:T(8,128)(2,1)S(1)}, u32[]{:S(2)}, u32[]{:S(2)}) %collective-permute-start.3) | collective-permute-done | bytes 393248 | tf_op jit(solution)/shard_map/ppermute | solution.py:105
  102.6 1.4 copy-done.2
  104.0 1.5 shard_map.88
  105.5 0.9 copy-done.5
  106.4 0.9 copy-done.7
  107.3 0.9 copy-done.9
  108.2 0.8 copy-done.20
  108.9 1.4 copy-done.3
  110.3 1.4 copy-done.4
  111.7 3.5 %shard_map.89 = bf16[192,4096]{1,0:T(8,128)(2,1)} custom-call(bf16[192,4096]{1,0:T(8,128)(2,1)S(1)} %copy-done.4, bf16[192,4096]{1,0:T(8,128)(2,1)S(1)} %bitcast.14, bf16[192,4096]{1,0:T(8,128)(2,1)S(1)} %bitcast.16, bf16[192,4096]{1,0:T(8,128)(2,1)S(1)} %bitcast.18, f32[192,192]{1,0:T(8,128)S(1)} %get-tuple-element.16.gate_ref, ...), custom_call_target="tpu_custom_call" | custom-call | flops 905969664 | bytes 9437184 | tf_op jit(solution)/shard_map/pallas_call | solution.py:223
  115.3 0.9 copy-done.21
  116.2 1.9 collective-permute-start.4
  118.1 6.6 %collective-permute-done.4 = bf16[2,192,512]{2,1,0:T(8,128)(2,1)S(1)} collective-permute-done((bf16[2,192,512]{2,1,0:T(8,128)(2,1)S(1)}, bf16[2,192,512]{2,1,0:T(8,128)(2,1)S(1)}, u32[]{:S(2)}, u32[]{:S(2)}) %collective-permute-start.4) | collective-permute-done | bytes 393248 | tf_op jit(solution)/shard_map/ppermute | solution.py:105
  124.7 0.1 add_convert_fusion.2
  124.9 4.0 %collective-permute-start.5 = (bf16[2,192,512]{2,1,0:T(8,128)(2,1)S(1)}, bf16[2,192,512]{2,1,0:T(8,128)(2,1)S(1)}, u32[]{:S(2)}, u32[]{:S(2)}) collective-permute-start(bf16[2,192,512]{2,1,0:T(8,128)(2,1)S(1)} %add_convert_fusion.2), channel_id=1, source_target_pairs={{0,96},{1,673},{2,98},{3,675},{4,100},{5,677},{6,102},{7,679},{8,1... | collective-permute-start | bytes 1179656 | tf_op jit(solution)/shard_map/ppermute | solution.py:105
  128.9 7.5 %collective-permute-done.5 = bf16[2,192,512]{2,1,0:T(8,128)(2,1)S(1)} collective-permute-done((bf16[2,192,512]{2,1,0:T(8,128)(2,1)S(1)}, bf16[2,192,512]{2,1,0:T(8,128)(2,1)S(1)}, u32[]{:S(2)}, u32[]{:S(2)}) %collective-permute-start.5) | collective-permute-done | bytes 393248 | tf_op jit(solution)/shard_map/ppermute | solution.py:105
  136.4 0.1 add_convert_fusion.1
  136.5 1.9 collective-permute-start.6
  138.4 14.4 %collective-permute-done.6 = bf16[2,192,512]{2,1,0:T(8,128)(2,1)S(1)} collective-permute-done((bf16[2,192,512]{2,1,0:T(8,128)(2,1)S(1)}, bf16[2,192,512]{2,1,0:T(8,128)(2,1)S(1)}, u32[]{:S(2)}, u32[]{:S(2)}) %collective-permute-start.6) | collective-permute-done | bytes 393248 | tf_op jit(solution)/shard_map/ppermute | solution.py:105
  152.8 0.1 add_convert_fusion.refs_0_
  153.0 6.3 %collective-permute-start.7 = (bf16[192,512]{1,0:T(8,128)(2,1)S(1)}, bf16[192,512]{1,0:T(8,128)(2,1)S(1)}, u32[]{:S(2)}, u32[]{:S(2)}) collective-permute-start(bf16[192,512]{1,0:T(8,128)(2,1)S(1)} %slice_bitcast_fusion), channel_id=1, source_target_pairs={{0,96},{1,673},{2,98},{3,675},{4,100},{5,677},{6,102},{7,679},{8,1... | collective-permute-start | bytes 589832 | tf_op jit(solution)/shard_map/ppermute | solution.py:105
  159.3 4.1 %collective-permute-done.7.refs_1_ = bf16[192,512]{1,0:T(8,128)(2,1)S(1)} collective-permute-done((bf16[192,512]{1,0:T(8,128)(2,1)S(1)}, bf16[192,512]{1,0:T(8,128)(2,1)S(1)}, u32[]{:S(2)}, u32[]{:S(2)}) %collective-permute-start.7) | collective-permute-done | bytes 196640 | tf_op jit(solution)/shard_map/ppermute | solution.py:105
  163.4 0.9 copy-done.11
  164.4 0.4 shard_map.90
  164.7 0.1 reshape.18
  164.8 42.4 %all_to_all.11 = bf16[96,4,512]{2,1,0:T(4,128)(2,1)S(1)} all-to-all(bf16[96,4,512]{2,1,0:T(4,128)(2,1)S(1)} %reshape.18), channel_id=1, replica_groups=mesh['etp'=8,'ep'=96] {'ep'}, dimensions={0} | all-to-all | bytes 786432 | tf_op jit(solution)/shard_map/all_to_all | solution.py:248
  207.2 0.1 reshape.19.refs_2_
  207.3 1.2 shard_map.91
  (35 shorter events, 0.2 us)
Async XLA Ops:
  7.2 101.8 %all-gather.2.cloned.1.call-start = ((), (), s32[]{:S(2)}) async-start(), calls=%async_computation.3 | async-start | bytes 1769472 | tf_op jit(solution)/shard_map/all_gather | solution.py:198
  7.2 0.7 copy-start.14
  7.9 0.7 copy-start.16
  8.6 0.7 copy-start.18
  9.3 0.7 copy-start.19
  10.8 91.8 %copy-start.1 = (bf16[1,4096,192]{1,2,0:T(8,128)(2,1)S(1)}, bf16[1,4096,192]{1,2,0:T(8,128)(2,1)}, u32[]{:S(2)}) copy-start(bf16[1,4096,192]{1,2,0:T(8,128)(2,1)} %param.12) | copy-start | bytes 4718596
  10.9 91.7 %copy-start = (bf16[1,4096,192]{1,2,0:T(8,128)(2,1)S(1)}, bf16[1,4096,192]{1,2,0:T(8,128)(2,1)}, u32[]{:S(2)}) copy-start(bf16[1,4096,192]{1,2,0:T(8,128)(2,1)} %param.11) | copy-start | bytes 4718596
  53.9 0.7 copy-start.12
  54.6 0.7 copy-start.13
  55.3 108.1 %reduce-scatter.2.cloned.1.call-start = ((), (), s32[]{:S(2)}) async-start(), calls=%async_computation.4 | async-start | bytes 1769472 | tf_op jit(solution)/shard_map/reduce_scatter | solution.py:237
  55.3 8.4 %collective-permute-start = (bf16[192,512]{1,0:T(8,128)(2,1)}, bf16[192,512]{1,0:T(8,128)(2,1)S(1)}, u32[]{:S(2)}, u32[]{:S(2)}) collective-permute-start(bf16[192,512]{1,0:T(8,128)(2,1)} %copy-done.13), channel_id=1, source_target_pairs={{0,96},{1,673},{2,98},{3,675},{4,100},{5,677},{6,102},{7,679},{8,1... | collective-permute-start | bytes 589832 | tf_op jit(solution)/shard_map/ppermute | solution.py:105
  64.7 13.3 %collective-permute-start.1 = (bf16[2,192,512]{2,1,0:T(8,128)(2,1)S(1)}, bf16[2,192,512]{2,1,0:T(8,128)(2,1)S(1)}, u32[]{:S(2)}, u32[]{:S(2)}) collective-permute-start(bf16[2,192,512]{2,1,0:T(8,128)(2,1)S(1)} %pad_maximum_fusion.refs_0_), channel_id=1, source_target_pairs={{0,672},{1,97},{2,674},{3,99},{4,676},{5,101},{6,678},{7,103},{8,6... | collective-permute-start | bytes 1179656 | tf_op jit(solution)/shard_map/ppermute | solution.py:105
  77.9 15.8 %collective-permute-start.2 = (bf16[2,192,512]{2,1,0:T(8,128)(2,1)S(1)}, bf16[2,192,512]{2,1,0:T(8,128)(2,1)S(1)}, u32[]{:S(2)}, u32[]{:S(2)}) collective-permute-start(bf16[2,192,512]{2,1,0:T(8,128)(2,1)S(1)} %collective-permute-done.1.refs_1_), channel_id=1, source_target_pairs={{0,96},{1,673},{2,98},{3,675},{4,100},{5,677},{6,102},{7,679},{8,1... | collective-permute-start | bytes 1179656 | tf_op jit(solution)/shard_map/ppermute | solution.py:105
  93.8 8.8 %collective-permute-start.3 = (bf16[2,192,512]{2,1,0:T(8,128)(2,1)S(1)}, bf16[2,192,512]{2,1,0:T(8,128)(2,1)S(1)}, u32[]{:S(2)}, u32[]{:S(2)}) collective-permute-start(bf16[2,192,512]{2,1,0:T(8,128)(2,1)S(1)} %collective-permute-done.2.refs_2_), channel_id=1, source_target_pairs={{0,672},{1,97},{2,674},{3,99},{4,676},{5,101},{6,678},{7,103},{8,6... | collective-permute-start | bytes 1179656 | tf_op jit(solution)/shard_map/ppermute | solution.py:105
  102.6 1.4 copy-start.2
  105.5 0.9 copy-start.5
  106.4 0.9 copy-start.7
  107.3 0.9 copy-start.9
  108.2 0.8 copy-start.20
  108.9 1.4 copy-start.3
  110.3 1.4 copy-start.4
  115.2 1.0 copy-start.21
  115.2 9.5 %copy-start.10 = (f32[2,192,512]{2,1,0:T(8,128)S(1)}, f32[2,192,512]{2,1,0:T(8,128)}, u32[]{:S(2)}) copy-start(f32[2,192,512]{2,1,0:T(8,128)} %copy-done.9) | copy-start | bytes 2359300
  115.2 21.1 %copy-start.8 = (f32[2,192,512]{2,1,0:T(8,128)S(1)}, f32[2,192,512]{2,1,0:T(8,128)}, u32[]{:S(2)}) copy-start(f32[2,192,512]{2,1,0:T(8,128)} %copy-done.7) | copy-start | bytes 2359300
  116.2 8.5 %collective-permute-start.4 = (bf16[2,192,512]{2,1,0:T(8,128)(2,1)S(1)}, bf16[2,192,512]{2,1,0:T(8,128)(2,1)S(1)}, u32[]{:S(2)}, u32[]{:S(2)}) collective-permute-start(bf16[2,192,512]{2,1,0:T(8,128)(2,1)S(1)} %copy-done.21), channel_id=1, source_target_pairs={{0,672},{1,97},{2,674},{3,99},{4,676},{5,101},{6,678},{7,103},{8,6... | collective-permute-start | bytes 1179656 | tf_op jit(solution)/shard_map/ppermute | solution.py:105
  124.7 28.1 %copy-start.6 = (f32[2,192,512]{2,1,0:T(8,128)S(1)}, f32[2,192,512]{2,1,0:T(8,128)}, u32[]{:S(2)}) copy-start(f32[2,192,512]{2,1,0:T(8,128)} %copy-done.5) | copy-start | bytes 2359300
  124.9 11.5 %collective-permute-start.5 = (bf16[2,192,512]{2,1,0:T(8,128)(2,1)S(1)}, bf16[2,192,512]{2,1,0:T(8,128)(2,1)S(1)}, u32[]{:S(2)}, u32[]{:S(2)}) collective-permute-start(bf16[2,192,512]{2,1,0:T(8,128)(2,1)S(1)} %add_convert_fusion.2), channel_id=1, source_target_pairs={{0,96},{1,673},{2,98},{3,675},{4,100},{5,677},{6,102},{7,679},{8,1... | collective-permute-start | bytes 1179656 | tf_op jit(solution)/shard_map/ppermute | solution.py:105
  136.5 16.3 %collective-permute-start.6 = (bf16[2,192,512]{2,1,0:T(8,128)(2,1)S(1)}, bf16[2,192,512]{2,1,0:T(8,128)(2,1)S(1)}, u32[]{:S(2)}, u32[]{:S(2)}) collective-permute-start(bf16[2,192,512]{2,1,0:T(8,128)(2,1)S(1)} %add_convert_fusion.1), channel_id=1, source_target_pairs={{0,672},{1,97},{2,674},{3,99},{4,676},{5,101},{6,678},{7,103},{8,6... | collective-permute-start | bytes 1179656 | tf_op jit(solution)/shard_map/ppermute | solution.py:105
  153.0 54.3 %copy-start.15 = (s32[16,8]{0,1:T(8,128)S(1)}, s32[16,8]{0,1:T(8,128)}, u32[]{:S(2)}) copy-start(s32[16,8]{0,1:T(8,128)} %param.8) | copy-start | bytes 1540
  153.0 54.3 %copy-start.17 = (f32[16,8]{0,1:T(8,128)S(1)}, f32[16,8]{0,1:T(8,128)}, u32[]{:S(2)}) copy-start(f32[16,8]{0,1:T(8,128)} %param.9) | copy-start | bytes 1540
  153.0 10.4 %collective-permute-start.7 = (bf16[192,512]{1,0:T(8,128)(2,1)S(1)}, bf16[192,512]{1,0:T(8,128)(2,1)S(1)}, u32[]{:S(2)}, u32[]{:S(2)}) collective-permute-start(bf16[192,512]{1,0:T(8,128)(2,1)S(1)} %slice_bitcast_fusion), channel_id=1, source_target_pairs={{0,96},{1,673},{2,98},{3,675},{4,100},{5,677},{6,102},{7,679},{8,1... | collective-permute-start | bytes 589832 | tf_op jit(solution)/shard_map/ppermute | solution.py:105
  163.4 0.9 copy-start.11
Sparse Core Ops, SparseCore 0:
  55.4 37.2 all-gather.1
  115.4 42.7 reduce-scatter.1

commit v5 on v3

--- a/solution.py
+++ b/solution.py
@@ -8,7 +8,8 @@
 bf16 = jnp.bfloat16
 f32 = jnp.float32
 VMEM = pl.BlockSpec(memory_space=pltpu.VMEM)
-VMEM_LIMIT = 28 * 1024 * 1024
+VMEM_LIMIT = 24 * 1024 * 1024
+SHARES = 2
 
 
 def dot_last(left, right):
@@ -60,20 +61,29 @@
     send[...] = out.astype(bf16)
 
 
-def sort_kernel(capacity, recv, token_rows, grad_rows):
+def sort_kernel(capacity, recv, *out):
     rows = recv.shape[0]
-    for kind, out in ((0, token_rows), (1, grad_rows)):
+    count = len(out) // 2
+    for kind in (0, 1):
         shape = (rows // 2, rows)
         source = travel_row(lax.broadcasted_iota(jnp.int32, shape, 0), kind, capacity)
         place = (source == lax.broadcasted_iota(jnp.int32, shape, 1)).astype(f32).astype(bf16)
-        out[...] = dot(place, recv[...]).astype(bf16)
-
-
-def unsort_kernel(capacity, out_sum, out_last, input_sum, input_last, unsorted):
+        value = dot(place, recv[...]).astype(bf16)
+        size = value.shape[0] // count
+        for h in range(count):
+            out[kind * count + h][...] = value[h * size : (h + 1) * size]
+
+
+def unsort_kernel(capacity, *refs):
+    unsorted = refs[-1]
     rows = unsorted.shape[0]
     total = None
-    for kind, held, last in ((0, out_sum, out_last), (1, input_sum, input_last)):
-        local = (held[0].astype(f32) + last[...].astype(f32)).astype(bf16)
+    for kind in (0, 1):
+        shares = []
+        for h in range(SHARES):
+            held, last = refs[2 * (kind * SHARES + h) : 2 * (kind * SHARES + h) + 2]
+            shares.append((held[0].astype(f32) + last[...].astype(f32)).astype(bf16))
+        local = jnp.concatenate(shares, axis=0)
         shape = (rows, rows // 2)
         target = travel_row(lax.broadcasted_iota(jnp.int32, shape, 1), kind, capacity)
         place = (target == lax.broadcasted_iota(jnp.int32, shape, 0)).astype(f32).astype(bf16)
@@ -115,15 +125,31 @@
     return out
 
 
+def split_refs(steps, refs):
+    count = steps * SHARES
+    held = [refs[k * SHARES : (k + 1) * SHARES] for k in range(steps)]
+    last = refs[count + 5 :]
+    parts = [last[k * SHARES : (k + 1) * SHARES] for k in range(steps)]
+    return held, refs[count : count + 3], refs[count + 3 : count + 5], parts
+
+
+def rows_of(shares, block):
+    return jnp.concatenate([share[block] for share in shares], axis=0)
+
+
+def store(shares, block, value):
+    count = value.shape[0] // SHARES
+    for h, share in enumerate(shares):
+        share[block] = value[h * count : (h + 1) * count].astype(share.dtype)
+
+
 def forward_kernel(steps, *refs):
-    held, (gate_w, up_w, down_w) = refs[:steps], refs[steps : steps + 3]
-    gate_ref, up_ref = refs[steps + 3 : steps + 5]
-    parts = refs[steps + 5 :]
-    columns = columns_of(steps, held[0].shape[2], 0)
+    held, (gate_w, up_w, down_w), (gate_ref, up_ref), parts = split_refs(steps, refs)
+    columns = columns_of(steps, held[0][0].shape[2], 0)
     gate = up = None
     for k in range(steps):
         for b in (0, 1):
-            rows = held[k][b]
+            rows = rows_of(held[k], b)
             gate_now = dot_last(rows, gate_w[:, columns[k][b]])
             up_now = dot_last(rows, up_w[:, columns[k][b]])
             gate = gate_now if gate is None else gate + gate_now
@@ -133,18 +159,16 @@
     hidden = (gate * jax.nn.sigmoid(gate) * up).astype(bf16)
     for k in reversed(range(steps)):
         for b in (0, 1):
-            parts[k][b] = dot(hidden, down_w[:, columns[k][b]]).astype(parts[k].dtype)
+            store(parts[k], b, dot(hidden, down_w[:, columns[k][b]]))
 
 
 def backward_kernel(steps, *refs):
-    held, (gate_w, up_w, down_w) = refs[:steps], refs[steps : steps + 3]
-    gate_ref, up_ref = refs[steps + 3 : steps + 5]
-    parts = refs[steps + 5 :]
-    columns = columns_of(steps, held[0].shape[2], 1)
+    held, (gate_w, up_w, down_w), (gate_ref, up_ref), parts = split_refs(steps, refs)
+    columns = columns_of(steps, held[0][0].shape[2], 1)
     hidden_grad = None
     for k in range(steps):
         for b in (0, 1):
-            now = dot_last(held[k][b], down_w[:, columns[k][b]])
+            now = dot_last(rows_of(held[k], b), down_w[:, columns[k][b]])
             hidden_grad = now if hidden_grad is None else hidden_grad + now
     gate, up = gate_ref[...], up_ref[...]
     squash = jax.nn.sigmoid(gate)
@@ -153,12 +177,14 @@
     for k in reversed(range(steps)):
         for b in (0, 1):
             part = dot(gate_grad, gate_w[:, columns[k][b]]) + dot(up_grad, up_w[:, columns[k][b]])
-            parts[k][b] = part.astype(parts[k].dtype)
+            store(parts[k], b, part)
 
 
 def call(kernel, steps, operands, extra_shapes, pair_shape, flops):
     shapes = extra_shapes + [
-        jax.ShapeDtypeStruct(pair_shape, f32 if k < steps - 1 else bf16) for k in range(steps)
+        jax.ShapeDtypeStruct(pair_shape, f32 if k < steps - 1 else bf16)
+        for k in range(steps)
+        for _ in range(SHARES)
     ]
     return pl.pallas_call(
         lambda *refs: kernel(steps, *refs),
@@ -170,9 +196,8 @@
     )(*operands)
 
 
-def sum_step(parts, arrived, step, chain):
-    received = exchange(arrived, step, chain)
-    return (parts[step - 1] + received.astype(f32)).astype(bf16)
+def sum_step(part, arrived, step, chain):
+    return (part + exchange(arrived, step, chain).astype(f32)).astype(bf16)
 
 
 def on_device(tokens, routes, route_weight, grad_out, w_gate, w_up, w_down):
@@ -190,27 +215,28 @@
     recv = lax.all_to_all(
         send.reshape(owners, 2 * capacity, local_width), "ep", split_axis=0, concat_axis=0, tiled=True
     ).reshape(rows, local_width)
-    half = jax.ShapeDtypeStruct((slots, local_width), bf16)
-    token_rows, grad_rows = pl.pallas_call(
+    share = jax.ShapeDtypeStruct((slots // SHARES, local_width), bf16)
+    own = pl.pallas_call(
         lambda *refs: sort_kernel(capacity, *refs),
-        out_shape=[half, half],
+        out_shape=[share] * (2 * SHARES),
         in_specs=[VMEM],
-        out_specs=[VMEM] * 2,
+        out_specs=[VMEM] * (2 * SHARES),
         compiler_params=pltpu.CompilerParams(vmem_limit_bytes=VMEM_LIMIT),
     )(recv)
-    token_next, grad_next = lax.optimization_barrier(
-        (exchange(token_rows, 0, 0), exchange(grad_rows, 0, 1))
-    )
-    token_held = [jnp.stack([token_rows, token_next])]
-    grad_held = [jnp.stack([grad_rows, grad_next])]
+    kinds = [q // SHARES for q in range(2 * SHARES)]
+    arrived = lax.optimization_barrier([exchange(own[q], 0, kinds[q]) for q in range(2 * SHARES)])
+    held = [[jnp.stack([own[q], arrived[q]])] for q in range(2 * SHARES)]
     for step in range(1, steps):
-        token_held.append(exchange(token_held[-1], step, 0))
-        grad_held.append(exchange(grad_held[-1], step, 1))
+        for q in range(2 * SHARES):
+            held[q].append(exchange(held[q][-1], step, kinds[q]))
+    token_held, grad_held = (
+        [held[kind * SHARES + h][k] for k in range(steps) for h in range(SHARES)] for kind in (0, 1)
+    )
     gate_weight, up_weight, down_weight = w_gate[0].T, w_up[0].T, w_down[0]
     weights = [gate_weight, up_weight, down_weight]
     hidden_width, width = down_weight.shape
     square = jax.ShapeDtypeStruct((slots, hidden_width), f32)
-    pair_shape = (2, slots, local_width)
+    pair_shape = (2, slots // SHARES, local_width)
     flops = 2 * slots * hidden_width * width
     gate, up, *out_parts = call(
         forward_kernel, steps, token_held + weights, [square, square], pair_shape, 3 * flops
@@ -218,17 +244,22 @@
     input_parts = call(
         backward_kernel, steps, grad_held + weights + [gate, up], [], pair_shape, 3 * flops
     )
-    out_sum, input_sum = out_parts[-1], input_parts[-1]
+    parts = [
+        [(out_parts, input_parts)[kind][k * SHARES + h] for k in range(steps)]
+        for kind in (0, 1)
+        for h in range(SHARES)
+    ]
+    sums = [parts[q][-1] for q in range(2 * SHARES)]
     for step in reversed(range(1, steps)):
-        out_sum = sum_step(out_parts, out_sum, step, 0)
-        input_sum = sum_step(input_parts, input_sum, step, 1)
+        sums = [sum_step(parts[q][step - 1], sums[q], step, kinds[q]) for q in range(2 * SHARES)]
+    ends = [ref for q in range(2 * SHARES) for ref in (sums[q], exchange(sums[q][1], 0, kinds[q]))]
     unsorted = pl.pallas_call(
         lambda *refs: unsort_kernel(capacity, *refs),
         out_shape=jax.ShapeDtypeStruct((rows, local_width), bf16),
-        in_specs=[VMEM] * 4,
+        in_specs=[VMEM] * len(ends),
         out_specs=VMEM,
         compiler_params=pltpu.CompilerParams(vmem_limit_bytes=VMEM_LIMIT),
-    )(out_sum, exchange(out_sum[1], 0, 0), input_sum, exchange(input_sum[1], 0, 1))
+    )(*ends)
     back = lax.all_to_all(
         unsorted.reshape(owners, 2 * capacity, local_width), "ep", split_axis=0, concat_axis=0, tiled=True
     ).reshape(rows, local_width)

time: 189 us -> 199 us (1.053)
  starting transfers between devices: 46.7 us -> 95 us
  waiting for transfers between devices: 43.2 us -> 5.69 us
    ppermute x16 -> x32, starting transfers between devices: 46.7 us -> 95 us  [exchange(): return lax.ppermute(value, ('etp', 'ep'), pairs)]
    ppermute x16 -> x32, waiting for transfers between devices: 43.2 us -> 5.69 us  [exchange(): return lax.ppermute(value, ('etp', 'ep'), pairs)]
  transfers between devices with their start and end apart: 16 -> 32, of which waited for: 15 -> 4; matrix products, arithmetic and copies ran while one was open for 0% -> 0% of each run, Pallas kernels for 2% -> 2%
where the time goes in v5:
time: 199 us; the launch traced here: 198 us
  starting transfers between devices  95 us (48%)
  blocking collectives  82.5 us (41%)
  Pallas kernels  6.58 us (3%)
  local copies, waits for them, and re-layouts  5.76 us (3%)
  waiting for transfers between devices  5.69 us (3%)
    ppermute x32, starting transfers between devices, exchange(): return lax.ppermute(value, ('etp', 'ep'), pairs)  95 us
    all_to_all x1, blocking collectives, on_device(): lax.all_to_all(send.reshape(owners, 2 * capacity, local_width), 'ep', spl...  41.5 us
    all_to_all x1, blocking collectives, on_device(): lax.all_to_all(unsorted.reshape(owners, 2 * capacity, local_width), 'ep',...  41 us
    ppermute x32, waiting for transfers between devices, exchange(): return lax.ppermute(value, ('etp', 'ep'), pairs)  5.69 us
    unnamed x18, local copies, waits for them, and re-layouts  4.23 us
  transfers between devices with their start and end apart: 32, of which 4 were waited for; matrix products, arithmetic and copies ran while one was open for 0% of the time, Pallas kernels for 2%

profile of v5, /device:TPU:1, one launch (start us, length us, event | category | flops | bytes accessed | tf_op | source)
XLA Modules:
  0.0 197.6 jit_solution(2837643000280446812)
XLA Ops:
  0.6 0.7 copy-done.3
  1.3 0.7 copy-done.5
  2.0 0.7 copy-done.7
  2.7 0.7 copy-done.8
  3.4 0.7 shard_map.86
  4.3 41.5 %all_to_all.10 = bf16[96,4,512]{2,1,0:T(4,128)(2,1)} all-to-all(bf16[96,4,512]{2,1,0:T(4,128)(2,1)S(1)} %reshape.16), channel_id=1, replica_groups=mesh['etp'=8,'ep'=96] {'ep'}, dimensions={0} | all-to-all | bytes 786432 | tf_op jit(solution)/shard_map/all_to_all | solution.py:215
  45.8 1.2 reshape.17.refs_0_
  47.4 5.1 %collective-permute-start = (bf16[96,512]{1,0:T(8,128)(2,1)S(1)}, bf16[96,512]{1,0:T(8,128)(2,1)S(1)}, u32[]{:S(2)}, u32[]{:S(2)}) collective-permute-start(bf16[96,512]{1,0:T(8,128)(2,1)S(1)} %get-tuple-element.28), channel_id=1, source_target_pairs={{0,96},{1,673},{2,98},{3,675},{4,100},{5,677},{6,102},{7,679},{8,1... | collective-permute-start | bytes 294920 | tf_op jit(solution)/shard_map/ppermute | solution.py:113
  52.5 1.9 collective-permute-start.1
  54.5 1.9 collective-permute-start.2
  56.4 3.4 %collective-permute-start.3 = (bf16[96,512]{1,0:T(8,128)(2,1)S(1)}, bf16[96,512]{1,0:T(8,128)(2,1)S(1)}, u32[]{:S(2)}, u32[]{:S(2)}) collective-permute-start(bf16[96,512]{1,0:T(8,128)(2,1)S(1)} %get-tuple-element.31), channel_id=1, source_target_pairs={{0,672},{1,97},{2,674},{3,99},{4,676},{5,101},{6,678},{7,103},{8,6... | collective-permute-start | bytes 294920 | tf_op jit(solution)/shard_map/ppermute | solution.py:113
  59.8 2.2 %collective-permute-done.3 = bf16[96,512]{1,0:T(8,128)(2,1)S(1)} collective-permute-done((bf16[96,512]{1,0:T(8,128)(2,1)S(1)}, bf16[96,512]{1,0:T(8,128)(2,1)S(1)}, u32[]{:S(2)}, u32[]{:S(2)}) %collective-permute-start.3) | collective-permute-done | bytes 98336 | tf_op jit(solution)/shard_map/ppermute | solution.py:113
  62.1 3.1 %collective-permute-start.4 = (bf16[2,96,512]{2,1,0:T(8,128)(2,1)S(1)}, bf16[2,96,512]{2,1,0:T(8,128)(2,1)S(1)}, u32[]{:S(2)}, u32[]{:S(2)}) collective-permute-start(bf16[2,96,512]{2,1,0:T(8,128)(2,1)S(1)} %pad_maximum_fusion.refs_0_), channel_id=1, source_target_pairs={{0,672},{1,97},{2,674},{3,99},{4,676},{5,101},{6,678},{7,103},{8,6... | collective-permute-start | bytes 589832 | tf_op jit(solution)/shard_map/ppermute | solution.py:113
  65.2 2.2 %collective-permute-start.5 = (bf16[2,96,512]{2,1,0:T(8,128)(2,1)S(1)}, bf16[2,96,512]{2,1,0:T(8,128)(2,1)S(1)}, u32[]{:S(2)}, u32[]{:S(2)}) collective-permute-start(bf16[2,96,512]{2,1,0:T(8,128)(2,1)S(1)} %pad_maximum_fusion.1.refs_1_), channel_id=1, source_target_pairs={{0,672},{1,97},{2,674},{3,99},{4,676},{5,101},{6,678},{7,103},{8,6... | collective-permute-start | bytes 589832 | tf_op jit(solution)/shard_map/ppermute | solution.py:113
  67.4 4.6 %collective-permute-start.18 = (bf16[2,96,512]{2,1,0:T(8,128)(2,1)S(1)}, bf16[2,96,512]{2,1,0:T(8,128)(2,1)S(1)}, u32[]{:S(2)}, u32[]{:S(2)}) collective-permute-start(bf16[2,96,512]{2,1,0:T(8,128)(2,1)S(1)} %pad_maximum_fusion.2.refs_0_), channel_id=1, source_target_pairs={{0,96},{1,673},{2,98},{3,675},{4,100},{5,677},{6,102},{7,679},{8,1... | collective-permute-start | bytes 589832 | tf_op jit(solution)/shard_map/ppermute | solution.py:113
  72.0 1.9 collective-permute-start.19
  74.0 4.6 %collective-permute-start.6 = (bf16[2,96,512]{2,1,0:T(8,128)(2,1)S(1)}, bf16[2,96,512]{2,1,0:T(8,128)(2,1)S(1)}, u32[]{:S(2)}, u32[]{:S(2)}) collective-permute-start(bf16[2,96,512]{2,1,0:T(8,128)(2,1)S(1)} %collective-permute-done.4.refs_2_), channel_id=1, source_target_pairs={{0,96},{1,673},{2,98},{3,675},{4,100},{5,677},{6,102},{7,679},{8,1... | collective-permute-start | bytes 589832 | tf_op jit(solution)/shard_map/ppermute | solution.py:113
  78.6 1.9 collective-permute-start.7
  80.5 1.9 collective-permute-start.20
  82.4 3.4 %collective-permute-start.21 = (bf16[2,96,512]{2,1,0:T(8,128)(2,1)S(1)}, bf16[2,96,512]{2,1,0:T(8,128)(2,1)S(1)}, u32[]{:S(2)}, u32[]{:S(2)}) collective-permute-start(bf16[2,96,512]{2,1,0:T(8,128)(2,1)S(1)} %collective-permute-done.19.refs_3_), channel_id=1, source_target_pairs={{0,672},{1,97},{2,674},{3,99},{4,676},{5,101},{6,678},{7,103},{8,6... | collective-permute-start | bytes 589832 | tf_op jit(solution)/shard_map/ppermute | solution.py:113
  85.8 1.9 collective-permute-start.8
  87.8 3.4 %collective-permute-start.9 = (bf16[2,96,512]{2,1,0:T(8,128)(2,1)S(1)}, bf16[2,96,512]{2,1,0:T(8,128)(2,1)S(1)}, u32[]{:S(2)}, u32[]{:S(2)}) collective-permute-start(bf16[2,96,512]{2,1,0:T(8,128)(2,1)S(1)} %collective-permute-done.7.refs_5_), channel_id=1, source_target_pairs={{0,672},{1,97},{2,674},{3,99},{4,676},{5,101},{6,678},{7,103},{8,6... | collective-permute-start | bytes 589832 | tf_op jit(solution)/shard_map/ppermute | solution.py:113
  91.1 4.6 %collective-permute-start.22 = (bf16[2,96,512]{2,1,0:T(8,128)(2,1)S(1)}, bf16[2,96,512]{2,1,0:T(8,128)(2,1)S(1)}, u32[]{:S(2)}, u32[]{:S(2)}) collective-permute-start(bf16[2,96,512]{2,1,0:T(8,128)(2,1)S(1)} %collective-permute-done.20.refs_4_), channel_id=1, source_target_pairs={{0,96},{1,673},{2,98},{3,675},{4,100},{5,677},{6,102},{7,679},{8,1... | collective-permute-start | bytes 589832 | tf_op jit(solution)/shard_map/ppermute | solution.py:113
  95.7 1.9 collective-permute-start.23
  97.7 1.4 copy-done.2
  99.1 1.5 shard_map.88
  100.6 2.8 %collective-permute-start.10 = (bf16[2,96,512]{2,1,0:T(8,128)(2,1)S(1)}, bf16[2,96,512]{2,1,0:T(8,128)(2,1)S(1)}, u32[]{:S(2)}, u32[]{:S(2)}) collective-permute-start(bf16[2,96,512]{2,1,0:T(8,128)(2,1)S(1)} %get-tuple-element.37), channel_id=1, source_target_pairs={{0,672},{1,97},{2,674},{3,99},{4,676},{5,101},{6,678},{7,103},{8,6... | collective-permute-start | bytes 589832 | tf_op jit(solution)/shard_map/ppermute | solution.py:113
  103.4 2.5 %collective-permute-start.14 = (bf16[2,96,512]{2,1,0:T(8,128)(2,1)S(1)}, bf16[2,96,512]{2,1,0:T(8,128)(2,1)S(1)}, u32[]{:S(2)}, u32[]{:S(2)}) collective-permute-start(bf16[2,96,512]{2,1,0:T(8,128)(2,1)S(1)} %get-tuple-element.41), channel_id=1, source_target_pairs={{0,672},{1,97},{2,674},{3,99},{4,676},{5,101},{6,678},{7,103},{8,6... | collective-permute-start | bytes 589832 | tf_op jit(solution)/shard_map/ppermute | solution.py:113
  105.9 2.3 %shard_map.89 = (f32[2,96,512]{2,1,0:T(8,128)S(1)}, f32[2,96,512]{2,1,0:T(8,128)S(1)}, f32[2,96,512]{2,1,0:T(8,128)S(1)}, f32[2,96,512]{2,1,0:T(8,128)S(1)}, f32...) custom-call(bf16[2,96,512]{2,1,0:T(8,128)(2,1)S(1)} %pad_maximum_fus, ...), custom_call_target="tpu_custom_call" | custom-call | flops 905969664 | bytes 9437184 | tf_op jit(solution)/shard_map/pallas_call | solution.py:189
  108.3 4.6 %collective-permute-start.24 = (bf16[2,96,512]{2,1,0:T(8,128)(2,1)S(1)}, bf16[2,96,512]{2,1,0:T(8,128)(2,1)S(1)}, u32[]{:S(2)}, u32[]{:S(2)}) collective-permute-start(bf16[2,96,512]{2,1,0:T(8,128)(2,1)S(1)} %get-tuple-element.49), channel_id=1, source_target_pairs={{0,96},{1,673},{2,98},{3,675},{4,100},{5,677},{6,102},{7,679},{8,1... | collective-permute-start | bytes 589832 | tf_op jit(solution)/shard_map/ppermute | solution.py:113
  112.9 1.9 collective-permute-start.28
  114.9 4.6 %collective-permute-start.11 = (bf16[2,96,512]{2,1,0:T(8,128)(2,1)S(1)}, bf16[2,96,512]{2,1,0:T(8,128)(2,1)S(1)}, u32[]{:S(2)}, u32[]{:S(2)}) collective-permute-start(bf16[2,96,512]{2,1,0:T(8,128)(2,1)S(1)} %add_convert_fusion.11), channel_id=1, source_target_pairs={{0,96},{1,673},{2,98},{3,675},{4,100},{5,677},{6,102},{7,679},{8,1... | collective-permute-start | bytes 589832 | tf_op jit(solution)/shard_map/ppermute | solution.py:113
  119.5 1.9 collective-permute-start.15
  121.5 1.9 collective-permute-start.25
  123.5 3.4 %collective-permute-start.29 = (bf16[2,96,512]{2,1,0:T(8,128)(2,1)S(1)}, bf16[2,96,512]{2,1,0:T(8,128)(2,1)S(1)}, u32[]{:S(2)}, u32[]{:S(2)}) collective-permute-start(bf16[2,96,512]{2,1,0:T(8,128)(2,1)S(1)} %add_convert_fusion.2), channel_id=1, source_target_pairs={{0,672},{1,97},{2,674},{3,99},{4,676},{5,101},{6,678},{7,103},{8,6... | collective-permute-start | bytes 589832 | tf_op jit(solution)/shard_map/ppermute | solution.py:113
  126.9 1.9 collective-permute-start.12
  128.9 3.4 %collective-permute-start.16 = (bf16[2,96,512]{2,1,0:T(8,128)(2,1)S(1)}, bf16[2,96,512]{2,1,0:T(8,128)(2,1)S(1)}, u32[]{:S(2)}, u32[]{:S(2)}) collective-permute-start(bf16[2,96,512]{2,1,0:T(8,128)(2,1)S(1)} %add_convert_fusion.7), channel_id=1, source_target_pairs={{0,672},{1,97},{2,674},{3,99},{4,676},{5,101},{6,678},{7,103},{8,6... | collective-permute-start | bytes 589832 | tf_op jit(solution)/shard_map/ppermute | solution.py:113
  132.3 4.6 %collective-permute-start.26 = (bf16[2,96,512]{2,1,0:T(8,128)(2,1)S(1)}, bf16[2,96,512]{2,1,0:T(8,128)(2,1)S(1)}, u32[]{:S(2)}, u32[]{:S(2)}) collective-permute-start(bf16[2,96,512]{2,1,0:T(8,128)(2,1)S(1)} %add_convert_fusion.4), channel_id=1, source_target_pairs={{0,96},{1,673},{2,98},{3,675},{4,100},{5,677},{6,102},{7,679},{8,1... | collective-permute-start | bytes 589832 | tf_op jit(solution)/shard_map/ppermute | solution.py:113
  137.0 2.2 %collective-permute-start.30 = (bf16[2,96,512]{2,1,0:T(8,128)(2,1)S(1)}, bf16[2,96,512]{2,1,0:T(8,128)(2,1)S(1)}, u32[]{:S(2)}, u32[]{:S(2)}) collective-permute-start(bf16[2,96,512]{2,1,0:T(8,128)(2,1)S(1)} %add_convert_fusion.1), channel_id=1, source_target_pairs={{0,96},{1,673},{2,98},{3,675},{4,100},{5,677},{6,102},{7,679},{8,1... | collective-permute-start | bytes 589832 | tf_op jit(solution)/shard_map/ppermute | solution.py:113
  139.3 4.3 %collective-permute-start.13 = (bf16[96,512]{1,0:T(8,128)(2,1)S(1)}, bf16[96,512]{1,0:T(8,128)(2,1)S(1)}, u32[]{:S(2)}, u32[]{:S(2)}) collective-permute-start(bf16[96,512]{1,0:T(8,128)(2,1)S(1)} %slice_bitcast_fusion.3), channel_id=1, source_target_pairs={{0,96},{1,673},{2,98},{3,675},{4,100},{5,677},{6,102},{7,679},{8,1... | collective-permute-start | bytes 294920 | tf_op jit(solution)/shard_map/ppermute | solution.py:113
  143.6 2.2 %collective-permute-start.17 = (bf16[96,512]{1,0:T(8,128)(2,1)S(1)}, bf16[96,512]{1,0:T(8,128)(2,1)S(1)}, u32[]{:S(2)}, u32[]{:S(2)}) collective-permute-start(bf16[96,512]{1,0:T(8,128)(2,1)S(1)} %slice_bitcast_fusion.2), channel_id=1, source_target_pairs={{0,96},{1,673},{2,98},{3,675},{4,100},{5,677},{6,102},{7,679},{8,1... | collective-permute-start | bytes 294920 | tf_op jit(solution)/shard_map/ppermute | solution.py:113
  146.0 1.9 collective-permute-start.27
  148.0 3.4 %collective-permute-start.31 = (bf16[96,512]{1,0:T(8,128)(2,1)S(1)}, bf16[96,512]{1,0:T(8,128)(2,1)S(1)}, u32[]{:S(2)}, u32[]{:S(2)}) collective-permute-start(bf16[96,512]{1,0:T(8,128)(2,1)S(1)} %slice_bitcast_fusion), channel_id=1, source_target_pairs={{0,672},{1,97},{2,674},{3,99},{4,676},{5,101},{6,678},{7,103},{8,6... | collective-permute-start | bytes 294920 | tf_op jit(solution)/shard_map/ppermute | solution.py:113
  151.6 1.0 collective-permute-done.27.refs_5_
  152.6 2.1 %collective-permute-done.31.refs_7_ = bf16[96,512]{1,0:T(8,128)(2,1)S(1)} collective-permute-done((bf16[96,512]{1,0:T(8,128)(2,1)S(1)}, bf16[96,512]{1,0:T(8,128)(2,1)S(1)}, u32[]{:S(2)}, u32[]{:S(2)}) %collective-permute-start.31) | collective-permute-done | bytes 98336 | tf_op jit(solution)/shard_map/ppermute | solution.py:113
  154.7 0.4 shard_map.90
  155.2 41.0 %all_to_all.11 = bf16[96,4,512]{2,1,0:T(4,128)(2,1)S(1)} all-to-all(bf16[96,4,512]{2,1,0:T(4,128)(2,1)S(1)} %reshape.18), channel_id=1, replica_groups=mesh['etp'=8,'ep'=96] {'ep'}, dimensions={0} | all-to-all | bytes 786432 | tf_op jit(solution)/shard_map/all_to_all | solution.py:263
  196.3 1.2 shard_map.91
  (66 shorter events, 1.7 us)
Async XLA Ops:
  0.6 0.7 copy-start.3
  1.3 0.7 copy-start.5
  2.0 0.7 copy-start.7
  2.7 0.7 copy-start.8
  4.3 93.4 %copy-start.1 = (bf16[1,4096,192]{1,2,0:T(8,128)(2,1)S(1)}, bf16[1,4096,192]{1,2,0:T(8,128)(2,1)}, u32[]{:S(2)}) copy-start(bf16[1,4096,192]{1,2,0:T(8,128)(2,1)} %param.12) | copy-start | bytes 4718596
  45.8 51.9 %copy-start = (bf16[1,4096,192]{1,2,0:T(8,128)(2,1)S(1)}, bf16[1,4096,192]{1,2,0:T(8,128)(2,1)}, u32[]{:S(2)}) copy-start(bf16[1,4096,192]{1,2,0:T(8,128)(2,1)} %param.11) | copy-start | bytes 4718596
  47.4 12.3 %collective-permute-start = (bf16[96,512]{1,0:T(8,128)(2,1)S(1)}, bf16[96,512]{1,0:T(8,128)(2,1)S(1)}, u32[]{:S(2)}, u32[]{:S(2)}) collective-permute-start(bf16[96,512]{1,0:T(8,128)(2,1)S(1)} %get-tuple-element.28), channel_id=1, source_target_pairs={{0,96},{1,673},{2,98},{3,675},{4,100},{5,677},{6,102},{7,679},{8,1... | collective-permute-start | bytes 294920 | tf_op jit(solution)/shard_map/ppermute | solution.py:113
  52.5 7.2 %collective-permute-start.1 = (bf16[96,512]{1,0:T(8,128)(2,1)S(1)}, bf16[96,512]{1,0:T(8,128)(2,1)S(1)}, u32[]{:S(2)}, u32[]{:S(2)}) collective-permute-start(bf16[96,512]{1,0:T(8,128)(2,1)S(1)} %get-tuple-element.29), channel_id=1, source_target_pairs={{0,96},{1,673},{2,98},{3,675},{4,100},{5,677},{6,102},{7,679},{8,1... | collective-permute-start | bytes 294920 | tf_op jit(solution)/shard_map/ppermute | solution.py:113
  54.5 5.4 %collective-permute-start.2 = (bf16[96,512]{1,0:T(8,128)(2,1)S(1)}, bf16[96,512]{1,0:T(8,128)(2,1)S(1)}, u32[]{:S(2)}, u32[]{:S(2)}) collective-permute-start(bf16[96,512]{1,0:T(8,128)(2,1)S(1)} %get-tuple-element.30), channel_id=1, source_target_pairs={{0,672},{1,97},{2,674},{3,99},{4,676},{5,101},{6,678},{7,103},{8,6... | collective-permute-start | bytes 294920 | tf_op jit(solution)/shard_map/ppermute | solution.py:113
  56.4 5.7 %collective-permute-start.3 = (bf16[96,512]{1,0:T(8,128)(2,1)S(1)}, bf16[96,512]{1,0:T(8,128)(2,1)S(1)}, u32[]{:S(2)}, u32[]{:S(2)}) collective-permute-start(bf16[96,512]{1,0:T(8,128)(2,1)S(1)} %get-tuple-element.31), channel_id=1, source_target_pairs={{0,672},{1,97},{2,674},{3,99},{4,676},{5,101},{6,678},{7,103},{8,6... | collective-permute-start | bytes 294920 | tf_op jit(solution)/shard_map/ppermute | solution.py:113
  62.1 11.9 %collective-permute-start.4 = (bf16[2,96,512]{2,1,0:T(8,128)(2,1)S(1)}, bf16[2,96,512]{2,1,0:T(8,128)(2,1)S(1)}, u32[]{:S(2)}, u32[]{:S(2)}) collective-permute-start(bf16[2,96,512]{2,1,0:T(8,128)(2,1)S(1)} %pad_maximum_fusion.refs_0_), channel_id=1, source_target_pairs={{0,672},{1,97},{2,674},{3,99},{4,676},{5,101},{6,678},{7,103},{8,6... | collective-permute-start | bytes 589832 | tf_op jit(solution)/shard_map/ppermute | solution.py:113
  65.2 13.4 %collective-permute-start.5 = (bf16[2,96,512]{2,1,0:T(8,128)(2,1)S(1)}, bf16[2,96,512]{2,1,0:T(8,128)(2,1)S(1)}, u32[]{:S(2)}, u32[]{:S(2)}) collective-permute-start(bf16[2,96,512]{2,1,0:T(8,128)(2,1)S(1)} %pad_maximum_fusion.1.refs_1_), channel_id=1, source_target_pairs={{0,672},{1,97},{2,674},{3,99},{4,676},{5,101},{6,678},{7,103},{8,6... | collective-permute-start | bytes 589832 | tf_op jit(solution)/shard_map/ppermute | solution.py:113
  67.4 13.1 %collective-permute-start.18 = (bf16[2,96,512]{2,1,0:T(8,128)(2,1)S(1)}, bf16[2,96,512]{2,1,0:T(8,128)(2,1)S(1)}, u32[]{:S(2)}, u32[]{:S(2)}) collective-permute-start(bf16[2,96,512]{2,1,0:T(8,128)(2,1)S(1)} %pad_maximum_fusion.2.refs_0_), channel_id=1, source_target_pairs={{0,96},{1,673},{2,98},{3,675},{4,100},{5,677},{6,102},{7,679},{8,1... | collective-permute-start | bytes 589832 | tf_op jit(solution)/shard_map/ppermute | solution.py:113
  72.0 10.4 %collective-permute-start.19 = (bf16[2,96,512]{2,1,0:T(8,128)(2,1)S(1)}, bf16[2,96,512]{2,1,0:T(8,128)(2,1)S(1)}, u32[]{:S(2)}, u32[]{:S(2)}) collective-permute-start(bf16[2,96,512]{2,1,0:T(8,128)(2,1)S(1)} %pad_maximum_fusion.3.refs_1_), channel_id=1, source_target_pairs={{0,96},{1,673},{2,98},{3,675},{4,100},{5,677},{6,102},{7,679},{8,1... | collective-permute-start | bytes 589832 | tf_op jit(solution)/shard_map/ppermute | solution.py:113
  74.0 11.8 %collective-permute-start.6 = (bf16[2,96,512]{2,1,0:T(8,128)(2,1)S(1)}, bf16[2,96,512]{2,1,0:T(8,128)(2,1)S(1)}, u32[]{:S(2)}, u32[]{:S(2)}) collective-permute-start(bf16[2,96,512]{2,1,0:T(8,128)(2,1)S(1)} %collective-permute-done.4.refs_2_), channel_id=1, source_target_pairs={{0,96},{1,673},{2,98},{3,675},{4,100},{5,677},{6,102},{7,679},{8,1... | collective-permute-start | bytes 589832 | tf_op jit(solution)/shard_map/ppermute | solution.py:113
  78.6 9.2 %collective-permute-start.7 = (bf16[2,96,512]{2,1,0:T(8,128)(2,1)S(1)}, bf16[2,96,512]{2,1,0:T(8,128)(2,1)S(1)}, u32[]{:S(2)}, u32[]{:S(2)}) collective-permute-start(bf16[2,96,512]{2,1,0:T(8,128)(2,1)S(1)} %collective-permute-done.5.refs_3_), channel_id=1, source_target_pairs={{0,96},{1,673},{2,98},{3,675},{4,100},{5,677},{6,102},{7,679},{8,1... | collective-permute-start | bytes 589832 | tf_op jit(solution)/shard_map/ppermute | solution.py:113
  80.5 10.6 %collective-permute-start.20 = (bf16[2,96,512]{2,1,0:T(8,128)(2,1)S(1)}, bf16[2,96,512]{2,1,0:T(8,128)(2,1)S(1)}, u32[]{:S(2)}, u32[]{:S(2)}) collective-permute-start(bf16[2,96,512]{2,1,0:T(8,128)(2,1)S(1)} %collective-permute-done.18.refs_2_), channel_id=1, source_target_pairs={{0,672},{1,97},{2,674},{3,99},{4,676},{5,101},{6,678},{7,103},{8,6... | collective-permute-start | bytes 589832 | tf_op jit(solution)/shard_map/ppermute | solution.py:113
  82.4 13.3 %collective-permute-start.21 = (bf16[2,96,512]{2,1,0:T(8,128)(2,1)S(1)}, bf16[2,96,512]{2,1,0:T(8,128)(2,1)S(1)}, u32[]{:S(2)}, u32[]{:S(2)}) collective-permute-start(bf16[2,96,512]{2,1,0:T(8,128)(2,1)S(1)} %collective-permute-done.19.refs_3_), channel_id=1, source_target_pairs={{0,672},{1,97},{2,674},{3,99},{4,676},{5,101},{6,678},{7,103},{8,6... | collective-permute-start | bytes 589832 | tf_op jit(solution)/shard_map/ppermute | solution.py:113
  85.8 11.8 %collective-permute-start.8 = (bf16[2,96,512]{2,1,0:T(8,128)(2,1)S(1)}, bf16[2,96,512]{2,1,0:T(8,128)(2,1)S(1)}, u32[]{:S(2)}, u32[]{:S(2)}) collective-permute-start(bf16[2,96,512]{2,1,0:T(8,128)(2,1)S(1)} %collective-permute-done.6.refs_4_), channel_id=1, source_target_pairs={{0,672},{1,97},{2,674},{3,99},{4,676},{5,101},{6,678},{7,103},{8,6... | collective-permute-start | bytes 589832 | tf_op jit(solution)/shard_map/ppermute | solution.py:113
  87.8 9.9 %collective-permute-start.9 = (bf16[2,96,512]{2,1,0:T(8,128)(2,1)S(1)}, bf16[2,96,512]{2,1,0:T(8,128)(2,1)S(1)}, u32[]{:S(2)}, u32[]{:S(2)}) collective-permute-start(bf16[2,96,512]{2,1,0:T(8,128)(2,1)S(1)} %collective-permute-done.7.refs_5_), channel_id=1, source_target_pairs={{0,672},{1,97},{2,674},{3,99},{4,676},{5,101},{6,678},{7,103},{8,6... | collective-permute-start | bytes 589832 | tf_op jit(solution)/shard_map/ppermute | solution.py:113
  91.1 14.8 %collective-permute-start.22 = (bf16[2,96,512]{2,1,0:T(8,128)(2,1)S(1)}, bf16[2,96,512]{2,1,0:T(8,128)(2,1)S(1)}, u32[]{:S(2)}, u32[]{:S(2)}) collective-permute-start(bf16[2,96,512]{2,1,0:T(8,128)(2,1)S(1)} %collective-permute-done.20.refs_4_), channel_id=1, source_target_pairs={{0,96},{1,673},{2,98},{3,675},{4,100},{5,677},{6,102},{7,679},{8,1... | collective-permute-start | bytes 589832 | tf_op jit(solution)/shard_map/ppermute | solution.py:113
  95.7 10.2 %collective-permute-start.23 = (bf16[2,96,512]{2,1,0:T(8,128)(2,1)S(1)}, bf16[2,96,512]{2,1,0:T(8,128)(2,1)S(1)}, u32[]{:S(2)}, u32[]{:S(2)}) collective-permute-start(bf16[2,96,512]{2,1,0:T(8,128)(2,1)S(1)} %collective-permute-done.21.refs_5_), channel_id=1, source_target_pairs={{0,96},{1,673},{2,98},{3,675},{4,100},{5,677},{6,102},{7,679},{8,1... | collective-permute-start | bytes 589832 | tf_op jit(solution)/shard_map/ppermute | solution.py:113
  97.7 1.4 copy-start.2
  100.6 14.2 %collective-permute-start.10 = (bf16[2,96,512]{2,1,0:T(8,128)(2,1)S(1)}, bf16[2,96,512]{2,1,0:T(8,128)(2,1)S(1)}, u32[]{:S(2)}, u32[]{:S(2)}) collective-permute-start(bf16[2,96,512]{2,1,0:T(8,128)(2,1)S(1)} %get-tuple-element.37), channel_id=1, source_target_pairs={{0,672},{1,97},{2,674},{3,99},{4,676},{5,101},{6,678},{7,103},{8,6... | collective-permute-start | bytes 589832 | tf_op jit(solution)/shard_map/ppermute | solution.py:113
  103.4 16.1 %collective-permute-start.14 = (bf16[2,96,512]{2,1,0:T(8,128)(2,1)S(1)}, bf16[2,96,512]{2,1,0:T(8,128)(2,1)S(1)}, u32[]{:S(2)}, u32[]{:S(2)}) collective-permute-start(bf16[2,96,512]{2,1,0:T(8,128)(2,1)S(1)} %get-tuple-element.41), channel_id=1, source_target_pairs={{0,672},{1,97},{2,674},{3,99},{4,676},{5,101},{6,678},{7,103},{8,6... | collective-permute-start | bytes 589832 | tf_op jit(solution)/shard_map/ppermute | solution.py:113
  108.3 13.1 %collective-permute-start.24 = (bf16[2,96,512]{2,1,0:T(8,128)(2,1)S(1)}, bf16[2,96,512]{2,1,0:T(8,128)(2,1)S(1)}, u32[]{:S(2)}, u32[]{:S(2)}) collective-permute-start(bf16[2,96,512]{2,1,0:T(8,128)(2,1)S(1)} %get-tuple-element.49), channel_id=1, source_target_pairs={{0,96},{1,673},{2,98},{3,675},{4,100},{5,677},{6,102},{7,679},{8,1... | collective-permute-start | bytes 589832 | tf_op jit(solution)/shard_map/ppermute | solution.py:113
  112.9 10.6 %collective-permute-start.28 = (bf16[2,96,512]{2,1,0:T(8,128)(2,1)S(1)}, bf16[2,96,512]{2,1,0:T(8,128)(2,1)S(1)}, u32[]{:S(2)}, u32[]{:S(2)}) collective-permute-start(bf16[2,96,512]{2,1,0:T(8,128)(2,1)S(1)} %get-tuple-element.53), channel_id=1, source_target_pairs={{0,96},{1,673},{2,98},{3,675},{4,100},{5,677},{6,102},{7,679},{8,1... | collective-permute-start | bytes 589832 | tf_op jit(solution)/shard_map/ppermute | solution.py:113
  114.9 12.0 %collective-permute-start.11 = (bf16[2,96,512]{2,1,0:T(8,128)(2,1)S(1)}, bf16[2,96,512]{2,1,0:T(8,128)(2,1)S(1)}, u32[]{:S(2)}, u32[]{:S(2)}) collective-permute-start(bf16[2,96,512]{2,1,0:T(8,128)(2,1)S(1)} %add_convert_fusion.11), channel_id=1, source_target_pairs={{0,96},{1,673},{2,98},{3,675},{4,100},{5,677},{6,102},{7,679},{8,1... | collective-permute-start | bytes 589832 | tf_op jit(solution)/shard_map/ppermute | solution.py:113
  119.5 9.3 %collective-permute-start.15 = (bf16[2,96,512]{2,1,0:T(8,128)(2,1)S(1)}, bf16[2,96,512]{2,1,0:T(8,128)(2,1)S(1)}, u32[]{:S(2)}, u32[]{:S(2)}) collective-permute-start(bf16[2,96,512]{2,1,0:T(8,128)(2,1)S(1)} %add_convert_fusion.8), channel_id=1, source_target_pairs={{0,96},{1,673},{2,98},{3,675},{4,100},{5,677},{6,102},{7,679},{8,1... | collective-permute-start | bytes 589832 | tf_op jit(solution)/shard_map/ppermute | solution.py:113
  121.5 10.8 %collective-permute-start.25 = (bf16[2,96,512]{2,1,0:T(8,128)(2,1)S(1)}, bf16[2,96,512]{2,1,0:T(8,128)(2,1)S(1)}, u32[]{:S(2)}, u32[]{:S(2)}) collective-permute-start(bf16[2,96,512]{2,1,0:T(8,128)(2,1)S(1)} %add_convert_fusion.5), channel_id=1, source_target_pairs={{0,672},{1,97},{2,674},{3,99},{4,676},{5,101},{6,678},{7,103},{8,6... | collective-permute-start | bytes 589832 | tf_op jit(solution)/shard_map/ppermute | solution.py:113
  123.5 13.4 %collective-permute-start.29 = (bf16[2,96,512]{2,1,0:T(8,128)(2,1)S(1)}, bf16[2,96,512]{2,1,0:T(8,128)(2,1)S(1)}, u32[]{:S(2)}, u32[]{:S(2)}) collective-permute-start(bf16[2,96,512]{2,1,0:T(8,128)(2,1)S(1)} %add_convert_fusion.2), channel_id=1, source_target_pairs={{0,672},{1,97},{2,674},{3,99},{4,676},{5,101},{6,678},{7,103},{8,6... | collective-permute-start | bytes 589832 | tf_op jit(solution)/shard_map/ppermute | solution.py:113
  126.9 12.3 %collective-permute-start.12 = (bf16[2,96,512]{2,1,0:T(8,128)(2,1)S(1)}, bf16[2,96,512]{2,1,0:T(8,128)(2,1)S(1)}, u32[]{:S(2)}, u32[]{:S(2)}) collective-permute-start(bf16[2,96,512]{2,1,0:T(8,128)(2,1)S(1)} %add_convert_fusion.10), channel_id=1, source_target_pairs={{0,672},{1,97},{2,674},{3,99},{4,676},{5,101},{6,678},{7,103},{8,6... | collective-permute-start | bytes 589832 | tf_op jit(solution)/shard_map/ppermute | solution.py:113
  128.9 14.7 %collective-permute-start.16 = (bf16[2,96,512]{2,1,0:T(8,128)(2,1)S(1)}, bf16[2,96,512]{2,1,0:T(8,128)(2,1)S(1)}, u32[]{:S(2)}, u32[]{:S(2)}) collective-permute-start(bf16[2,96,512]{2,1,0:T(8,128)(2,1)S(1)} %add_convert_fusion.7), channel_id=1, source_target_pairs={{0,672},{1,97},{2,674},{3,99},{4,676},{5,101},{6,678},{7,103},{8,6... | collective-permute-start | bytes 589832 | tf_op jit(solution)/shard_map/ppermute | solution.py:113
  132.3 13.5 %collective-permute-start.26 = (bf16[2,96,512]{2,1,0:T(8,128)(2,1)S(1)}, bf16[2,96,512]{2,1,0:T(8,128)(2,1)S(1)}, u32[]{:S(2)}, u32[]{:S(2)}) collective-permute-start(bf16[2,96,512]{2,1,0:T(8,128)(2,1)S(1)} %add_convert_fusion.4), channel_id=1, source_target_pairs={{0,96},{1,673},{2,98},{3,675},{4,100},{5,677},{6,102},{7,679},{8,1... | collective-permute-start | bytes 589832 | tf_op jit(solution)/shard_map/ppermute | solution.py:113
  137.0 10.9 %collective-permute-start.30 = (bf16[2,96,512]{2,1,0:T(8,128)(2,1)S(1)}, bf16[2,96,512]{2,1,0:T(8,128)(2,1)S(1)}, u32[]{:S(2)}, u32[]{:S(2)}) collective-permute-start(bf16[2,96,512]{2,1,0:T(8,128)(2,1)S(1)} %add_convert_fusion.1), channel_id=1, source_target_pairs={{0,96},{1,673},{2,98},{3,675},{4,100},{5,677},{6,102},{7,679},{8,1... | collective-permute-start | bytes 589832 | tf_op jit(solution)/shard_map/ppermute | solution.py:113
  139.3 12.1 %collective-permute-start.13 = (bf16[96,512]{1,0:T(8,128)(2,1)S(1)}, bf16[96,512]{1,0:T(8,128)(2,1)S(1)}, u32[]{:S(2)}, u32[]{:S(2)}) collective-permute-start(bf16[96,512]{1,0:T(8,128)(2,1)S(1)} %slice_bitcast_fusion.3), channel_id=1, source_target_pairs={{0,96},{1,673},{2,98},{3,675},{4,100},{5,677},{6,102},{7,679},{8,1... | collective-permute-start | bytes 294920 | tf_op jit(solution)/shard_map/ppermute | solution.py:113
  143.6 8.0 %collective-permute-start.17 = (bf16[96,512]{1,0:T(8,128)(2,1)S(1)}, bf16[96,512]{1,0:T(8,128)(2,1)S(1)}, u32[]{:S(2)}, u32[]{:S(2)}) collective-permute-start(bf16[96,512]{1,0:T(8,128)(2,1)S(1)} %slice_bitcast_fusion.2), channel_id=1, source_target_pairs={{0,96},{1,673},{2,98},{3,675},{4,100},{5,677},{6,102},{7,679},{8,1... | collective-permute-start | bytes 294920 | tf_op jit(solution)/shard_map/ppermute | solution.py:113
  146.0 6.6 %collective-permute-start.27 = (bf16[96,512]{1,0:T(8,128)(2,1)S(1)}, bf16[96,512]{1,0:T(8,128)(2,1)S(1)}, u32[]{:S(2)}, u32[]{:S(2)}) collective-permute-start(bf16[96,512]{1,0:T(8,128)(2,1)S(1)} %slice_bitcast_fusion.1), channel_id=1, source_target_pairs={{0,672},{1,97},{2,674},{3,99},{4,676},{5,101},{6,678},{7,103},{8,6... | collective-permute-start | bytes 294920 | tf_op jit(solution)/shard_map/ppermute | solution.py:113
  148.0 6.7 %collective-permute-start.31 = (bf16[96,512]{1,0:T(8,128)(2,1)S(1)}, bf16[96,512]{1,0:T(8,128)(2,1)S(1)}, u32[]{:S(2)}, u32[]{:S(2)}) collective-permute-start(bf16[96,512]{1,0:T(8,128)(2,1)S(1)} %slice_bitcast_fusion), channel_id=1, source_target_pairs={{0,672},{1,97},{2,674},{3,99},{4,676},{5,101},{6,678},{7,103},{8,6... | collective-permute-start | bytes 294920 | tf_op jit(solution)/shard_map/ppermute | solution.py:113
  155.1 41.2 %copy-start.4 = (s32[16,8]{0,1:T(8,128)S(1)}, s32[16,8]{0,1:T(8,128)}, u32[]{:S(2)}) copy-start(s32[16,8]{0,1:T(8,128)} %param.8) | copy-start | bytes 1540
  155.1 41.2 %copy-start.6 = (f32[16,8]{0,1:T(8,128)S(1)}, f32[16,8]{0,1:T(8,128)}, u32[]{:S(2)}) copy-start(f32[16,8]{0,1:T(8,128)} %param.9) | copy-start | bytes 1540

commit v6 on v3

--- a/solution.py
+++ b/solution.py
@@ -8,7 +8,9 @@
 bf16 = jnp.bfloat16
 f32 = jnp.float32
 VMEM = pl.BlockSpec(memory_space=pltpu.VMEM)
-VMEM_LIMIT = 28 * 1024 * 1024
+HBM = pl.BlockSpec(memory_space=pltpu.HBM)
+VMEM_LIMIT = 16 * 1024 * 1024
+BIG = 60 * 1024 * 1024
 
 
 def dot_last(left, right):
@@ -52,7 +54,14 @@
     return jnp.where(here, named, 0.0), jnp.where(here, scale, 0.0), gradient
 
 
-def dispatch_kernel(capacity, routes, weight, tokens, grads, send):
+def dispatch_kernel(capacity, *refs):
+    outside, send, inside, sems = refs[:4], refs[4], refs[5:9], refs[9]
+    copies = [pltpu.make_async_copy(outside[i], inside[i], sems.at[i]) for i in range(4)]
+    for copy in copies:
+        copy.start()
+    for copy in copies:
+        copy.wait()
+    routes, weight, tokens, grads = inside
     pick, weighted, gradient = picks(capacity, routes, weight, send.shape[0])
     out = dot(jnp.where(gradient, 0.0, pick).astype(bf16), tokens[...])
     for part in split3(jnp.where(gradient, weighted, 0.0)):
@@ -60,7 +69,8 @@
     send[...] = out.astype(bf16)
 
 
-def sort_kernel(capacity, recv, token_rows, grad_rows):
+def sort_kernel(capacity, recv, down_w, token_rows, grad_rows):
+    del down_w
     rows = recv.shape[0]
     for kind, out in ((0, token_rows), (1, grad_rows)):
         shape = (rows // 2, rows)
@@ -182,11 +192,16 @@
     capacity = min(tok_rows, max(2, (3 * tok_rows * top_count + 2 * owners - 1) // (2 * owners)))
     slots = owners * capacity
     rows = 2 * slots
+    inputs = (routes.T, route_weight.T, tokens, grad_out)
     send = pl.pallas_call(
         lambda *refs: dispatch_kernel(capacity, *refs),
         out_shape=jax.ShapeDtypeStruct((rows, local_width), bf16),
-        compiler_params=pltpu.CompilerParams(vmem_limit_bytes=VMEM_LIMIT),
-    )(routes.T, route_weight.T, tokens, grad_out)
+        in_specs=[HBM] * 4,
+        out_specs=VMEM,
+        scratch_shapes=[pltpu.VMEM(value.shape, value.dtype) for value in inputs]
+        + [pltpu.SemaphoreType.DMA((4,))],
+        compiler_params=pltpu.CompilerParams(vmem_limit_bytes=BIG),
+    )(*inputs)
     recv = lax.all_to_all(
         send.reshape(owners, 2 * capacity, local_width), "ep", split_axis=0, concat_axis=0, tiled=True
     ).reshape(rows, local_width)
@@ -194,10 +209,10 @@
     token_rows, grad_rows = pl.pallas_call(
         lambda *refs: sort_kernel(capacity, *refs),
         out_shape=[half, half],
-        in_specs=[VMEM],
+        in_specs=[VMEM, VMEM],
         out_specs=[VMEM] * 2,
         compiler_params=pltpu.CompilerParams(vmem_limit_bytes=VMEM_LIMIT),
-    )(recv)
+    )(recv, w_down[0])
     token_next, grad_next = lax.optimization_barrier(
         (exchange(token_rows, 0, 0), exchange(grad_rows, 0, 1))
     )

time: 189 us -> 186 us (0.984)
  local copies, waits for them, and re-layouts: 5.76 us -> 1.44 us
  blocking collectives: 84.2 us -> 79.9 us
  waiting for transfers between devices: 43.2 us -> 46.7 us
    unnamed x18 -> x10, local copies, waits for them, and re-layouts: 4.23 us -> 0.03 us
    all_to_all x1, blocking collectives: 42.6 us -> 38.6 us  [on_device(): lax.all_to_all(unsorted.reshape(owners, 2 * capacity, local_width), 'ep',...]
    ppermute x16, waiting for transfers between devices: 43.2 us -> 46.7 us  [exchange(): return lax.ppermute(value, ('etp', 'ep'), pairs)]
  transfers between devices with their start and end apart: 16 -> 16, of which waited for: 15 -> 16; matrix products, arithmetic and copies ran while one was open for 0% -> 0% of each run, Pallas kernels for 2% -> 2%
where the time goes in v6:
time: 186 us; the launch traced here: 185 us
  blocking collectives  79.9 us (43%)
  starting transfers between devices  47 us (25%)
  waiting for transfers between devices  46.7 us (25%)
  Pallas kernels  8.34 us (4%)
    ppermute x16, starting transfers between devices, exchange(): return lax.ppermute(value, ('etp', 'ep'), pairs)  47 us
    ppermute x16, waiting for transfers between devices, exchange(): return lax.ppermute(value, ('etp', 'ep'), pairs)  46.7 us
    all_to_all x1, blocking collectives, on_device(): lax.all_to_all(send.reshape(owners, 2 * capacity, local_width), 'ep', spl...  41.3 us
    all_to_all x1, blocking collectives, on_device(): lax.all_to_all(unsorted.reshape(owners, 2 * capacity, local_width), 'ep',...  38.6 us
    pallas_call x2, Pallas kernels, call(): pl.pallas_call(lambda *refs: kernel(steps, *refs), out_shape=shapes, in_s...  3.82 us
  transfers between devices with their start and end apart: 16, of which 16 were waited for; matrix products, arithmetic and copies ran while one was open for 0% of the time, Pallas kernels for 2%

profile of v6, /device:TPU:1, one launch (start us, length us, event | category | flops | bytes accessed | tf_op | source)
XLA Modules:
  0.0 185.1 jit_solution(8510206595360858564)
XLA Ops:
  0.6 2.5 %shard_map.86 = bf16[384,512]{1,0:T(8,128)(2,1)} custom-call(s32[8,16]{1,0:T(8,128)} %bitcast.26, f32[8,16]{1,0:T(8,128)} %bitcast.28, bf16[16,512]{1,0:T(8,128)(2,1)} %refs_2_.1, bf16[16,512]{1,0:T(8,128)(2,1)} %refs_3_.1), custom_call_target="tpu_custom_call" | custom-call | tf_op jit(solution)/shard_map/pallas_call | solution.py:196
  3.2 1.1 reshape.16
  4.3 41.3 %all_to_all.10 = bf16[96,4,512]{2,1,0:T(4,128)(2,1)S(1)} all-to-all(bf16[96,4,512]{2,1,0:T(4,128)(2,1)S(1)} %reshape.16), channel_id=1, replica_groups=mesh['etp'=8,'ep'=96] {'ep'}, dimensions={0} | all-to-all | bytes 786432 | tf_op jit(solution)/shard_map/all_to_all | solution.py:205
  45.7 0.4 shard_map.87
  46.1 5.2 %collective-permute-start = (bf16[192,512]{1,0:T(8,128)(2,1)S(1)}, bf16[192,512]{1,0:T(8,128)(2,1)S(1)}, u32[]{:S(2)}, u32[]{:S(2)}) collective-permute-start(bf16[192,512]{1,0:T(8,128)(2,1)S(1)} %get-tuple-element.16), channel_id=1, source_target_pairs={{0,96},{1,673},{2,98},{3,675},{4,100},{5,677},{6,102},{7,679},{8,1... | collective-permute-start | bytes 589832 | tf_op jit(solution)/shard_map/ppermute | solution.py:113
  51.3 1.9 %collective-permute-start.1 = (bf16[192,512]{1,0:T(8,128)(2,1)S(1)}, bf16[192,512]{1,0:T(8,128)(2,1)S(1)}, u32[]{:S(2)}, u32[]{:S(2)}) collective-permute-start(bf16[192,512]{1,0:T(8,128)(2,1)S(1)} %get-tuple-element.17), channel_id=1, source_target_pairs={{0,672},{1,97},{2,674},{3,99},{4,676},{5,101},{6,678},{7,103},{8,6... | collective-permute-start | bytes 589832 | tf_op jit(solution)/shard_map/ppermute | solution.py:113
  53.2 1.1 collective-permute-done
  54.4 3.7 %collective-permute-done.1 = bf16[192,512]{1,0:T(8,128)(2,1)S(1)} collective-permute-done((bf16[192,512]{1,0:T(8,128)(2,1)S(1)}, bf16[192,512]{1,0:T(8,128)(2,1)S(1)}, u32[]{:S(2)}, u32[]{:S(2)}) %collective-permute-start.1) | collective-permute-done | bytes 196640 | tf_op jit(solution)/shard_map/ppermute | solution.py:113
  58.1 2.2 %collective-permute-start.2 = (bf16[2,192,512]{2,1,0:T(8,128)(2,1)S(1)}, bf16[2,192,512]{2,1,0:T(8,128)(2,1)S(1)}, u32[]{:S(2)}, u32[]{:S(2)}) collective-permute-start(bf16[2,192,512]{2,1,0:T(8,128)(2,1)S(1)} %pad_maximum_fusion.refs_0_), channel_id=1, source_target_pairs={{0,672},{1,97},{2,674},{3,99},{4,676},{5,101},{6,678},{7,103},{8,6... | collective-permute-start | bytes 1179656 | tf_op jit(solution)/shard_map/ppermute | solution.py:113
  60.3 4.9 %collective-permute-start.9 = (bf16[2,192,512]{2,1,0:T(8,128)(2,1)S(1)}, bf16[2,192,512]{2,1,0:T(8,128)(2,1)S(1)}, u32[]{:S(2)}, u32[]{:S(2)}) collective-permute-start(bf16[2,192,512]{2,1,0:T(8,128)(2,1)S(1)} %pad_maximum_fusion.1.refs_0_), channel_id=1, source_target_pairs={{0,96},{1,673},{2,98},{3,675},{4,100},{5,677},{6,102},{7,679},{8,1... | collective-permute-start | bytes 1179656 | tf_op jit(solution)/shard_map/ppermute | solution.py:113
  65.2 1.7 collective-permute-done.2.refs_1_
  66.9 3.5 %collective-permute-start.3 = (bf16[2,192,512]{2,1,0:T(8,128)(2,1)S(1)}, bf16[2,192,512]{2,1,0:T(8,128)(2,1)S(1)}, u32[]{:S(2)}, u32[]{:S(2)}) collective-permute-start(bf16[2,192,512]{2,1,0:T(8,128)(2,1)S(1)} %collective-permute-done.2.refs_1_), channel_id=1, source_target_pairs={{0,96},{1,673},{2,98},{3,675},{4,100},{5,677},{6,102},{7,679},{8,1... | collective-permute-start | bytes 1179656 | tf_op jit(solution)/shard_map/ppermute | solution.py:113
  70.4 4.3 %collective-permute-done.9.refs_1_ = bf16[2,192,512]{2,1,0:T(8,128)(2,1)S(1)} collective-permute-done((bf16[2,192,512]{2,1,0:T(8,128)(2,1)S(1)}, bf16[2,192,512]{2,1,0:T(8,128)(2,1)S(1)}, u32[]{:S(2)}, u32[]{:S(2)}) %collective-permute-start.9) | collective-permute-done | bytes 393248 | tf_op jit(solution)/shard_map/ppermute | solution.py:113
  74.7 1.9 %collective-permute-start.10 = (bf16[2,192,512]{2,1,0:T(8,128)(2,1)S(1)}, bf16[2,192,512]{2,1,0:T(8,128)(2,1)S(1)}, u32[]{:S(2)}, u32[]{:S(2)}) collective-permute-start(bf16[2,192,512]{2,1,0:T(8,128)(2,1)S(1)} %collective-permute-done.9.refs_1_), channel_id=1, source_target_pairs={{0,672},{1,97},{2,674},{3,99},{4,676},{5,101},{6,678},{7,103},{8,6... | collective-permute-start | bytes 1179656 | tf_op jit(solution)/shard_map/ppermute | solution.py:113
  76.6 2.1 %collective-permute-done.3.refs_2_ = bf16[2,192,512]{2,1,0:T(8,128)(2,1)S(1)} collective-permute-done((bf16[2,192,512]{2,1,0:T(8,128)(2,1)S(1)}, bf16[2,192,512]{2,1,0:T(8,128)(2,1)S(1)}, u32[]{:S(2)}, u32[]{:S(2)}) %collective-permute-start.3) | collective-permute-done | bytes 393248 | tf_op jit(solution)/shard_map/ppermute | solution.py:113
  78.7 1.9 %collective-permute-start.4 = (bf16[2,192,512]{2,1,0:T(8,128)(2,1)S(1)}, bf16[2,192,512]{2,1,0:T(8,128)(2,1)S(1)}, u32[]{:S(2)}, u32[]{:S(2)}) collective-permute-start(bf16[2,192,512]{2,1,0:T(8,128)(2,1)S(1)} %collective-permute-done.3.refs_2_), channel_id=1, source_target_pairs={{0,672},{1,97},{2,674},{3,99},{4,676},{5,101},{6,678},{7,103},{8,6... | collective-permute-start | bytes 1179656 | tf_op jit(solution)/shard_map/ppermute | solution.py:113
  80.6 6.3 %collective-permute-done.10.refs_2_ = bf16[2,192,512]{2,1,0:T(8,128)(2,1)S(1)} collective-permute-done((bf16[2,192,512]{2,1,0:T(8,128)(2,1)S(1)}, bf16[2,192,512]{2,1,0:T(8,128)(2,1)S(1)}, u32[]{:S(2)}, u32[]{:S(2)}) %collective-permute-start.10) | collective-permute-done | bytes 393248 | tf_op jit(solution)/shard_map/ppermute | solution.py:113
  86.8 4.1 %collective-permute-start.11 = (bf16[2,192,512]{2,1,0:T(8,128)(2,1)S(1)}, bf16[2,192,512]{2,1,0:T(8,128)(2,1)S(1)}, u32[]{:S(2)}, u32[]{:S(2)}) collective-permute-start(bf16[2,192,512]{2,1,0:T(8,128)(2,1)S(1)} %collective-permute-done.10.refs_2_), channel_id=1, source_target_pairs={{0,96},{1,673},{2,98},{3,675},{4,100},{5,677},{6,102},{7,679},{8,1... | collective-permute-start | bytes 1179656 | tf_op jit(solution)/shard_map/ppermute | solution.py:113
  91.0 0.6 collective-permute-done.4.refs_3_
  91.6 1.5 shard_map.88
  93.1 1.9 %collective-permute-start.5 = (bf16[2,192,512]{2,1,0:T(8,128)(2,1)S(1)}, bf16[2,192,512]{2,1,0:T(8,128)(2,1)S(1)}, u32[]{:S(2)}, u32[]{:S(2)}) collective-permute-start(bf16[2,192,512]{2,1,0:T(8,128)(2,1)S(1)} %get-tuple-element.22), channel_id=1, source_target_pairs={{0,672},{1,97},{2,674},{3,99},{4,676},{5,101},{6,678},{7,103},{8,6... | collective-permute-start | bytes 1179656 | tf_op jit(solution)/shard_map/ppermute | solution.py:113
  95.0 3.3 %collective-permute-done.11.refs_3_ = bf16[2,192,512]{2,1,0:T(8,128)(2,1)S(1)} collective-permute-done((bf16[2,192,512]{2,1,0:T(8,128)(2,1)S(1)}, bf16[2,192,512]{2,1,0:T(8,128)(2,1)S(1)}, u32[]{:S(2)}, u32[]{:S(2)}) %collective-permute-start.11) | collective-permute-done | bytes 393248 | tf_op jit(solution)/shard_map/ppermute | solution.py:113
  98.3 2.3 %shard_map.89 = (f32[2,192,512]{2,1,0:T(8,128)S(1)}, f32[2,192,512]{2,1,0:T(8,128)S(1)}, f32[2,192,512]{2,1,0:T(8,128)S(1)}, bf16[2,192,512]{2,1,0:T(8,128)(2,1)S(1)}) custom-call(bf16[2,192,512]{2,1,0:T(8,128)(2,1)S(1)} %pad_maximum_fusion.1.refs_0_, bf16[2,192,512]{2,1,0:T(8,128)(2,1)S(1)} %collective-permute-done.9.refs_1_, ...), custom_call_target="tpu_custom_call" | custom-call | flops 905969664 | bytes 9437184 | tf_op jit(solution)/shard_map/pallas_call | solution.py:173
  100.7 3.4 %collective-permute-start.12 = (bf16[2,192,512]{2,1,0:T(8,128)(2,1)S(1)}, bf16[2,192,512]{2,1,0:T(8,128)(2,1)S(1)}, u32[]{:S(2)}, u32[]{:S(2)}) collective-permute-start(bf16[2,192,512]{2,1,0:T(8,128)(2,1)S(1)} %get-tuple-element.29), channel_id=1, source_target_pairs={{0,96},{1,673},{2,98},{3,675},{4,100},{5,677},{6,102},{7,679},{8,1... | collective-permute-start | bytes 1179656 | tf_op jit(solution)/shard_map/ppermute | solution.py:113
  104.1 0.4 collective-permute-done.5
  104.5 0.1 add_convert_fusion.5
  104.6 4.5 %collective-permute-start.6 = (bf16[2,192,512]{2,1,0:T(8,128)(2,1)S(1)}, bf16[2,192,512]{2,1,0:T(8,128)(2,1)S(1)}, u32[]{:S(2)}, u32[]{:S(2)}) collective-permute-start(bf16[2,192,512]{2,1,0:T(8,128)(2,1)S(1)} %add_convert_fusion.5), channel_id=1, source_target_pairs={{0,96},{1,673},{2,98},{3,675},{4,100},{5,677},{6,102},{7,679},{8,1... | collective-permute-start | bytes 1179656 | tf_op jit(solution)/shard_map/ppermute | solution.py:113
  109.1 2.9 %collective-permute-done.12 = bf16[2,192,512]{2,1,0:T(8,128)(2,1)S(1)} collective-permute-done((bf16[2,192,512]{2,1,0:T(8,128)(2,1)S(1)}, bf16[2,192,512]{2,1,0:T(8,128)(2,1)S(1)}, u32[]{:S(2)}, u32[]{:S(2)}) %collective-permute-start.12) | collective-permute-done | bytes 393248 | tf_op jit(solution)/shard_map/ppermute | solution.py:113
  112.1 0.1 add_convert_fusion.2
  112.2 1.9 %collective-permute-start.13 = (bf16[2,192,512]{2,1,0:T(8,128)(2,1)S(1)}, bf16[2,192,512]{2,1,0:T(8,128)(2,1)S(1)}, u32[]{:S(2)}, u32[]{:S(2)}) collective-permute-start(bf16[2,192,512]{2,1,0:T(8,128)(2,1)S(1)} %add_convert_fusion.2), channel_id=1, source_target_pairs={{0,672},{1,97},{2,674},{3,99},{4,676},{5,101},{6,678},{7,103},{8,6... | collective-permute-start | bytes 1179656 | tf_op jit(solution)/shard_map/ppermute | solution.py:113
  114.1 4.7 %collective-permute-done.6 = bf16[2,192,512]{2,1,0:T(8,128)(2,1)S(1)} collective-permute-done((bf16[2,192,512]{2,1,0:T(8,128)(2,1)S(1)}, bf16[2,192,512]{2,1,0:T(8,128)(2,1)S(1)}, u32[]{:S(2)}, u32[]{:S(2)}) %collective-permute-start.6) | collective-permute-done | bytes 393248 | tf_op jit(solution)/shard_map/ppermute | solution.py:113
  118.8 0.1 add_convert_fusion.4
  118.9 1.9 %collective-permute-start.7 = (bf16[2,192,512]{2,1,0:T(8,128)(2,1)S(1)}, bf16[2,192,512]{2,1,0:T(8,128)(2,1)S(1)}, u32[]{:S(2)}, u32[]{:S(2)}) collective-permute-start(bf16[2,192,512]{2,1,0:T(8,128)(2,1)S(1)} %add_convert_fusion.4), channel_id=1, source_target_pairs={{0,672},{1,97},{2,674},{3,99},{4,676},{5,101},{6,678},{7,103},{8,6... | collective-permute-start | bytes 1179656 | tf_op jit(solution)/shard_map/ppermute | solution.py:113
  120.9 2.1 %collective-permute-done.13 = bf16[2,192,512]{2,1,0:T(8,128)(2,1)S(1)} collective-permute-done((bf16[2,192,512]{2,1,0:T(8,128)(2,1)S(1)}, bf16[2,192,512]{2,1,0:T(8,128)(2,1)S(1)}, u32[]{:S(2)}, u32[]{:S(2)}) %collective-permute-start.13) | collective-permute-done | bytes 393248 | tf_op jit(solution)/shard_map/ppermute | solution.py:113
  122.9 0.1 add_convert_fusion.1
  123.1 2.4 %collective-permute-start.14 = (bf16[2,192,512]{2,1,0:T(8,128)(2,1)S(1)}, bf16[2,192,512]{2,1,0:T(8,128)(2,1)S(1)}, u32[]{:S(2)}, u32[]{:S(2)}) collective-permute-start(bf16[2,192,512]{2,1,0:T(8,128)(2,1)S(1)} %add_convert_fusion.1), channel_id=1, source_target_pairs={{0,96},{1,673},{2,98},{3,675},{4,100},{5,677},{6,102},{7,679},{8,1... | collective-permute-start | bytes 1179656 | tf_op jit(solution)/shard_map/ppermute | solution.py:113
  125.4 6.3 %collective-permute-done.7 = bf16[2,192,512]{2,1,0:T(8,128)(2,1)S(1)} collective-permute-done((bf16[2,192,512]{2,1,0:T(8,128)(2,1)S(1)}, bf16[2,192,512]{2,1,0:T(8,128)(2,1)S(1)}, u32[]{:S(2)}, u32[]{:S(2)}) %collective-permute-start.7) | collective-permute-done | bytes 393248 | tf_op jit(solution)/shard_map/ppermute | solution.py:113
  131.7 0.1 add_convert_fusion.3.refs_0_
  131.9 3.4 %collective-permute-start.8 = (bf16[192,512]{1,0:T(8,128)(2,1)S(1)}, bf16[192,512]{1,0:T(8,128)(2,1)S(1)}, u32[]{:S(2)}, u32[]{:S(2)}) collective-permute-start(bf16[192,512]{1,0:T(8,128)(2,1)S(1)} %slice_bitcast_fusion.1), channel_id=1, source_target_pairs={{0,96},{1,673},{2,98},{3,675},{4,100},{5,677},{6,102},{7,679},{8,1... | collective-permute-start | bytes 589832 | tf_op jit(solution)/shard_map/ppermute | solution.py:113
  135.3 0.8 collective-permute-done.14
  136.1 0.1 add_convert_fusion.refs_2_
  136.3 1.9 %collective-permute-start.15 = (bf16[192,512]{1,0:T(8,128)(2,1)S(1)}, bf16[192,512]{1,0:T(8,128)(2,1)S(1)}, u32[]{:S(2)}, u32[]{:S(2)}) collective-permute-start(bf16[192,512]{1,0:T(8,128)(2,1)S(1)} %slice_bitcast_fusion), channel_id=1, source_target_pairs={{0,672},{1,97},{2,674},{3,99},{4,676},{5,101},{6,678},{7,103},{8,6... | collective-permute-start | bytes 589832 | tf_op jit(solution)/shard_map/ppermute | solution.py:113
  138.2 3.2 %collective-permute-done.8.refs_1_ = bf16[192,512]{1,0:T(8,128)(2,1)S(1)} collective-permute-done((bf16[192,512]{1,0:T(8,128)(2,1)S(1)}, bf16[192,512]{1,0:T(8,128)(2,1)S(1)}, u32[]{:S(2)}, u32[]{:S(2)}) %collective-permute-start.8) | collective-permute-done | bytes 196640 | tf_op jit(solution)/shard_map/ppermute | solution.py:113
  141.4 3.3 %collective-permute-done.15.refs_3_ = bf16[192,512]{1,0:T(8,128)(2,1)S(1)} collective-permute-done((bf16[192,512]{1,0:T(8,128)(2,1)S(1)}, bf16[192,512]{1,0:T(8,128)(2,1)S(1)}, u32[]{:S(2)}, u32[]{:S(2)}) %collective-permute-start.15) | collective-permute-done | bytes 196640 | tf_op jit(solution)/shard_map/ppermute | solution.py:113
  144.6 0.4 shard_map.90
  145.0 0.1 reshape.18
  145.1 38.6 %all_to_all.11 = bf16[96,4,512]{2,1,0:T(4,128)(2,1)S(1)} all-to-all(bf16[96,4,512]{2,1,0:T(4,128)(2,1)S(1)} %reshape.18), channel_id=1, replica_groups=mesh['etp'=8,'ep'=96] {'ep'}, dimensions={0} | all-to-all | bytes 786432 | tf_op jit(solution)/shard_map/all_to_all | solution.py:247
  183.8 1.2 shard_map.91
  (16 shorter events, 0.3 us)
Async XLA Ops:
  0.6 45.0 %copy-start = (bf16[1,192,4096]{2,1,0:T(8,128)(2,1)S(1)}, bf16[1,192,4096]{2,1,0:T(8,128)(2,1)}, u32[]{:S(2)}) copy-start(bf16[1,192,4096]{2,1,0:T(8,128)(2,1)} %param.13) | copy-start | bytes 4718596
  45.7 45.9 %copy-start.1 = (bf16[1,4096,192]{1,2,0:T(8,128)(2,1)S(1)}, bf16[1,4096,192]{1,2,0:T(8,128)(2,1)}, u32[]{:S(2)}) copy-start(bf16[1,4096,192]{1,2,0:T(8,128)(2,1)} %param.11) | copy-start | bytes 4718596
  45.7 45.9 %copy-start.2 = (bf16[1,4096,192]{1,2,0:T(8,128)(2,1)S(1)}, bf16[1,4096,192]{1,2,0:T(8,128)(2,1)}, u32[]{:S(2)}) copy-start(bf16[1,4096,192]{1,2,0:T(8,128)(2,1)} %param.12) | copy-start | bytes 4718596
  46.1 8.3 %collective-permute-start = (bf16[192,512]{1,0:T(8,128)(2,1)S(1)}, bf16[192,512]{1,0:T(8,128)(2,1)S(1)}, u32[]{:S(2)}, u32[]{:S(2)}) collective-permute-start(bf16[192,512]{1,0:T(8,128)(2,1)S(1)} %get-tuple-element.16), channel_id=1, source_target_pairs={{0,96},{1,673},{2,98},{3,675},{4,100},{5,677},{6,102},{7,679},{8,1... | collective-permute-start | bytes 589832 | tf_op jit(solution)/shard_map/ppermute | solution.py:113
  51.3 6.7 %collective-permute-start.1 = (bf16[192,512]{1,0:T(8,128)(2,1)S(1)}, bf16[192,512]{1,0:T(8,128)(2,1)S(1)}, u32[]{:S(2)}, u32[]{:S(2)}) collective-permute-start(bf16[192,512]{1,0:T(8,128)(2,1)S(1)} %get-tuple-element.17), channel_id=1, source_target_pairs={{0,672},{1,97},{2,674},{3,99},{4,676},{5,101},{6,678},{7,103},{8,6... | collective-permute-start | bytes 589832 | tf_op jit(solution)/shard_map/ppermute | solution.py:113
  58.1 8.8 %collective-permute-start.2 = (bf16[2,192,512]{2,1,0:T(8,128)(2,1)S(1)}, bf16[2,192,512]{2,1,0:T(8,128)(2,1)S(1)}, u32[]{:S(2)}, u32[]{:S(2)}) collective-permute-start(bf16[2,192,512]{2,1,0:T(8,128)(2,1)S(1)} %pad_maximum_fusion.refs_0_), channel_id=1, source_target_pairs={{0,672},{1,97},{2,674},{3,99},{4,676},{5,101},{6,678},{7,103},{8,6... | collective-permute-start | bytes 1179656 | tf_op jit(solution)/shard_map/ppermute | solution.py:113
  60.3 14.4 %collective-permute-start.9 = (bf16[2,192,512]{2,1,0:T(8,128)(2,1)S(1)}, bf16[2,192,512]{2,1,0:T(8,128)(2,1)S(1)}, u32[]{:S(2)}, u32[]{:S(2)}) collective-permute-start(bf16[2,192,512]{2,1,0:T(8,128)(2,1)S(1)} %pad_maximum_fusion.1.refs_0_), channel_id=1, source_target_pairs={{0,96},{1,673},{2,98},{3,675},{4,100},{5,677},{6,102},{7,679},{8,1... | collective-permute-start | bytes 1179656 | tf_op jit(solution)/shard_map/ppermute | solution.py:113
  66.9 11.8 %collective-permute-start.3 = (bf16[2,192,512]{2,1,0:T(8,128)(2,1)S(1)}, bf16[2,192,512]{2,1,0:T(8,128)(2,1)S(1)}, u32[]{:S(2)}, u32[]{:S(2)}) collective-permute-start(bf16[2,192,512]{2,1,0:T(8,128)(2,1)S(1)} %collective-permute-done.2.refs_1_), channel_id=1, source_target_pairs={{0,96},{1,673},{2,98},{3,675},{4,100},{5,677},{6,102},{7,679},{8,1... | collective-permute-start | bytes 1179656 | tf_op jit(solution)/shard_map/ppermute | solution.py:113
  74.7 12.2 %collective-permute-start.10 = (bf16[2,192,512]{2,1,0:T(8,128)(2,1)S(1)}, bf16[2,192,512]{2,1,0:T(8,128)(2,1)S(1)}, u32[]{:S(2)}, u32[]{:S(2)}) collective-permute-start(bf16[2,192,512]{2,1,0:T(8,128)(2,1)S(1)} %collective-permute-done.9.refs_1_), channel_id=1, source_target_pairs={{0,672},{1,97},{2,674},{3,99},{4,676},{5,101},{6,678},{7,103},{8,6... | collective-permute-start | bytes 1179656 | tf_op jit(solution)/shard_map/ppermute | solution.py:113
  78.7 12.9 %collective-permute-start.4 = (bf16[2,192,512]{2,1,0:T(8,128)(2,1)S(1)}, bf16[2,192,512]{2,1,0:T(8,128)(2,1)S(1)}, u32[]{:S(2)}, u32[]{:S(2)}) collective-permute-start(bf16[2,192,512]{2,1,0:T(8,128)(2,1)S(1)} %collective-permute-done.3.refs_2_), channel_id=1, source_target_pairs={{0,672},{1,97},{2,674},{3,99},{4,676},{5,101},{6,678},{7,103},{8,6... | collective-permute-start | bytes 1179656 | tf_op jit(solution)/shard_map/ppermute | solution.py:113
  86.8 11.5 %collective-permute-start.11 = (bf16[2,192,512]{2,1,0:T(8,128)(2,1)S(1)}, bf16[2,192,512]{2,1,0:T(8,128)(2,1)S(1)}, u32[]{:S(2)}, u32[]{:S(2)}) collective-permute-start(bf16[2,192,512]{2,1,0:T(8,128)(2,1)S(1)} %collective-permute-done.10.refs_2_), channel_id=1, source_target_pairs={{0,96},{1,673},{2,98},{3,675},{4,100},{5,677},{6,102},{7,679},{8,1... | collective-permute-start | bytes 1179656 | tf_op jit(solution)/shard_map/ppermute | solution.py:113
  93.1 11.4 %collective-permute-start.5 = (bf16[2,192,512]{2,1,0:T(8,128)(2,1)S(1)}, bf16[2,192,512]{2,1,0:T(8,128)(2,1)S(1)}, u32[]{:S(2)}, u32[]{:S(2)}) collective-permute-start(bf16[2,192,512]{2,1,0:T(8,128)(2,1)S(1)} %get-tuple-element.22), channel_id=1, source_target_pairs={{0,672},{1,97},{2,674},{3,99},{4,676},{5,101},{6,678},{7,103},{8,6... | collective-permute-start | bytes 1179656 | tf_op jit(solution)/shard_map/ppermute | solution.py:113
  100.7 11.4 %collective-permute-start.12 = (bf16[2,192,512]{2,1,0:T(8,128)(2,1)S(1)}, bf16[2,192,512]{2,1,0:T(8,128)(2,1)S(1)}, u32[]{:S(2)}, u32[]{:S(2)}) collective-permute-start(bf16[2,192,512]{2,1,0:T(8,128)(2,1)S(1)} %get-tuple-element.29), channel_id=1, source_target_pairs={{0,96},{1,673},{2,98},{3,675},{4,100},{5,677},{6,102},{7,679},{8,1... | collective-permute-start | bytes 1179656 | tf_op jit(solution)/shard_map/ppermute | solution.py:113
  104.6 14.2 %collective-permute-start.6 = (bf16[2,192,512]{2,1,0:T(8,128)(2,1)S(1)}, bf16[2,192,512]{2,1,0:T(8,128)(2,1)S(1)}, u32[]{:S(2)}, u32[]{:S(2)}) collective-permute-start(bf16[2,192,512]{2,1,0:T(8,128)(2,1)S(1)} %add_convert_fusion.5), channel_id=1, source_target_pairs={{0,96},{1,673},{2,98},{3,675},{4,100},{5,677},{6,102},{7,679},{8,1... | collective-permute-start | bytes 1179656 | tf_op jit(solution)/shard_map/ppermute | solution.py:113
  112.2 10.8 %collective-permute-start.13 = (bf16[2,192,512]{2,1,0:T(8,128)(2,1)S(1)}, bf16[2,192,512]{2,1,0:T(8,128)(2,1)S(1)}, u32[]{:S(2)}, u32[]{:S(2)}) collective-permute-start(bf16[2,192,512]{2,1,0:T(8,128)(2,1)S(1)} %add_convert_fusion.2), channel_id=1, source_target_pairs={{0,672},{1,97},{2,674},{3,99},{4,676},{5,101},{6,678},{7,103},{8,6... | collective-permute-start | bytes 1179656 | tf_op jit(solution)/shard_map/ppermute | solution.py:113
  118.9 12.8 %collective-permute-start.7 = (bf16[2,192,512]{2,1,0:T(8,128)(2,1)S(1)}, bf16[2,192,512]{2,1,0:T(8,128)(2,1)S(1)}, u32[]{:S(2)}, u32[]{:S(2)}) collective-permute-start(bf16[2,192,512]{2,1,0:T(8,128)(2,1)S(1)} %add_convert_fusion.4), channel_id=1, source_target_pairs={{0,672},{1,97},{2,674},{3,99},{4,676},{5,101},{6,678},{7,103},{8,6... | collective-permute-start | bytes 1179656 | tf_op jit(solution)/shard_map/ppermute | solution.py:113
  123.1 13.0 %collective-permute-start.14 = (bf16[2,192,512]{2,1,0:T(8,128)(2,1)S(1)}, bf16[2,192,512]{2,1,0:T(8,128)(2,1)S(1)}, u32[]{:S(2)}, u32[]{:S(2)}) collective-permute-start(bf16[2,192,512]{2,1,0:T(8,128)(2,1)S(1)} %add_convert_fusion.1), channel_id=1, source_target_pairs={{0,96},{1,673},{2,98},{3,675},{4,100},{5,677},{6,102},{7,679},{8,1... | collective-permute-start | bytes 1179656 | tf_op jit(solution)/shard_map/ppermute | solution.py:113
  131.9 9.5 %collective-permute-start.8 = (bf16[192,512]{1,0:T(8,128)(2,1)S(1)}, bf16[192,512]{1,0:T(8,128)(2,1)S(1)}, u32[]{:S(2)}, u32[]{:S(2)}) collective-permute-start(bf16[192,512]{1,0:T(8,128)(2,1)S(1)} %slice_bitcast_fusion.1), channel_id=1, source_target_pairs={{0,96},{1,673},{2,98},{3,675},{4,100},{5,677},{6,102},{7,679},{8,1... | collective-permute-start | bytes 589832 | tf_op jit(solution)/shard_map/ppermute | solution.py:113
  136.3 8.3 %collective-permute-start.15 = (bf16[192,512]{1,0:T(8,128)(2,1)S(1)}, bf16[192,512]{1,0:T(8,128)(2,1)S(1)}, u32[]{:S(2)}, u32[]{:S(2)}) collective-permute-start(bf16[192,512]{1,0:T(8,128)(2,1)S(1)} %slice_bitcast_fusion), channel_id=1, source_target_pairs={{0,672},{1,97},{2,674},{3,99},{4,676},{5,101},{6,678},{7,103},{8,6... | collective-permute-start | bytes 589832 | tf_op jit(solution)/shard_map/ppermute | solution.py:113
  145.0 38.8 %copy-start.3 = (s32[16,8]{0,1:T(8,128)S(1)}, s32[16,8]{0,1:T(8,128)}, u32[]{:S(2)}) copy-start(s32[16,8]{0,1:T(8,128)} %param.8) | copy-start | bytes 1540
  145.0 38.8 %copy-start.4 = (f32[16,8]{0,1:T(8,128)S(1)}, f32[16,8]{0,1:T(8,128)}, u32[]{:S(2)}) copy-start(f32[16,8]{0,1:T(8,128)} %param.9) | copy-start | bytes 1540

commit v7 on v6

v7 whole, which is shorter than its diff:
```python
import jax
import jax.numpy as jnp
from jax import lax
from jax.experimental import pallas as pl
from jax.experimental.pallas import tpu as pltpu
from jax.sharding import PartitionSpec as P

bf16 = jnp.bfloat16
f32 = jnp.float32
VMEM = pl.BlockSpec(memory_space=pltpu.VMEM)
HBM = pl.BlockSpec(memory_space=pltpu.HBM)
VMEM_LIMIT = 16 * 1024 * 1024
BIG = 60 * 1024 * 1024


def dot_last(left, right):
    return lax.dot_general(left, right, (((1,), (1,)), ((), ())), preferred_element_type=f32)


def dot(left, right):
    return lax.dot_general(left, right, (((1,), (0,)), ((), ())), preferred_element_type=f32)


def split3(value):
    high = value.astype(bf16)
    rest = value - high.astype(f32)
    middle = rest.astype(bf16)
    return high, middle, (rest - middle.astype(f32)).astype(bf16)


def dot_first(left, right):
    return lax.dot_general(left, right, (((0,), (0,)), ((), ())), preferred_element_type=f32)


def travel_row(slot, kind, capacity):
    return lax.div(slot, capacity) * (2 * capacity) + kind * capacity + lax.rem(slot, capacity)


def picks(capacity, routes, weight, rows):
    shape = (rows, routes.shape[1])
    row = lax.broadcasted_iota(jnp.int32, shape, 0)
    owner = lax.div(row, 2 * capacity)
    named = jnp.zeros(shape, f32)
    scale = jnp.zeros(shape, f32)
    for k in range(routes.shape[0]):
        hit = routes[k : k + 1, :] == owner
        named = jnp.where(hit, 1.0, named)
        scale = jnp.where(hit, weight[k : k + 1, :], scale)
    square = (shape[1], shape[1])
    before = lax.broadcasted_iota(jnp.int32, square, 0) < lax.broadcasted_iota(jnp.int32, square, 1)
    earlier = dot(named.astype(bf16), before.astype(f32).astype(bf16))
    here = earlier == lax.rem(row, capacity).astype(f32)
    gradient = lax.rem(row, 2 * capacity) >= capacity
    return jnp.where(here, named, 0.0), jnp.where(here, scale, 0.0), gradient


def dispatch_kernel(capacity, *refs):
    outside, send, inside, sems = refs[:4], refs[4], refs[5:9], refs[9]
    copies = [pltpu.make_async_copy(outside[i], inside[i], sems.at[i]) for i in range(4)]
    for copy in copies:
        copy.start()
    for copy in copies:
        copy.wait()
    routes, weight, tokens, grads = inside
    pick, weighted, gradient = picks(capacity, routes, weight, send.shape[0])
    out = dot(jnp.where(gradient, 0.0, pick).astype(bf16), tokens[...])
    for part in split3(jnp.where(gradient, weighted, 0.0)):
        out = out + dot(part, grads[...])
    send[...] = out.astype(bf16)


def sort_kernel(capacity, recv, down_w, out):
    del down_w
    rows = recv.shape[0]
    for kind in (0, 1):
        shape = (rows // 2, rows)
        source = travel_row(lax.broadcasted_iota(jnp.int32, shape, 0), kind, capacity)
        place = (source == lax.broadcasted_iota(jnp.int32, shape, 1)).astype(f32).astype(bf16)
        out[kind * (rows // 2) : (kind + 1) * (rows // 2)] = dot(place, recv[...]).astype(bf16)


def unsort_kernel(capacity, held, last, unsorted):
    rows = unsorted.shape[0]
    half = rows // 2
    total = None
    for kind in (0, 1):
        part = slice(kind * half, (kind + 1) * half)
        local = (held[0, part].astype(f32) + last[part].astype(f32)).astype(bf16)
        target = travel_row(lax.broadcasted_iota(jnp.int32, (rows, half), 1), kind, capacity)
        place = (target == lax.broadcasted_iota(jnp.int32, (rows, half), 0)).astype(f32).astype(bf16)
        now = dot(place, local)
        total = now if total is None else total + now
    unsorted[...] = total.astype(bf16)


def combine_kernel(capacity, routes, weight, back, mixed, grad_tokens):
    pick, weighted, gradient = picks(capacity, routes, weight, back.shape[0])
    rows = back[...]
    out = None
    for part in split3(jnp.where(gradient, 0.0, weighted)):
        now = dot_first(part, rows)
        out = now if out is None else out + now
    mixed[...] = out.astype(bf16)
    grad_tokens[...] = dot_first(jnp.where(gradient, pick, 0.0).astype(bf16), rows).astype(bf16)


def exchange(value, step):
    size, owners = lax.axis_size("etp"), lax.axis_size("ep")
    pairs = []
    for y in range(size):
        for j in range(owners):
            sign = 1 if (y + j + step) % 2 == 0 else -1
            pairs.append((y * owners + j, (y + sign) % size * owners + j))
    return lax.ppermute(value, ("etp", "ep"), pairs)


def columns_of(steps, width):
    size = 2 * steps
    y = lax.axis_index("etp")
    sign = 1 - 2 * lax.rem(y + lax.axis_index("ep"), 2)
    out = []
    for k in range(steps):
        turn = sign if k % 2 == 0 else -sign
        blocks = [lax.rem(y + turn * (k + b) + 2 * size, size) for b in (0, 1)]
        out.append([pl.ds(pl.multiple_of(block * width, width), width) for block in blocks])
    return out


def add_pair(held, columns, weights, totals):
    slots = held.shape[1] // 2
    gate_w, up_w, down_w = weights
    for b in (0, 1):
        token_rows, grad_rows = held[b, :slots], held[b, slots:]
        now = (
            dot_last(token_rows, gate_w[:, columns[b]]),
            dot_last(token_rows, up_w[:, columns[b]]),
            dot_last(grad_rows, down_w[:, columns[b]]),
        )
        totals = now if totals is None else tuple(x + y for x, y in zip(totals, now))
    return totals


def store_pair(part, columns, weights, hidden, gate_grad, up_grad):
    slots = part.shape[1] // 2
    gate_w, up_w, down_w = weights
    for b in (0, 1):
        part[b, :slots] = dot(hidden, down_w[:, columns[b]]).astype(part.dtype)
        now = dot(gate_grad, gate_w[:, columns[b]]) + dot(up_grad, up_w[:, columns[b]])
        part[b, slots:] = now.astype(part.dtype)


def first_kernel(steps, *refs):
    held, weights, totals = refs[: steps - 1], refs[steps - 1 : steps + 2], refs[steps + 2 :]
    columns = columns_of(steps, held[0].shape[2])
    sums = None
    for k in range(steps - 1):
        sums = add_pair(held[k], columns[k], weights, sums)
    for total, value in zip(totals, sums):
        total[...] = value


def middle_kernel(steps, *refs):
    held, weights, totals = refs[0], refs[1:4], refs[4:7]
    hidden_ref, gate_grad_ref, up_grad_ref, part = refs[7:]
    columns = columns_of(steps, held.shape[2])[-1]
    gate, up, hidden_grad = add_pair(held, columns, weights, tuple(x[...] for x in totals))
    squash = jax.nn.sigmoid(gate)
    active = gate * squash
    hidden = (active * up).astype(bf16)
    up_grad = (hidden_grad * active).astype(bf16)
    gate_grad = (hidden_grad * up * squash * (1.0 + gate * (1.0 - squash))).astype(bf16)
    hidden_ref[...] = hidden
    gate_grad_ref[...] = gate_grad
    up_grad_ref[...] = up_grad
    store_pair(part, columns, weights, hidden, gate_grad, up_grad)


def last_kernel(steps, *refs):
    weights, (hidden, gate_grad, up_grad), parts = refs[:3], refs[3:6], refs[6:]
    columns = columns_of(steps, parts[0].shape[2])
    for k in reversed(range(steps - 1)):
        store_pair(parts[k], columns[k], weights, hidden[...], gate_grad[...], up_grad[...])


def call(kernel, steps, operands, shapes, flops):
    return pl.pallas_call(
        lambda *refs: kernel(steps, *refs),
        out_shape=shapes,
        in_specs=[VMEM] * len(operands),
        out_specs=[VMEM] * len(shapes),
        compiler_params=pltpu.CompilerParams(vmem_limit_bytes=VMEM_LIMIT),
        cost_estimate=pl.CostEstimate(flops=flops, bytes_accessed=6 << 20, transcendentals=0),
    )(*operands)


def sum_step(part, arrived, step):
    return (part + exchange(arrived, step).astype(f32)).astype(bf16)


def on_device(tokens, routes, route_weight, grad_out, w_gate, w_up, w_down):
    owners, steps = lax.axis_size("ep"), lax.axis_size("etp") // 2
    tok_rows, local_width = tokens.shape
    top_count = routes.shape[1]
    capacity = min(tok_rows, max(2, (3 * tok_rows * top_count + 2 * owners - 1) // (2 * owners)))
    slots = owners * capacity
    rows = 2 * slots
    inputs = (routes.T, route_weight.T, tokens, grad_out)
    send = pl.pallas_call(
        lambda *refs: dispatch_kernel(capacity, *refs),
        out_shape=jax.ShapeDtypeStruct((rows, local_width), bf16),
        in_specs=[HBM] * 4,
        out_specs=VMEM,
        scratch_shapes=[pltpu.VMEM(value.shape, value.dtype) for value in inputs]
        + [pltpu.SemaphoreType.DMA((4,))],
        compiler_params=pltpu.CompilerParams(vmem_limit_bytes=BIG),
    )(*inputs)
    recv = lax.all_to_all(
        send.reshape(owners, 2 * capacity, local_width), "ep", split_axis=0, concat_axis=0, tiled=True
    ).reshape(rows, local_width)
    own = pl.pallas_call(
        lambda *refs: sort_kernel(capacity, *refs),
        out_shape=jax.ShapeDtypeStruct((rows, local_width), bf16),
        in_specs=[VMEM] * 2,
        out_specs=VMEM,
        compiler_params=pltpu.CompilerParams(vmem_limit_bytes=VMEM_LIMIT),
    )(recv, w_down[0])
    held = [jnp.stack([own, exchange(own, 0)])]
    for step in range(1, steps):
        held.append(exchange(held[-1], step))
    weights = [w_gate[0].T, w_up[0].T, w_down[0]]
    hidden_width, width = weights[2].shape
    square = jax.ShapeDtypeStruct((slots, hidden_width), f32)
    factor = jax.ShapeDtypeStruct((slots, hidden_width), bf16)
    pair = (2, rows, local_width)
    flops = 6 * slots * hidden_width * width // steps
    totals = call(first_kernel, steps, held[:-1] + weights, [square] * 3, flops * (steps - 1))
    *factors, total = call(
        middle_kernel,
        steps,
        [held[-1]] + weights + list(totals),
        [factor] * 3 + [jax.ShapeDtypeStruct(pair, bf16)],
        flops * 2,
    )
    parts = call(
        last_kernel,
        steps,
        weights + factors,
        [jax.ShapeDtypeStruct(pair, f32)] * (steps - 1),
        flops * (steps - 1),
    )
    for step in reversed(range(1, steps)):
        total = sum_step(parts[step - 1], total, step)
    unsorted = pl.pallas_call(
        lambda *refs: unsort_kernel(capacity, *refs),
        out_shape=jax.ShapeDtypeStruct((rows, local_width), bf16),
        in_specs=[VMEM] * 2,
        out_specs=VMEM,
        compiler_params=pltpu.CompilerParams(vmem_limit_bytes=VMEM_LIMIT),
    )(total, exchange(total[1], 0))
    back = lax.all_to_all(
        unsorted.reshape(owners, 2 * capacity, local_width), "ep", split_axis=0, concat_axis=0, tiled=True
    ).reshape(rows, local_width)
    mine = jax.ShapeDtypeStruct((tok_rows, local_width), bf16)
    mixed, grad_tokens = pl.pallas_call(
        lambda *refs: combine_kernel(capacity, *refs),
        out_shape=[mine, mine],
        in_specs=[VMEM] * 3,
        out_specs=[VMEM] * 2,
        compiler_params=pltpu.CompilerParams(vmem_limit_bytes=VMEM_LIMIT),
    )(routes.T, route_weight.T, back)
    return (mixed, grad_tokens)


def solution(mesh):
    in_specs = (
        P("ep", "etp"),
        P("ep", None),
        P("ep", None),
        P("ep", "etp"),
        P("ep", None, "etp"),
        P("ep", None, "etp"),
        P("ep", "etp", None),
    )
    out_specs = (P("ep", "etp"), P("ep", "etp"))
    return jax.shard_map(
        on_device, mesh=mesh, in_specs=in_specs, out_specs=out_specs, check_vma=False
    )
```

time: 186 us -> 196 us (1.054)
  waiting for transfers between devices: 46.7 us -> 76.5 us
  starting transfers between devices: 47 us -> 27.2 us
    ppermute x16 -> x8, waiting for transfers between devices: 46.7 us -> 76.5 us  [exchange(): return lax.ppermute(value, ('etp', 'ep'), pairs)]
    ppermute x16 -> x8, starting transfers between devices: 47 us -> 27.2 us  [exchange(): return lax.ppermute(value, ('etp', 'ep'), pairs)]
  transfers between devices with their start and end apart: 16 -> 8, of which waited for: 16 -> 8; matrix products, arithmetic and copies ran while one was open for 0% -> 0% of each run, Pallas kernels for 2% -> 1%
where the time goes in v7:
time: 196 us
  blocking collectives  81 us (41%)
  waiting for transfers between devices  76.5 us (39%)
  starting transfers between devices  27.2 us (14%)
  Pallas kernels  7.78 us (4%)
    ppermute x8, waiting for transfers between devices, exchange(): return lax.ppermute(value, ('etp', 'ep'), pairs)  76.5 us
    all_to_all x1, blocking collectives, on_device(): lax.all_to_all(send.reshape(owners, 2 * capacity, local_width), 'ep', spl...  41.3 us
    all_to_all x1, blocking collectives, on_device(): lax.all_to_all(unsorted.reshape(owners, 2 * capacity, local_width), 'ep',...  39.7 us
    ppermute x8, starting transfers between devices, exchange(): return lax.ppermute(value, ('etp', 'ep'), pairs)  27.2 us
  transfers between devices with their start and end apart: 8, of which 8 were waited for; matrix products, arithmetic and copies ran while one was open for 0% of the time, Pallas kernels for 1%

profile of v7, /device:TPU:1, one launch (start us, length us, event | category | flops | bytes accessed | tf_op | source)
XLA Modules:
  0.0 195.7 jit_solution(7112933237638348209)
XLA Ops:
  0.6 0.0 copy-start
  0.6 2.5 %shard_map.86 = bf16[384,512]{1,0:T(8,128)(2,1)} custom-call(s32[8,16]{1,0:T(8,128)} %bitcast.24, f32[8,16]{1,0:T(8,128)} %bitcast.26, bf16[16,512]{1,0:T(8,128)(2,1)} %refs_2_.1, bf16[16,512]{1,0:T(8,128)(2,1)} %refs_3_.1), custom_call_target="tpu_custom_call" | custom-call | tf_op jit(solution)/shard_map/pallas_call | solution.py:208
  3.2 1.1 reshape.16
  4.3 41.3 %all_to_all.10 = bf16[96,4,512]{2,1,0:T(4,128)(2,1)S(1)} all-to-all(bf16[96,4,512]{2,1,0:T(4,128)(2,1)S(1)} %reshape.16), channel_id=1, replica_groups=mesh['etp'=8,'ep'=96] {'ep'}, dimensions={0} | all-to-all | bytes 786432 | tf_op jit(solution)/shard_map/all_to_all | solution.py:217
  45.6 0.1 reshape.17.refs_0_
  45.7 0.0 copy-done
  45.7 0.0 copy-start.1
  45.7 0.0 copy-start.2
  45.7 0.4 shard_map.87
  46.1 5.2 %collective-permute-start = (bf16[384,512]{1,0:T(8,128)(2,1)S(1)}, bf16[384,512]{1,0:T(8,128)(2,1)S(1)}, u32[]{:S(2)}, u32[]{:S(2)}) collective-permute-start(bf16[384,512]{1,0:T(8,128)(2,1)S(1)} %shard_map.87), channel_id=1, source_target_pairs={{0,96},{1,673},{2,98},{3,675},{4,100},{5,677},{6,102},{7,679},{8,1... | collective-permute-start | bytes 1179656 | tf_op jit(solution)/shard_map/ppermute | solution.py:114
  51.3 5.2 %collective-permute-done = bf16[384,512]{1,0:T(8,128)(2,1)S(1)} collective-permute-done((bf16[384,512]{1,0:T(8,128)(2,1)S(1)}, bf16[384,512]{1,0:T(8,128)(2,1)S(1)}, u32[]{:S(2)}, u32[]{:S(2)}) %collective-permute-start) | collective-permute-done | bytes 393248 | tf_op jit(solution)/shard_map/ppermute | solution.py:114
  56.5 0.1 pad_maximum_fusion.refs_0_
  56.5 1.9 collective-permute-start.1
  58.5 11.1 %collective-permute-done.1.refs_1_ = bf16[2,384,512]{2,1,0:T(8,128)(2,1)S(1)} collective-permute-done((bf16[2,384,512]{2,1,0:T(8,128)(2,1)S(1)}, bf16[2,384,512]{2,1,0:T(8,128)(2,1)S(1)}, u32[]{:S(2)}, u32[]{:S(2)}) %collective-permute-start.1) | collective-permute-done | bytes 786464 | tf_op jit(solution)/shard_map/ppermute | solution.py:114
  69.6 4.6 %collective-permute-start.2 = (bf16[2,384,512]{2,1,0:T(8,128)(2,1)S(1)}, bf16[2,384,512]{2,1,0:T(8,128)(2,1)S(1)}, u32[]{:S(2)}, u32[]{:S(2)}) collective-permute-start(bf16[2,384,512]{2,1,0:T(8,128)(2,1)S(1)} %collective-permute-done.1.refs_1_), channel_id=1, source_target_pairs={{0,96},{1,673},{2,98},{3,675},{4,100},{5,677},{6,102},{7,679},{8,1... | collective-permute-start | bytes 2359304 | tf_op jit(solution)/shard_map/ppermute | solution.py:114
  74.1 9.4 %collective-permute-done.2.refs_2_ = bf16[2,384,512]{2,1,0:T(8,128)(2,1)S(1)} collective-permute-done((bf16[2,384,512]{2,1,0:T(8,128)(2,1)S(1)}, bf16[2,384,512]{2,1,0:T(8,128)(2,1)S(1)}, u32[]{:S(2)}, u32[]{:S(2)}) %collective-permute-start.2) | collective-permute-done | bytes 786464 | tf_op jit(solution)/shard_map/ppermute | solution.py:114
  83.5 1.9 collective-permute-start.3
  85.4 0.0 copy-done.1
  85.4 0.0 copy-done.2
  85.4 1.1 shard_map.88
  86.6 10.0 %collective-permute-done.3.refs_0_ = bf16[2,384,512]{2,1,0:T(8,128)(2,1)S(1)} collective-permute-done((bf16[2,384,512]{2,1,0:T(8,128)(2,1)S(1)}, bf16[2,384,512]{2,1,0:T(8,128)(2,1)S(1)}, u32[]{:S(2)}, u32[]{:S(2)}) %collective-permute-start.3) | collective-permute-done | bytes 786464 | tf_op jit(solution)/shard_map/ppermute | solution.py:114
  96.5 1.0 shard_map.89
  97.5 1.9 collective-permute-start.4
  99.5 1.1 shard_map.90
  100.6 10.0 %collective-permute-done.4 = bf16[2,384,512]{2,1,0:T(8,128)(2,1)S(1)} collective-permute-done((bf16[2,384,512]{2,1,0:T(8,128)(2,1)S(1)}, bf16[2,384,512]{2,1,0:T(8,128)(2,1)S(1)}, u32[]{:S(2)}, u32[]{:S(2)}) %collective-permute-start.4) | collective-permute-done | bytes 786464 | tf_op jit(solution)/shard_map/ppermute | solution.py:114
  110.6 0.3 add_convert_fusion.2
  110.8 4.6 %collective-permute-start.5 = (bf16[2,384,512]{2,1,0:T(8,128)(2,1)S(1)}, bf16[2,384,512]{2,1,0:T(8,128)(2,1)S(1)}, u32[]{:S(2)}, u32[]{:S(2)}) collective-permute-start(bf16[2,384,512]{2,1,0:T(8,128)(2,1)S(1)} %add_convert_fusion.2), channel_id=1, source_target_pairs={{0,96},{1,673},{2,98},{3,675},{4,100},{5,677},{6,102},{7,679},{8,1... | collective-permute-start | bytes 2359304 | tf_op jit(solution)/shard_map/ppermute | solution.py:114
  115.4 10.2 %collective-permute-done.5 = bf16[2,384,512]{2,1,0:T(8,128)(2,1)S(1)} collective-permute-done((bf16[2,384,512]{2,1,0:T(8,128)(2,1)S(1)}, bf16[2,384,512]{2,1,0:T(8,128)(2,1)S(1)}, u32[]{:S(2)}, u32[]{:S(2)}) %collective-permute-start.5) | collective-permute-done | bytes 786464 | tf_op jit(solution)/shard_map/ppermute | solution.py:114
  125.6 0.3 add_convert_fusion.1
  125.9 1.9 collective-permute-start.6
  127.9 12.7 %collective-permute-done.6 = bf16[2,384,512]{2,1,0:T(8,128)(2,1)S(1)} collective-permute-done((bf16[2,384,512]{2,1,0:T(8,128)(2,1)S(1)}, bf16[2,384,512]{2,1,0:T(8,128)(2,1)S(1)}, u32[]{:S(2)}, u32[]{:S(2)}) %collective-permute-start.6) | collective-permute-done | bytes 786464 | tf_op jit(solution)/shard_map/ppermute | solution.py:114
  140.5 0.3 add_convert_fusion.refs_0_
  140.9 5.1 %collective-permute-start.7 = (bf16[384,512]{1,0:T(8,128)(2,1)S(1)}, bf16[384,512]{1,0:T(8,128)(2,1)S(1)}, u32[]{:S(2)}, u32[]{:S(2)}) collective-permute-start(bf16[384,512]{1,0:T(8,128)(2,1)S(1)} %slice_bitcast_fusion), channel_id=1, source_target_pairs={{0,96},{1,673},{2,98},{3,675},{4,100},{5,677},{6,102},{7,679},{8,1... | collective-permute-start | bytes 1179656 | tf_op jit(solution)/shard_map/ppermute | solution.py:114
  146.0 8.1 %collective-permute-done.7.refs_1_ = bf16[384,512]{1,0:T(8,128)(2,1)S(1)} collective-permute-done((bf16[384,512]{1,0:T(8,128)(2,1)S(1)}, bf16[384,512]{1,0:T(8,128)(2,1)S(1)}, u32[]{:S(2)}, u32[]{:S(2)}) %collective-permute-start.7) | collective-permute-done | bytes 393248 | tf_op jit(solution)/shard_map/ppermute | solution.py:114
  154.1 0.4 shard_map.91
  154.5 0.0 copy-start.3
  154.5 0.0 copy-start.4
  154.5 0.1 reshape.18
  154.6 39.7 %all_to_all.11 = bf16[96,4,512]{2,1,0:T(4,128)(2,1)S(1)} all-to-all(bf16[96,4,512]{2,1,0:T(4,128)(2,1)S(1)} %reshape.18), channel_id=1, replica_groups=mesh['etp'=8,'ep'=96] {'ep'}, dimensions={0} | all-to-all | bytes 786432 | tf_op jit(solution)/shard_map/all_to_all | solution.py:260
  194.4 0.1 reshape.19.refs_2_
  194.5 0.0 copy-done.3
  194.5 0.0 copy-done.4
  194.5 1.2 shard_map.92
  (1 shorter events, 0.0 us)
Async XLA Ops:
  0.6 45.0 %copy-start = (bf16[1,192,4096]{2,1,0:T(8,128)(2,1)S(1)}, bf16[1,192,4096]{2,1,0:T(8,128)(2,1)}, u32[]{:S(2)}) copy-start(bf16[1,192,4096]{2,1,0:T(8,128)(2,1)} %param.13) | copy-start | bytes 4718596
  45.7 39.8 %copy-start.1 = (bf16[1,4096,192]{1,2,0:T(8,128)(2,1)S(1)}, bf16[1,4096,192]{1,2,0:T(8,128)(2,1)}, u32[]{:S(2)}) copy-start(bf16[1,4096,192]{1,2,0:T(8,128)(2,1)} %param.11) | copy-start | bytes 4718596
  45.7 39.7 %copy-start.2 = (bf16[1,4096,192]{1,2,0:T(8,128)(2,1)S(1)}, bf16[1,4096,192]{1,2,0:T(8,128)(2,1)}, u32[]{:S(2)}) copy-start(bf16[1,4096,192]{1,2,0:T(8,128)(2,1)} %param.12) | copy-start | bytes 4718596
  46.1 10.4 %collective-permute-start = (bf16[384,512]{1,0:T(8,128)(2,1)S(1)}, bf16[384,512]{1,0:T(8,128)(2,1)S(1)}, u32[]{:S(2)}, u32[]{:S(2)}) collective-permute-start(bf16[384,512]{1,0:T(8,128)(2,1)S(1)} %shard_map.87), channel_id=1, source_target_pairs={{0,96},{1,673},{2,98},{3,675},{4,100},{5,677},{6,102},{7,679},{8,1... | collective-permute-start | bytes 1179656 | tf_op jit(solution)/shard_map/ppermute | solution.py:114
  56.5 13.0 %collective-permute-start.1 = (bf16[2,384,512]{2,1,0:T(8,128)(2,1)S(1)}, bf16[2,384,512]{2,1,0:T(8,128)(2,1)S(1)}, u32[]{:S(2)}, u32[]{:S(2)}) collective-permute-start(bf16[2,384,512]{2,1,0:T(8,128)(2,1)S(1)} %pad_maximum_fusion.refs_0_), channel_id=1, source_target_pairs={{0,672},{1,97},{2,674},{3,99},{4,676},{5,101},{6,678},{7,103},{8,6... | collective-permute-start | bytes 2359304 | tf_op jit(solution)/shard_map/ppermute | solution.py:114
  69.6 13.9 %collective-permute-start.2 = (bf16[2,384,512]{2,1,0:T(8,128)(2,1)S(1)}, bf16[2,384,512]{2,1,0:T(8,128)(2,1)S(1)}, u32[]{:S(2)}, u32[]{:S(2)}) collective-permute-start(bf16[2,384,512]{2,1,0:T(8,128)(2,1)S(1)} %collective-permute-done.1.refs_1_), channel_id=1, source_target_pairs={{0,96},{1,673},{2,98},{3,675},{4,100},{5,677},{6,102},{7,679},{8,1... | collective-permute-start | bytes 2359304 | tf_op jit(solution)/shard_map/ppermute | solution.py:114
  83.5 13.0 %collective-permute-start.3 = (bf16[2,384,512]{2,1,0:T(8,128)(2,1)S(1)}, bf16[2,384,512]{2,1,0:T(8,128)(2,1)S(1)}, u32[]{:S(2)}, u32[]{:S(2)}) collective-permute-start(bf16[2,384,512]{2,1,0:T(8,128)(2,1)S(1)} %collective-permute-done.2.refs_2_), channel_id=1, source_target_pairs={{0,672},{1,97},{2,674},{3,99},{4,676},{5,101},{6,678},{7,103},{8,6... | collective-permute-start | bytes 2359304 | tf_op jit(solution)/shard_map/ppermute | solution.py:114
  97.5 13.0 %collective-permute-start.4 = (bf16[2,384,512]{2,1,0:T(8,128)(2,1)S(1)}, bf16[2,384,512]{2,1,0:T(8,128)(2,1)S(1)}, u32[]{:S(2)}, u32[]{:S(2)}) collective-permute-start(bf16[2,384,512]{2,1,0:T(8,128)(2,1)S(1)} %get-tuple-element.21), channel_id=1, source_target_pairs={{0,672},{1,97},{2,674},{3,99},{4,676},{5,101},{6,678},{7,103},{8,6... | collective-permute-start | bytes 2359304 | tf_op jit(solution)/shard_map/ppermute | solution.py:114
  110.8 14.8 %collective-permute-start.5 = (bf16[2,384,512]{2,1,0:T(8,128)(2,1)S(1)}, bf16[2,384,512]{2,1,0:T(8,128)(2,1)S(1)}, u32[]{:S(2)}, u32[]{:S(2)}) collective-permute-start(bf16[2,384,512]{2,1,0:T(8,128)(2,1)S(1)} %add_convert_fusion.2), channel_id=1, source_target_pairs={{0,96},{1,673},{2,98},{3,675},{4,100},{5,677},{6,102},{7,679},{8,1... | collective-permute-start | bytes 2359304 | tf_op jit(solution)/shard_map/ppermute | solution.py:114
  125.9 14.6 %collective-permute-start.6 = (bf16[2,384,512]{2,1,0:T(8,128)(2,1)S(1)}, bf16[2,384,512]{2,1,0:T(8,128)(2,1)S(1)}, u32[]{:S(2)}, u32[]{:S(2)}) collective-permute-start(bf16[2,384,512]{2,1,0:T(8,128)(2,1)S(1)} %add_convert_fusion.1), channel_id=1, source_target_pairs={{0,672},{1,97},{2,674},{3,99},{4,676},{5,101},{6,678},{7,103},{8,6... | collective-permute-start | bytes 2359304 | tf_op jit(solution)/shard_map/ppermute | solution.py:114
  140.9 13.2 %collective-permute-start.7 = (bf16[384,512]{1,0:T(8,128)(2,1)S(1)}, bf16[384,512]{1,0:T(8,128)(2,1)S(1)}, u32[]{:S(2)}, u32[]{:S(2)}) collective-permute-start(bf16[384,512]{1,0:T(8,128)(2,1)S(1)} %slice_bitcast_fusion), channel_id=1, source_target_pairs={{0,96},{1,673},{2,98},{3,675},{4,100},{5,677},{6,102},{7,679},{8,1... | collective-permute-start | bytes 1179656 | tf_op jit(solution)/shard_map/ppermute | solution.py:114
  154.5 40.0 %copy-start.3 = (s32[16,8]{0,1:T(8,128)S(1)}, s32[16,8]{0,1:T(8,128)}, u32[]{:S(2)}) copy-start(s32[16,8]{0,1:T(8,128)} %param.8) | copy-start | bytes 1540
  154.5 40.0 %copy-start.4 = (f32[16,8]{0,1:T(8,128)S(1)}, f32[16,8]{0,1:T(8,128)}, u32[]{:S(2)}) copy-start(f32[16,8]{0,1:T(8,128)} %param.9) | copy-start | bytes 1540

commit v8 on v6

--- a/solution.py
+++ b/solution.py
@@ -1,3 +1,5 @@
+import functools
+
 import jax
 import jax.numpy as jnp
 from jax import lax
@@ -125,58 +127,71 @@
     return out
 
 
-def forward_kernel(steps, *refs):
-    held, (gate_w, up_w, down_w) = refs[:steps], refs[steps : steps + 3]
-    gate_ref, up_ref = refs[steps + 3 : steps + 5]
-    parts = refs[steps + 5 :]
-    columns = columns_of(steps, held[0].shape[2], 0)
-    gate = up = None
-    for k in range(steps):
-        for b in (0, 1):
-            rows = held[k][b]
-            gate_now = dot_last(rows, gate_w[:, columns[k][b]])
-            up_now = dot_last(rows, up_w[:, columns[k][b]])
-            gate = gate_now if gate is None else gate + gate_now
-            up = up_now if up is None else up + up_now
+def add_pair(held, columns, weights, totals):
+    for b in (0, 1):
+        now = [dot_last(held[b], weight[:, columns[b]]) for weight in weights]
+        totals = now if totals is None else [x + y for x, y in zip(totals, now)]
+    return totals
+
+
+def store_pair(part, columns, weights, factors):
+    for b in (0, 1):
+        terms = [dot(f, weight[:, columns[b]]) for f, weight in zip(factors, weights)]
+        part[b] = sum(terms[1:], terms[0]).astype(part.dtype)
+
+
+def early_kernel(steps, chain, *refs):
+    held, rest = refs[: steps - 1], refs[steps - 1 :]
+    weights, totals = rest[: len(rest) // 2], rest[len(rest) // 2 :]
+    columns = columns_of(steps, held[0].shape[2], chain)
+    sums = None
+    for k in range(steps - 1):
+        sums = add_pair(held[k], columns[k], weights, sums)
+    for total, value in zip(totals, sums):
+        total[...] = value
+
+
+def forward_kernel(steps, held, gate_w, up_w, down_w, gate_sum, up_sum, gate_ref, up_ref, *parts):
+    columns = columns_of(steps, held.shape[2], 0)
+    gate, up = add_pair(held, columns[-1], (gate_w, up_w), [gate_sum[...], up_sum[...]])
     gate_ref[...] = gate
     up_ref[...] = up
     hidden = (gate * jax.nn.sigmoid(gate) * up).astype(bf16)
     for k in reversed(range(steps)):
-        for b in (0, 1):
-            parts[k][b] = dot(hidden, down_w[:, columns[k][b]]).astype(parts[k].dtype)
-
-
-def backward_kernel(steps, *refs):
-    held, (gate_w, up_w, down_w) = refs[:steps], refs[steps : steps + 3]
-    gate_ref, up_ref = refs[steps + 3 : steps + 5]
-    parts = refs[steps + 5 :]
-    columns = columns_of(steps, held[0].shape[2], 1)
-    hidden_grad = None
-    for k in range(steps):
-        for b in (0, 1):
-            now = dot_last(held[k][b], down_w[:, columns[k][b]])
-            hidden_grad = now if hidden_grad is None else hidden_grad + now
+        store_pair(parts[k], columns[k], (down_w,), (hidden,))
+
+
+def backward_kernel(
+    steps, held, gate_w, up_w, down_w, grad_sum, gate_ref, up_ref, gate_grad_ref, up_grad_ref, part
+):
+    columns = columns_of(steps, held.shape[2], 1)[-1]
+    (hidden_grad,) = add_pair(held, columns, (down_w,), [grad_sum[...]])
     gate, up = gate_ref[...], up_ref[...]
     squash = jax.nn.sigmoid(gate)
     up_grad = (hidden_grad * (gate * squash)).astype(bf16)
     gate_grad = (hidden_grad * up * squash * (1.0 + gate * (1.0 - squash))).astype(bf16)
-    for k in reversed(range(steps)):
-        for b in (0, 1):
-            part = dot(gate_grad, gate_w[:, columns[k][b]]) + dot(up_grad, up_w[:, columns[k][b]])
-            parts[k][b] = part.astype(parts[k].dtype)
-
-
-def call(kernel, steps, operands, extra_shapes, pair_shape, flops):
-    shapes = extra_shapes + [
-        jax.ShapeDtypeStruct(pair_shape, f32 if k < steps - 1 else bf16) for k in range(steps)
-    ]
+    gate_grad_ref[...] = gate_grad
+    up_grad_ref[...] = up_grad
+    store_pair(part, columns, (gate_w, up_w), (gate_grad, up_grad))
+
+
+def late_kernel(steps, chain, *refs):
+    parts = refs[-(steps - 1) :]
+    rest = refs[: -(steps - 1)]
+    weights, factors = rest[: len(rest) // 2], [f[...] for f in rest[len(rest) // 2 :]]
+    columns = columns_of(steps, parts[0].shape[2], chain)
+    for k in reversed(range(steps - 1)):
+        store_pair(parts[k], columns[k], weights, factors)
+
+
+def call(kernel, operands, shapes, flops, moved=4 << 20):
     return pl.pallas_call(
-        lambda *refs: kernel(steps, *refs),
+        kernel,
         out_shape=shapes,
         in_specs=[VMEM] * len(operands),
         out_specs=[VMEM] * len(shapes),
         compiler_params=pltpu.CompilerParams(vmem_limit_bytes=VMEM_LIMIT),
-        cost_estimate=pl.CostEstimate(flops=flops, bytes_accessed=9 << 20, transcendentals=0),
+        cost_estimate=pl.CostEstimate(flops=flops, bytes_accessed=moved, transcendentals=0),
     )(*operands)
 
 
@@ -221,18 +236,41 @@
     for step in range(1, steps):
         token_held.append(exchange(token_held[-1], step, 0))
         grad_held.append(exchange(grad_held[-1], step, 1))
-    gate_weight, up_weight, down_weight = w_gate[0].T, w_up[0].T, w_down[0]
-    weights = [gate_weight, up_weight, down_weight]
-    hidden_width, width = down_weight.shape
-    square = jax.ShapeDtypeStruct((slots, hidden_width), f32)
-    pair_shape = (2, slots, local_width)
+    gate_w, up_w, down_w = w_gate[0].T, w_up[0].T, w_down[0]
+    hidden_width, width = down_w.shape
+    total = jax.ShapeDtypeStruct((slots, hidden_width), f32)
+    factor = jax.ShapeDtypeStruct((slots, hidden_width), bf16)
+    leaving = jax.ShapeDtypeStruct((2, slots, local_width), bf16)
+    kept = [jax.ShapeDtypeStruct((2, slots, local_width), f32)] * (steps - 1)
     flops = 2 * slots * hidden_width * width
+
+    def early(*refs, chain):
+        early_kernel(steps, chain, *refs)
+
+    def late(*refs, chain):
+        late_kernel(steps, chain, *refs)
+
+    sums = call(
+        functools.partial(early, chain=0), token_held[:-1] + [gate_w, up_w], [total] * 2, 2 * flops
+    )
+    (grad_sum,) = call(functools.partial(early, chain=1), grad_held[:-1] + [down_w], [total], flops)
     gate, up, *out_parts = call(
-        forward_kernel, steps, token_held + weights, [square, square], pair_shape, 3 * flops
-    )
-    input_parts = call(
-        backward_kernel, steps, grad_held + weights + [gate, up], [], pair_shape, 3 * flops
-    )
+        functools.partial(forward_kernel, steps),
+        [token_held[-1], gate_w, up_w, down_w, *sums],
+        [total, total, *kept, leaving],
+        flops,
+    )
+    gate_grad, up_grad, input_first = call(
+        functools.partial(backward_kernel, steps),
+        [grad_held[-1], gate_w, up_w, down_w, grad_sum, gate, up],
+        [factor, factor, leaving],
+        3 * flops,
+        9 << 20,
+    )
+    input_parts = [
+        *call(functools.partial(late, chain=1), [gate_w, up_w, gate_grad, up_grad], kept, 2 * flops),
+        input_first,
+    ]
     out_sum, input_sum = out_parts[-1], input_parts[-1]
     for step in reversed(range(1, steps)):
         out_sum = sum_step(out_parts, out_sum, step, 0)

time: 186 us -> 185 us (level)
    pallas_call x2 -> x5, Pallas kernels: 3.82 us -> 3.84 us  [call(): pl.pallas_call(kernel, out_shape=shapes, in_specs=[VMEM] * len(operands),...]
  transfers between devices with their start and end apart: 16 -> 16, of which waited for: 16 -> 14; matrix products, arithmetic and copies ran while one was open for 0% -> 0% of each run, Pallas kernels for 2% -> 2%
where the time goes in v8:
time: 185 us; the launch traced here: 184 us
  blocking collectives  80.5 us (44%)
  starting transfers between devices  46.9 us (25%)
  waiting for transfers between devices  45.3 us (24%)
  Pallas kernels  8.35 us (5%)
    ppermute x16, starting transfers between devices, exchange(): return lax.ppermute(value, ('etp', 'ep'), pairs)  46.9 us
    ppermute x16, waiting for transfers between devices, exchange(): return lax.ppermute(value, ('etp', 'ep'), pairs)  45.3 us
    all_to_all x1, blocking collectives, on_device(): lax.all_to_all(send.reshape(owners, 2 * capacity, local_width), 'ep', spl...  41.3 us
    all_to_all x1, blocking collectives, on_device(): lax.all_to_all(unsorted.reshape(owners, 2 * capacity, local_width), 'ep',...  39.2 us
    pallas_call x5, Pallas kernels, call(): pl.pallas_call(kernel, out_shape=shapes, in_specs=[VMEM] * len(operands),...  3.84 us
  transfers between devices with their start and end apart: 16, of which 14 were waited for; matrix products, arithmetic and copies ran while one was open for 0% of the time, Pallas kernels for 2%

profile of v8, /device:TPU:1, one launch (start us, length us, event | category | flops | bytes accessed | tf_op | source)
XLA Modules:
  0.0 184.2 jit_solution(587002452042381769)
XLA Ops:
  0.6 2.5 %shard_map.86 = bf16[384,512]{1,0:T(8,128)(2,1)} custom-call(s32[8,16]{1,0:T(8,128)} %bitcast.31, f32[8,16]{1,0:T(8,128)} %bitcast.33, bf16[16,512]{1,0:T(8,128)(2,1)} %refs_2_.1, bf16[16,512]{1,0:T(8,128)(2,1)} %refs_3_.1), custom_call_target="tpu_custom_call" | custom-call | tf_op jit(solution)/shard_map/pallas_call | solution.py:211
  3.2 1.1 reshape.16
  4.3 41.3 %all_to_all.10 = bf16[96,4,512]{2,1,0:T(4,128)(2,1)S(1)} all-to-all(bf16[96,4,512]{2,1,0:T(4,128)(2,1)S(1)} %reshape.16), channel_id=1, replica_groups=mesh['etp'=8,'ep'=96] {'ep'}, dimensions={0} | all-to-all | bytes 786432 | tf_op jit(solution)/shard_map/all_to_all | solution.py:220
  45.7 0.4 shard_map.87
  46.1 5.2 %collective-permute-start = (bf16[192,512]{1,0:T(8,128)(2,1)S(1)}, bf16[192,512]{1,0:T(8,128)(2,1)S(1)}, u32[]{:S(2)}, u32[]{:S(2)}) collective-permute-start(bf16[192,512]{1,0:T(8,128)(2,1)S(1)} %get-tuple-element.20), channel_id=1, source_target_pairs={{0,96},{1,673},{2,98},{3,675},{4,100},{5,677},{6,102},{7,679},{8,1... | collective-permute-start | bytes 589832 | tf_op jit(solution)/shard_map/ppermute | solution.py:115
  51.3 1.9 %collective-permute-start.1 = (bf16[192,512]{1,0:T(8,128)(2,1)S(1)}, bf16[192,512]{1,0:T(8,128)(2,1)S(1)}, u32[]{:S(2)}, u32[]{:S(2)}) collective-permute-start(bf16[192,512]{1,0:T(8,128)(2,1)S(1)} %get-tuple-element.21), channel_id=1, source_target_pairs={{0,672},{1,97},{2,674},{3,99},{4,676},{5,101},{6,678},{7,103},{8,6... | collective-permute-start | bytes 589832 | tf_op jit(solution)/shard_map/ppermute | solution.py:115
  53.2 1.1 collective-permute-done
  54.4 3.7 %collective-permute-done.1 = bf16[192,512]{1,0:T(8,128)(2,1)S(1)} collective-permute-done((bf16[192,512]{1,0:T(8,128)(2,1)S(1)}, bf16[192,512]{1,0:T(8,128)(2,1)S(1)}, u32[]{:S(2)}, u32[]{:S(2)}) %collective-permute-start.1) | collective-permute-done | bytes 196640 | tf_op jit(solution)/shard_map/ppermute | solution.py:115
  58.1 2.2 %collective-permute-start.2 = (bf16[2,192,512]{2,1,0:T(8,128)(2,1)S(1)}, bf16[2,192,512]{2,1,0:T(8,128)(2,1)S(1)}, u32[]{:S(2)}, u32[]{:S(2)}) collective-permute-start(bf16[2,192,512]{2,1,0:T(8,128)(2,1)S(1)} %pad_maximum_fusion.refs_0_), channel_id=1, source_target_pairs={{0,672},{1,97},{2,674},{3,99},{4,676},{5,101},{6,678},{7,103},{8,6... | collective-permute-start | bytes 1179656 | tf_op jit(solution)/shard_map/ppermute | solution.py:115
  60.3 4.9 %collective-permute-start.9 = (bf16[2,192,512]{2,1,0:T(8,128)(2,1)S(1)}, bf16[2,192,512]{2,1,0:T(8,128)(2,1)S(1)}, u32[]{:S(2)}, u32[]{:S(2)}) collective-permute-start(bf16[2,192,512]{2,1,0:T(8,128)(2,1)S(1)} %pad_maximum_fusion.1.refs_0_), channel_id=1, source_target_pairs={{0,96},{1,673},{2,98},{3,675},{4,100},{5,677},{6,102},{7,679},{8,1... | collective-permute-start | bytes 1179656 | tf_op jit(solution)/shard_map/ppermute | solution.py:115
  65.2 1.7 collective-permute-done.2.refs_1_
  66.9 3.5 %collective-permute-start.3 = (bf16[2,192,512]{2,1,0:T(8,128)(2,1)S(1)}, bf16[2,192,512]{2,1,0:T(8,128)(2,1)S(1)}, u32[]{:S(2)}, u32[]{:S(2)}) collective-permute-start(bf16[2,192,512]{2,1,0:T(8,128)(2,1)S(1)} %collective-permute-done.2.refs_1_), channel_id=1, source_target_pairs={{0,96},{1,673},{2,98},{3,675},{4,100},{5,677},{6,102},{7,679},{8,1... | collective-permute-start | bytes 1179656 | tf_op jit(solution)/shard_map/ppermute | solution.py:115
  70.3 4.3 %collective-permute-done.9.refs_1_ = bf16[2,192,512]{2,1,0:T(8,128)(2,1)S(1)} collective-permute-done((bf16[2,192,512]{2,1,0:T(8,128)(2,1)S(1)}, bf16[2,192,512]{2,1,0:T(8,128)(2,1)S(1)}, u32[]{:S(2)}, u32[]{:S(2)}) %collective-permute-start.9) | collective-permute-done | bytes 393248 | tf_op jit(solution)/shard_map/ppermute | solution.py:115
  74.6 1.9 %collective-permute-start.10 = (bf16[2,192,512]{2,1,0:T(8,128)(2,1)S(1)}, bf16[2,192,512]{2,1,0:T(8,128)(2,1)S(1)}, u32[]{:S(2)}, u32[]{:S(2)}) collective-permute-start(bf16[2,192,512]{2,1,0:T(8,128)(2,1)S(1)} %collective-permute-done.9.refs_1_), channel_id=1, source_target_pairs={{0,672},{1,97},{2,674},{3,99},{4,676},{5,101},{6,678},{7,103},{8,6... | collective-permute-start | bytes 1179656 | tf_op jit(solution)/shard_map/ppermute | solution.py:115
  76.6 2.1 %collective-permute-done.3.refs_2_ = bf16[2,192,512]{2,1,0:T(8,128)(2,1)S(1)} collective-permute-done((bf16[2,192,512]{2,1,0:T(8,128)(2,1)S(1)}, bf16[2,192,512]{2,1,0:T(8,128)(2,1)S(1)}, u32[]{:S(2)}, u32[]{:S(2)}) %collective-permute-start.3) | collective-permute-done | bytes 393248 | tf_op jit(solution)/shard_map/ppermute | solution.py:115
  78.7 1.9 %collective-permute-start.4 = (bf16[2,192,512]{2,1,0:T(8,128)(2,1)S(1)}, bf16[2,192,512]{2,1,0:T(8,128)(2,1)S(1)}, u32[]{:S(2)}, u32[]{:S(2)}) collective-permute-start(bf16[2,192,512]{2,1,0:T(8,128)(2,1)S(1)} %collective-permute-done.3.refs_2_), channel_id=1, source_target_pairs={{0,672},{1,97},{2,674},{3,99},{4,676},{5,101},{6,678},{7,103},{8,6... | collective-permute-start | bytes 1179656 | tf_op jit(solution)/shard_map/ppermute | solution.py:115
  80.6 6.3 %collective-permute-done.10.refs_2_ = bf16[2,192,512]{2,1,0:T(8,128)(2,1)S(1)} collective-permute-done((bf16[2,192,512]{2,1,0:T(8,128)(2,1)S(1)}, bf16[2,192,512]{2,1,0:T(8,128)(2,1)S(1)}, u32[]{:S(2)}, u32[]{:S(2)}) %collective-permute-start.10) | collective-permute-done | bytes 393248 | tf_op jit(solution)/shard_map/ppermute | solution.py:115
  86.8 4.1 %collective-permute-start.11 = (bf16[2,192,512]{2,1,0:T(8,128)(2,1)S(1)}, bf16[2,192,512]{2,1,0:T(8,128)(2,1)S(1)}, u32[]{:S(2)}, u32[]{:S(2)}) collective-permute-start(bf16[2,192,512]{2,1,0:T(8,128)(2,1)S(1)} %collective-permute-done.10.refs_2_), channel_id=1, source_target_pairs={{0,96},{1,673},{2,98},{3,675},{4,100},{5,677},{6,102},{7,679},{8,1... | collective-permute-start | bytes 1179656 | tf_op jit(solution)/shard_map/ppermute | solution.py:115
  91.0 0.8 shard_map.88
  91.8 0.9 shard_map.89
  92.7 1.9 %collective-permute-start.5 = (bf16[2,192,512]{2,1,0:T(8,128)(2,1)S(1)}, bf16[2,192,512]{2,1,0:T(8,128)(2,1)S(1)}, u32[]{:S(2)}, u32[]{:S(2)}) collective-permute-start(bf16[2,192,512]{2,1,0:T(8,128)(2,1)S(1)} %get-tuple-element.28), channel_id=1, source_target_pairs={{0,672},{1,97},{2,674},{3,99},{4,676},{5,101},{6,678},{7,103},{8,6... | collective-permute-start | bytes 1179656 | tf_op jit(solution)/shard_map/ppermute | solution.py:115
  94.7 0.5 shard_map.90.grad_sum
  95.2 3.1 %collective-permute-done.11.held = bf16[2,192,512]{2,1,0:T(8,128)(2,1)S(1)} collective-permute-done((bf16[2,192,512]{2,1,0:T(8,128)(2,1)S(1)}, bf16[2,192,512]{2,1,0:T(8,128)(2,1)S(1)}, u32[]{:S(2)}, u32[]{:S(2)}) %collective-permute-start.11) | collective-permute-done | bytes 393248 | tf_op jit(solution)/shard_map/ppermute | solution.py:115
  98.3 0.8 shard_map.91
  99.1 3.4 %collective-permute-start.12 = (bf16[2,192,512]{2,1,0:T(8,128)(2,1)S(1)}, bf16[2,192,512]{2,1,0:T(8,128)(2,1)S(1)}, u32[]{:S(2)}, u32[]{:S(2)}) collective-permute-start(bf16[2,192,512]{2,1,0:T(8,128)(2,1)S(1)} %get-tuple-element.37), channel_id=1, source_target_pairs={{0,96},{1,673},{2,98},{3,675},{4,100},{5,677},{6,102},{7,679},{8,1... | collective-permute-start | bytes 1179656 | tf_op jit(solution)/shard_map/ppermute | solution.py:115
  102.6 1.2 collective-permute-done.5
  103.8 0.1 add_convert_fusion.5
  103.9 5.2 %collective-permute-start.6 = (bf16[2,192,512]{2,1,0:T(8,128)(2,1)S(1)}, bf16[2,192,512]{2,1,0:T(8,128)(2,1)S(1)}, u32[]{:S(2)}, u32[]{:S(2)}) collective-permute-start(bf16[2,192,512]{2,1,0:T(8,128)(2,1)S(1)} %add_convert_fusion.5), channel_id=1, source_target_pairs={{0,96},{1,673},{2,98},{3,675},{4,100},{5,677},{6,102},{7,679},{8,1... | collective-permute-start | bytes 1179656 | tf_op jit(solution)/shard_map/ppermute | solution.py:115
  109.1 0.8 shard_map.92
  109.9 0.1 add_convert_fusion.2
  110.1 1.9 %collective-permute-start.13 = (bf16[2,192,512]{2,1,0:T(8,128)(2,1)S(1)}, bf16[2,192,512]{2,1,0:T(8,128)(2,1)S(1)}, u32[]{:S(2)}, u32[]{:S(2)}) collective-permute-start(bf16[2,192,512]{2,1,0:T(8,128)(2,1)S(1)} %add_convert_fusion.2), channel_id=1, source_target_pairs={{0,672},{1,97},{2,674},{3,99},{4,676},{5,101},{6,678},{7,103},{8,6... | collective-permute-start | bytes 1179656 | tf_op jit(solution)/shard_map/ppermute | solution.py:115
  112.0 5.3 %collective-permute-done.6 = bf16[2,192,512]{2,1,0:T(8,128)(2,1)S(1)} collective-permute-done((bf16[2,192,512]{2,1,0:T(8,128)(2,1)S(1)}, bf16[2,192,512]{2,1,0:T(8,128)(2,1)S(1)}, u32[]{:S(2)}, u32[]{:S(2)}) %collective-permute-start.6) | collective-permute-done | bytes 393248 | tf_op jit(solution)/shard_map/ppermute | solution.py:115
  117.3 0.1 add_convert_fusion.4
  117.4 1.9 %collective-permute-start.7 = (bf16[2,192,512]{2,1,0:T(8,128)(2,1)S(1)}, bf16[2,192,512]{2,1,0:T(8,128)(2,1)S(1)}, u32[]{:S(2)}, u32[]{:S(2)}) collective-permute-start(bf16[2,192,512]{2,1,0:T(8,128)(2,1)S(1)} %add_convert_fusion.4), channel_id=1, source_target_pairs={{0,672},{1,97},{2,674},{3,99},{4,676},{5,101},{6,678},{7,103},{8,6... | collective-permute-start | bytes 1179656 | tf_op jit(solution)/shard_map/ppermute | solution.py:115
  119.3 2.0 %collective-permute-done.13 = bf16[2,192,512]{2,1,0:T(8,128)(2,1)S(1)} collective-permute-done((bf16[2,192,512]{2,1,0:T(8,128)(2,1)S(1)}, bf16[2,192,512]{2,1,0:T(8,128)(2,1)S(1)}, u32[]{:S(2)}, u32[]{:S(2)}) %collective-permute-start.13) | collective-permute-done | bytes 393248 | tf_op jit(solution)/shard_map/ppermute | solution.py:115
  121.3 0.1 add_convert_fusion.1
  121.5 2.4 %collective-permute-start.14 = (bf16[2,192,512]{2,1,0:T(8,128)(2,1)S(1)}, bf16[2,192,512]{2,1,0:T(8,128)(2,1)S(1)}, u32[]{:S(2)}, u32[]{:S(2)}) collective-permute-start(bf16[2,192,512]{2,1,0:T(8,128)(2,1)S(1)} %add_convert_fusion.1), channel_id=1, source_target_pairs={{0,96},{1,673},{2,98},{3,675},{4,100},{5,677},{6,102},{7,679},{8,1... | collective-permute-start | bytes 1179656 | tf_op jit(solution)/shard_map/ppermute | solution.py:115
  123.8 6.5 %collective-permute-done.7 = bf16[2,192,512]{2,1,0:T(8,128)(2,1)S(1)} collective-permute-done((bf16[2,192,512]{2,1,0:T(8,128)(2,1)S(1)}, bf16[2,192,512]{2,1,0:T(8,128)(2,1)S(1)}, u32[]{:S(2)}, u32[]{:S(2)}) %collective-permute-start.7) | collective-permute-done | bytes 393248 | tf_op jit(solution)/shard_map/ppermute | solution.py:115
  130.3 0.1 add_convert_fusion.3.refs_0_
  130.5 2.6 %collective-permute-start.8 = (bf16[192,512]{1,0:T(8,128)(2,1)S(1)}, bf16[192,512]{1,0:T(8,128)(2,1)S(1)}, u32[]{:S(2)}, u32[]{:S(2)}) collective-permute-start(bf16[192,512]{1,0:T(8,128)(2,1)S(1)} %slice_bitcast_fusion.1), channel_id=1, source_target_pairs={{0,96},{1,673},{2,98},{3,675},{4,100},{5,677},{6,102},{7,679},{8,1... | collective-permute-start | bytes 589832 | tf_op jit(solution)/shard_map/ppermute | solution.py:115
  133.1 1.9 %collective-permute-done.14 = bf16[2,192,512]{2,1,0:T(8,128)(2,1)S(1)} collective-permute-done((bf16[2,192,512]{2,1,0:T(8,128)(2,1)S(1)}, bf16[2,192,512]{2,1,0:T(8,128)(2,1)S(1)}, u32[]{:S(2)}, u32[]{:S(2)}) %collective-permute-start.14) | collective-permute-done | bytes 393248 | tf_op jit(solution)/shard_map/ppermute | solution.py:115
  135.0 0.1 add_convert_fusion.refs_2_
  135.2 1.9 %collective-permute-start.15 = (bf16[192,512]{1,0:T(8,128)(2,1)S(1)}, bf16[192,512]{1,0:T(8,128)(2,1)S(1)}, u32[]{:S(2)}, u32[]{:S(2)}) collective-permute-start(bf16[192,512]{1,0:T(8,128)(2,1)S(1)} %slice_bitcast_fusion), channel_id=1, source_target_pairs={{0,672},{1,97},{2,674},{3,99},{4,676},{5,101},{6,678},{7,103},{8,6... | collective-permute-start | bytes 589832 | tf_op jit(solution)/shard_map/ppermute | solution.py:115
  137.1 2.7 %collective-permute-done.8.refs_1_ = bf16[192,512]{1,0:T(8,128)(2,1)S(1)} collective-permute-done((bf16[192,512]{1,0:T(8,128)(2,1)S(1)}, bf16[192,512]{1,0:T(8,128)(2,1)S(1)}, u32[]{:S(2)}, u32[]{:S(2)}) %collective-permute-start.8) | collective-permute-done | bytes 196640 | tf_op jit(solution)/shard_map/ppermute | solution.py:115
  139.8 3.3 %collective-permute-done.15.refs_3_ = bf16[192,512]{1,0:T(8,128)(2,1)S(1)} collective-permute-done((bf16[192,512]{1,0:T(8,128)(2,1)S(1)}, bf16[192,512]{1,0:T(8,128)(2,1)S(1)}, u32[]{:S(2)}, u32[]{:S(2)}) %collective-permute-start.15) | collective-permute-done | bytes 196640 | tf_op jit(solution)/shard_map/ppermute | solution.py:115
  143.2 0.4 shard_map.93
  143.7 39.2 %all_to_all.11 = bf16[96,4,512]{2,1,0:T(4,128)(2,1)S(1)} all-to-all(bf16[96,4,512]{2,1,0:T(4,128)(2,1)S(1)} %reshape.18), channel_id=1, replica_groups=mesh['etp'=8,'ep'=96] {'ep'}, dimensions={0} | all-to-all | bytes 786432 | tf_op jit(solution)/shard_map/all_to_all | solution.py:285
  183.0 1.2 shard_map.94
  (19 shorter events, 0.4 us)
Async XLA Ops:
  0.6 45.0 %copy-start.2 = (bf16[1,192,4096]{2,1,0:T(8,128)(2,1)S(1)}, bf16[1,192,4096]{2,1,0:T(8,128)(2,1)}, u32[]{:S(2)}) copy-start(bf16[1,192,4096]{2,1,0:T(8,128)(2,1)} %param.13) | copy-start | bytes 4718596
  45.7 45.3 %copy-start = (bf16[1,4096,192]{1,2,0:T(8,128)(2,1)S(1)}, bf16[1,4096,192]{1,2,0:T(8,128)(2,1)}, u32[]{:S(2)}) copy-start(bf16[1,4096,192]{1,2,0:T(8,128)(2,1)} %param.11) | copy-start | bytes 4718596
  45.7 45.3 %copy-start.1 = (bf16[1,4096,192]{1,2,0:T(8,128)(2,1)S(1)}, bf16[1,4096,192]{1,2,0:T(8,128)(2,1)}, u32[]{:S(2)}) copy-start(bf16[1,4096,192]{1,2,0:T(8,128)(2,1)} %param.12) | copy-start | bytes 4718596
  46.1 8.3 %collective-permute-start = (bf16[192,512]{1,0:T(8,128)(2,1)S(1)}, bf16[192,512]{1,0:T(8,128)(2,1)S(1)}, u32[]{:S(2)}, u32[]{:S(2)}) collective-permute-start(bf16[192,512]{1,0:T(8,128)(2,1)S(1)} %get-tuple-element.20), channel_id=1, source_target_pairs={{0,96},{1,673},{2,98},{3,675},{4,100},{5,677},{6,102},{7,679},{8,1... | collective-permute-start | bytes 589832 | tf_op jit(solution)/shard_map/ppermute | solution.py:115
  51.3 6.7 %collective-permute-start.1 = (bf16[192,512]{1,0:T(8,128)(2,1)S(1)}, bf16[192,512]{1,0:T(8,128)(2,1)S(1)}, u32[]{:S(2)}, u32[]{:S(2)}) collective-permute-start(bf16[192,512]{1,0:T(8,128)(2,1)S(1)} %get-tuple-element.21), channel_id=1, source_target_pairs={{0,672},{1,97},{2,674},{3,99},{4,676},{5,101},{6,678},{7,103},{8,6... | collective-permute-start | bytes 589832 | tf_op jit(solution)/shard_map/ppermute | solution.py:115
  58.1 8.8 %collective-permute-start.2 = (bf16[2,192,512]{2,1,0:T(8,128)(2,1)S(1)}, bf16[2,192,512]{2,1,0:T(8,128)(2,1)S(1)}, u32[]{:S(2)}, u32[]{:S(2)}) collective-permute-start(bf16[2,192,512]{2,1,0:T(8,128)(2,1)S(1)} %pad_maximum_fusion.refs_0_), channel_id=1, source_target_pairs={{0,672},{1,97},{2,674},{3,99},{4,676},{5,101},{6,678},{7,103},{8,6... | collective-permute-start | bytes 1179656 | tf_op jit(solution)/shard_map/ppermute | solution.py:115
  60.3 14.4 %collective-permute-start.9 = (bf16[2,192,512]{2,1,0:T(8,128)(2,1)S(1)}, bf16[2,192,512]{2,1,0:T(8,128)(2,1)S(1)}, u32[]{:S(2)}, u32[]{:S(2)}) collective-permute-start(bf16[2,192,512]{2,1,0:T(8,128)(2,1)S(1)} %pad_maximum_fusion.1.refs_0_), channel_id=1, source_target_pairs={{0,96},{1,673},{2,98},{3,675},{4,100},{5,677},{6,102},{7,679},{8,1... | collective-permute-start | bytes 1179656 | tf_op jit(solution)/shard_map/ppermute | solution.py:115
  66.9 11.8 %collective-permute-start.3 = (bf16[2,192,512]{2,1,0:T(8,128)(2,1)S(1)}, bf16[2,192,512]{2,1,0:T(8,128)(2,1)S(1)}, u32[]{:S(2)}, u32[]{:S(2)}) collective-permute-start(bf16[2,192,512]{2,1,0:T(8,128)(2,1)S(1)} %collective-permute-done.2.refs_1_), channel_id=1, source_target_pairs={{0,96},{1,673},{2,98},{3,675},{4,100},{5,677},{6,102},{7,679},{8,1... | collective-permute-start | bytes 1179656 | tf_op jit(solution)/shard_map/ppermute | solution.py:115
  74.6 12.2 %collective-permute-start.10 = (bf16[2,192,512]{2,1,0:T(8,128)(2,1)S(1)}, bf16[2,192,512]{2,1,0:T(8,128)(2,1)S(1)}, u32[]{:S(2)}, u32[]{:S(2)}) collective-permute-start(bf16[2,192,512]{2,1,0:T(8,128)(2,1)S(1)} %collective-permute-done.9.refs_1_), channel_id=1, source_target_pairs={{0,672},{1,97},{2,674},{3,99},{4,676},{5,101},{6,678},{7,103},{8,6... | collective-permute-start | bytes 1179656 | tf_op jit(solution)/shard_map/ppermute | solution.py:115
  78.7 13.1 %collective-permute-start.4 = (bf16[2,192,512]{2,1,0:T(8,128)(2,1)S(1)}, bf16[2,192,512]{2,1,0:T(8,128)(2,1)S(1)}, u32[]{:S(2)}, u32[]{:S(2)}) collective-permute-start(bf16[2,192,512]{2,1,0:T(8,128)(2,1)S(1)} %collective-permute-done.3.refs_2_), channel_id=1, source_target_pairs={{0,672},{1,97},{2,674},{3,99},{4,676},{5,101},{6,678},{7,103},{8,6... | collective-permute-start | bytes 1179656 | tf_op jit(solution)/shard_map/ppermute | solution.py:115
  86.8 11.5 %collective-permute-start.11 = (bf16[2,192,512]{2,1,0:T(8,128)(2,1)S(1)}, bf16[2,192,512]{2,1,0:T(8,128)(2,1)S(1)}, u32[]{:S(2)}, u32[]{:S(2)}) collective-permute-start(bf16[2,192,512]{2,1,0:T(8,128)(2,1)S(1)} %collective-permute-done.10.refs_2_), channel_id=1, source_target_pairs={{0,96},{1,673},{2,98},{3,675},{4,100},{5,677},{6,102},{7,679},{8,1... | collective-permute-start | bytes 1179656 | tf_op jit(solution)/shard_map/ppermute | solution.py:115
  92.7 11.1 %collective-permute-start.5 = (bf16[2,192,512]{2,1,0:T(8,128)(2,1)S(1)}, bf16[2,192,512]{2,1,0:T(8,128)(2,1)S(1)}, u32[]{:S(2)}, u32[]{:S(2)}) collective-permute-start(bf16[2,192,512]{2,1,0:T(8,128)(2,1)S(1)} %get-tuple-element.28), channel_id=1, source_target_pairs={{0,672},{1,97},{2,674},{3,99},{4,676},{5,101},{6,678},{7,103},{8,6... | collective-permute-start | bytes 1179656 | tf_op jit(solution)/shard_map/ppermute | solution.py:115
  99.1 10.8 %collective-permute-start.12 = (bf16[2,192,512]{2,1,0:T(8,128)(2,1)S(1)}, bf16[2,192,512]{2,1,0:T(8,128)(2,1)S(1)}, u32[]{:S(2)}, u32[]{:S(2)}) collective-permute-start(bf16[2,192,512]{2,1,0:T(8,128)(2,1)S(1)} %get-tuple-element.37), channel_id=1, source_target_pairs={{0,96},{1,673},{2,98},{3,675},{4,100},{5,677},{6,102},{7,679},{8,1... | collective-permute-start | bytes 1179656 | tf_op jit(solution)/shard_map/ppermute | solution.py:115
  103.9 13.4 %collective-permute-start.6 = (bf16[2,192,512]{2,1,0:T(8,128)(2,1)S(1)}, bf16[2,192,512]{2,1,0:T(8,128)(2,1)S(1)}, u32[]{:S(2)}, u32[]{:S(2)}) collective-permute-start(bf16[2,192,512]{2,1,0:T(8,128)(2,1)S(1)} %add_convert_fusion.5), channel_id=1, source_target_pairs={{0,96},{1,673},{2,98},{3,675},{4,100},{5,677},{6,102},{7,679},{8,1... | collective-permute-start | bytes 1179656 | tf_op jit(solution)/shard_map/ppermute | solution.py:115
  110.1 11.3 %collective-permute-start.13 = (bf16[2,192,512]{2,1,0:T(8,128)(2,1)S(1)}, bf16[2,192,512]{2,1,0:T(8,128)(2,1)S(1)}, u32[]{:S(2)}, u32[]{:S(2)}) collective-permute-start(bf16[2,192,512]{2,1,0:T(8,128)(2,1)S(1)} %add_convert_fusion.2), channel_id=1, source_target_pairs={{0,672},{1,97},{2,674},{3,99},{4,676},{5,101},{6,678},{7,103},{8,6... | collective-permute-start | bytes 1179656 | tf_op jit(solution)/shard_map/ppermute | solution.py:115
  117.4 12.9 %collective-permute-start.7 = (bf16[2,192,512]{2,1,0:T(8,128)(2,1)S(1)}, bf16[2,192,512]{2,1,0:T(8,128)(2,1)S(1)}, u32[]{:S(2)}, u32[]{:S(2)}) collective-permute-start(bf16[2,192,512]{2,1,0:T(8,128)(2,1)S(1)} %add_convert_fusion.4), channel_id=1, source_target_pairs={{0,672},{1,97},{2,674},{3,99},{4,676},{5,101},{6,678},{7,103},{8,6... | collective-permute-start | bytes 1179656 | tf_op jit(solution)/shard_map/ppermute | solution.py:115
  121.5 13.6 %collective-permute-start.14 = (bf16[2,192,512]{2,1,0:T(8,128)(2,1)S(1)}, bf16[2,192,512]{2,1,0:T(8,128)(2,1)S(1)}, u32[]{:S(2)}, u32[]{:S(2)}) collective-permute-start(bf16[2,192,512]{2,1,0:T(8,128)(2,1)S(1)} %add_convert_fusion.1), channel_id=1, source_target_pairs={{0,96},{1,673},{2,98},{3,675},{4,100},{5,677},{6,102},{7,679},{8,1... | collective-permute-start | bytes 1179656 | tf_op jit(solution)/shard_map/ppermute | solution.py:115
  130.5 9.4 %collective-permute-start.8 = (bf16[192,512]{1,0:T(8,128)(2,1)S(1)}, bf16[192,512]{1,0:T(8,128)(2,1)S(1)}, u32[]{:S(2)}, u32[]{:S(2)}) collective-permute-start(bf16[192,512]{1,0:T(8,128)(2,1)S(1)} %slice_bitcast_fusion.1), channel_id=1, source_target_pairs={{0,96},{1,673},{2,98},{3,675},{4,100},{5,677},{6,102},{7,679},{8,1... | collective-permute-start | bytes 589832 | tf_op jit(solution)/shard_map/ppermute | solution.py:115
  135.2 8.0 %collective-permute-start.15 = (bf16[192,512]{1,0:T(8,128)(2,1)S(1)}, bf16[192,512]{1,0:T(8,128)(2,1)S(1)}, u32[]{:S(2)}, u32[]{:S(2)}) collective-permute-start(bf16[192,512]{1,0:T(8,128)(2,1)S(1)} %slice_bitcast_fusion), channel_id=1, source_target_pairs={{0,672},{1,97},{2,674},{3,99},{4,676},{5,101},{6,678},{7,103},{8,6... | collective-permute-start | bytes 589832 | tf_op jit(solution)/shard_map/ppermute | solution.py:115
  143.6 39.4 %copy-start.3 = (s32[16,8]{0,1:T(8,128)S(1)}, s32[16,8]{0,1:T(8,128)}, u32[]{:S(2)}) copy-start(s32[16,8]{0,1:T(8,128)} %param.8) | copy-start | bytes 1540
  143.6 39.4 %copy-start.4 = (f32[16,8]{0,1:T(8,128)S(1)}, f32[16,8]{0,1:T(8,128)}, u32[]{:S(2)}) copy-start(f32[16,8]{0,1:T(8,128)} %param.9) | copy-start | bytes 1540

commit v9 on v8

--- a/solution.py
+++ b/solution.py
@@ -110,7 +110,7 @@
     pairs = []
     for y in range(size):
         for j in range(owners):
-            sign = 1 if (y + j + step + chain) % 2 == 0 else -1
+            sign = 1 if (y + 1 + step + chain) % 2 == 0 else -1
             pairs.append((y * owners + j, (y + sign) % size * owners + j))
     return lax.ppermute(value, ("etp", "ep"), pairs)
 
@@ -118,7 +118,7 @@
 def columns_of(steps, width, chain):
     size = 2 * steps
     y = lax.axis_index("etp")
-    sign = 1 - 2 * lax.rem(y + lax.axis_index("ep") + chain, 2)
+    sign = 1 - 2 * lax.rem(y + 1 + chain, 2)
     out = []
     for k in range(steps):
         turn = sign if k % 2 == 0 else -sign

time: 185 us -> 181 us (0.978)
  waiting for transfers between devices: 45.3 us -> 38.1 us
  starting transfers between devices: 46.9 us -> 49.5 us
    ppermute x16, waiting for transfers between devices: 45.3 us -> 38.1 us  [exchange(): return lax.ppermute(value, ('etp', 'ep'), pairs)]
    ppermute x16, starting transfers between devices: 46.9 us -> 49.5 us  [exchange(): return lax.ppermute(value, ('etp', 'ep'), pairs)]
  transfers between devices with their start and end apart: 16 -> 16, of which waited for: 14 -> 11; matrix products, arithmetic and copies ran while one was open for 0% -> 0% of each run, Pallas kernels for 2% -> 2%
where the time goes in v9:
time: 181 us; the launch traced here: 180 us
  blocking collectives  80.9 us (45%)
  starting transfers between devices  49.5 us (27%)
  waiting for transfers between devices  38.1 us (21%)
  Pallas kernels  8.33 us (5%)
    ppermute x16, starting transfers between devices, exchange(): return lax.ppermute(value, ('etp', 'ep'), pairs)  49.5 us
    all_to_all x1, blocking collectives, on_device(): lax.all_to_all(send.reshape(owners, 2 * capacity, local_width), 'ep', spl...  41.3 us
    all_to_all x1, blocking collectives, on_device(): lax.all_to_all(unsorted.reshape(owners, 2 * capacity, local_width), 'ep',...  39.7 us
    ppermute x16, waiting for transfers between devices, exchange(): return lax.ppermute(value, ('etp', 'ep'), pairs)  38.1 us
    pallas_call x5, Pallas kernels, call(): pl.pallas_call(kernel, out_shape=shapes, in_specs=[VMEM] * len(operands),...  3.83 us
  transfers between devices with their start and end apart: 16, of which 11 were waited for; matrix products, arithmetic and copies ran while one was open for 0% of the time, Pallas kernels for 2%

profile of v9, /device:TPU:1, one launch (start us, length us, event | category | flops | bytes accessed | tf_op | source)
XLA Modules:
  0.0 180.1 jit_solution(14724531355216696869)
XLA Ops:
  0.6 2.5 %shard_map.86 = bf16[384,512]{1,0:T(8,128)(2,1)} custom-call(s32[8,16]{1,0:T(8,128)} %bitcast.31, f32[8,16]{1,0:T(8,128)} %bitcast.33, bf16[16,512]{1,0:T(8,128)(2,1)} %refs_2_.1, bf16[16,512]{1,0:T(8,128)(2,1)} %refs_3_.1), custom_call_target="tpu_custom_call" | custom-call | tf_op jit(solution)/shard_map/pallas_call | solution.py:211
  3.2 1.1 reshape.16
  4.3 41.3 %all_to_all.10 = bf16[96,4,512]{2,1,0:T(4,128)(2,1)S(1)} all-to-all(bf16[96,4,512]{2,1,0:T(4,128)(2,1)S(1)} %reshape.16), channel_id=1, replica_groups=mesh['etp'=8,'ep'=96] {'ep'}, dimensions={0} | all-to-all | bytes 786432 | tf_op jit(solution)/shard_map/all_to_all | solution.py:220
  45.6 0.1 reshape.17.refs_0_
  45.7 0.4 shard_map.87
  46.1 5.2 %collective-permute-start = (bf16[192,512]{1,0:T(8,128)(2,1)S(1)}, bf16[192,512]{1,0:T(8,128)(2,1)S(1)}, u32[]{:S(2)}, u32[]{:S(2)}) collective-permute-start(bf16[192,512]{1,0:T(8,128)(2,1)S(1)} %get-tuple-element.20), channel_id=1, source_target_pairs={{0,672},{1,673},{2,674},{3,675},{4,676},{5,677},{6,678},{7,679},{8... | collective-permute-start | bytes 589832 | tf_op jit(solution)/shard_map/ppermute | solution.py:115
  51.3 1.9 %collective-permute-start.1 = (bf16[192,512]{1,0:T(8,128)(2,1)S(1)}, bf16[192,512]{1,0:T(8,128)(2,1)S(1)}, u32[]{:S(2)}, u32[]{:S(2)}) collective-permute-start(bf16[192,512]{1,0:T(8,128)(2,1)S(1)} %get-tuple-element.21), channel_id=1, source_target_pairs={{0,96},{1,97},{2,98},{3,99},{4,100},{5,101},{6,102},{7,103},{8,104... | collective-permute-start | bytes 589832 | tf_op jit(solution)/shard_map/ppermute | solution.py:115
  53.2 1.8 collective-permute-done
  55.0 2.7 %collective-permute-done.1 = bf16[192,512]{1,0:T(8,128)(2,1)S(1)} collective-permute-done((bf16[192,512]{1,0:T(8,128)(2,1)S(1)}, bf16[192,512]{1,0:T(8,128)(2,1)S(1)}, u32[]{:S(2)}, u32[]{:S(2)}) %collective-permute-start.1) | collective-permute-done | bytes 196640 | tf_op jit(solution)/shard_map/ppermute | solution.py:115
  57.8 2.3 %collective-permute-start.2 = (bf16[2,192,512]{2,1,0:T(8,128)(2,1)S(1)}, bf16[2,192,512]{2,1,0:T(8,128)(2,1)S(1)}, u32[]{:S(2)}, u32[]{:S(2)}) collective-permute-start(bf16[2,192,512]{2,1,0:T(8,128)(2,1)S(1)} %pad_maximum_fusion.refs_0_), channel_id=1, source_target_pairs={{0,96},{1,97},{2,98},{3,99},{4,100},{5,101},{6,102},{7,103},{8,104... | collective-permute-start | bytes 1179656 | tf_op jit(solution)/shard_map/ppermute | solution.py:115
  60.1 3.7 %collective-permute-start.9 = (bf16[2,192,512]{2,1,0:T(8,128)(2,1)S(1)}, bf16[2,192,512]{2,1,0:T(8,128)(2,1)S(1)}, u32[]{:S(2)}, u32[]{:S(2)}) collective-permute-start(bf16[2,192,512]{2,1,0:T(8,128)(2,1)S(1)} %pad_maximum_fusion.1.refs_0_), channel_id=1, source_target_pairs={{0,672},{1,673},{2,674},{3,675},{4,676},{5,677},{6,678},{7,679},{8... | collective-permute-start | bytes 1179656 | tf_op jit(solution)/shard_map/ppermute | solution.py:115
  63.8 3.5 %collective-permute-done.2.refs_1_ = bf16[2,192,512]{2,1,0:T(8,128)(2,1)S(1)} collective-permute-done((bf16[2,192,512]{2,1,0:T(8,128)(2,1)S(1)}, bf16[2,192,512]{2,1,0:T(8,128)(2,1)S(1)}, u32[]{:S(2)}, u32[]{:S(2)}) %collective-permute-start.2) | collective-permute-done | bytes 393248 | tf_op jit(solution)/shard_map/ppermute | solution.py:115
  67.3 3.4 %collective-permute-start.3 = (bf16[2,192,512]{2,1,0:T(8,128)(2,1)S(1)}, bf16[2,192,512]{2,1,0:T(8,128)(2,1)S(1)}, u32[]{:S(2)}, u32[]{:S(2)}) collective-permute-start(bf16[2,192,512]{2,1,0:T(8,128)(2,1)S(1)} %collective-permute-done.2.refs_1_), channel_id=1, source_target_pairs={{0,672},{1,673},{2,674},{3,675},{4,676},{5,677},{6,678},{7,679},{8... | collective-permute-start | bytes 1179656 | tf_op jit(solution)/shard_map/ppermute | solution.py:115
  70.8 0.3 collective-permute-done.9.refs_1_
  71.1 2.7 %collective-permute-start.10 = (bf16[2,192,512]{2,1,0:T(8,128)(2,1)S(1)}, bf16[2,192,512]{2,1,0:T(8,128)(2,1)S(1)}, u32[]{:S(2)}, u32[]{:S(2)}) collective-permute-start(bf16[2,192,512]{2,1,0:T(8,128)(2,1)S(1)} %collective-permute-done.9.refs_1_), channel_id=1, source_target_pairs={{0,96},{1,97},{2,98},{3,99},{4,100},{5,101},{6,102},{7,103},{8,104... | collective-permute-start | bytes 1179656 | tf_op jit(solution)/shard_map/ppermute | solution.py:115
  73.8 5.8 %collective-permute-done.3.refs_2_ = bf16[2,192,512]{2,1,0:T(8,128)(2,1)S(1)} collective-permute-done((bf16[2,192,512]{2,1,0:T(8,128)(2,1)S(1)}, bf16[2,192,512]{2,1,0:T(8,128)(2,1)S(1)}, u32[]{:S(2)}, u32[]{:S(2)}) %collective-permute-start.3) | collective-permute-done | bytes 393248 | tf_op jit(solution)/shard_map/ppermute | solution.py:115
  79.6 3.0 %collective-permute-start.4 = (bf16[2,192,512]{2,1,0:T(8,128)(2,1)S(1)}, bf16[2,192,512]{2,1,0:T(8,128)(2,1)S(1)}, u32[]{:S(2)}, u32[]{:S(2)}) collective-permute-start(bf16[2,192,512]{2,1,0:T(8,128)(2,1)S(1)} %collective-permute-done.3.refs_2_), channel_id=1, source_target_pairs={{0,96},{1,97},{2,98},{3,99},{4,100},{5,101},{6,102},{7,103},{8,104... | collective-permute-start | bytes 1179656 | tf_op jit(solution)/shard_map/ppermute | solution.py:115
  82.7 3.2 %collective-permute-start.11 = (bf16[2,192,512]{2,1,0:T(8,128)(2,1)S(1)}, bf16[2,192,512]{2,1,0:T(8,128)(2,1)S(1)}, u32[]{:S(2)}, u32[]{:S(2)}) collective-permute-start(bf16[2,192,512]{2,1,0:T(8,128)(2,1)S(1)} %collective-permute-done.10.refs_2_), channel_id=1, source_target_pairs={{0,672},{1,673},{2,674},{3,675},{4,676},{5,677},{6,678},{7,679},{8... | collective-permute-start | bytes 1179656 | tf_op jit(solution)/shard_map/ppermute | solution.py:115
  85.9 0.8 shard_map.88
  86.7 3.7 %collective-permute-done.4.held = bf16[2,192,512]{2,1,0:T(8,128)(2,1)S(1)} collective-permute-done((bf16[2,192,512]{2,1,0:T(8,128)(2,1)S(1)}, bf16[2,192,512]{2,1,0:T(8,128)(2,1)S(1)}, u32[]{:S(2)}, u32[]{:S(2)}) %collective-permute-start.4) | collective-permute-done | bytes 393248 | tf_op jit(solution)/shard_map/ppermute | solution.py:115
  90.5 0.9 shard_map.89
  91.4 2.5 %collective-permute-start.5 = (bf16[2,192,512]{2,1,0:T(8,128)(2,1)S(1)}, bf16[2,192,512]{2,1,0:T(8,128)(2,1)S(1)}, u32[]{:S(2)}, u32[]{:S(2)}) collective-permute-start(bf16[2,192,512]{2,1,0:T(8,128)(2,1)S(1)} %get-tuple-element.28), channel_id=1, source_target_pairs={{0,96},{1,97},{2,98},{3,99},{4,100},{5,101},{6,102},{7,103},{8,104... | collective-permute-start | bytes 1179656 | tf_op jit(solution)/shard_map/ppermute | solution.py:115
  93.8 0.5 shard_map.90.grad_sum
  94.4 0.8 shard_map.91
  95.2 3.5 %collective-permute-start.12 = (bf16[2,192,512]{2,1,0:T(8,128)(2,1)S(1)}, bf16[2,192,512]{2,1,0:T(8,128)(2,1)S(1)}, u32[]{:S(2)}, u32[]{:S(2)}) collective-permute-start(bf16[2,192,512]{2,1,0:T(8,128)(2,1)S(1)} %get-tuple-element.37), channel_id=1, source_target_pairs={{0,672},{1,673},{2,674},{3,675},{4,676},{5,677},{6,678},{7,679},{8... | collective-permute-start | bytes 1179656 | tf_op jit(solution)/shard_map/ppermute | solution.py:115
  98.7 1.6 collective-permute-done.5
  100.4 0.1 add_convert_fusion.5
  100.5 4.3 %collective-permute-start.6 = (bf16[2,192,512]{2,1,0:T(8,128)(2,1)S(1)}, bf16[2,192,512]{2,1,0:T(8,128)(2,1)S(1)}, u32[]{:S(2)}, u32[]{:S(2)}) collective-permute-start(bf16[2,192,512]{2,1,0:T(8,128)(2,1)S(1)} %add_convert_fusion.5), channel_id=1, source_target_pairs={{0,672},{1,673},{2,674},{3,675},{4,676},{5,677},{6,678},{7,679},{8... | collective-permute-start | bytes 1179656 | tf_op jit(solution)/shard_map/ppermute | solution.py:115
  104.8 0.8 shard_map.92
  105.6 0.1 add_convert_fusion.2
  105.7 1.9 %collective-permute-start.13 = (bf16[2,192,512]{2,1,0:T(8,128)(2,1)S(1)}, bf16[2,192,512]{2,1,0:T(8,128)(2,1)S(1)}, u32[]{:S(2)}, u32[]{:S(2)}) collective-permute-start(bf16[2,192,512]{2,1,0:T(8,128)(2,1)S(1)} %add_convert_fusion.2), channel_id=1, source_target_pairs={{0,96},{1,97},{2,98},{3,99},{4,100},{5,101},{6,102},{7,103},{8,104... | collective-permute-start | bytes 1179656 | tf_op jit(solution)/shard_map/ppermute | solution.py:115
  107.6 7.1 %collective-permute-done.6 = bf16[2,192,512]{2,1,0:T(8,128)(2,1)S(1)} collective-permute-done((bf16[2,192,512]{2,1,0:T(8,128)(2,1)S(1)}, bf16[2,192,512]{2,1,0:T(8,128)(2,1)S(1)}, u32[]{:S(2)}, u32[]{:S(2)}) %collective-permute-start.6) | collective-permute-done | bytes 393248 | tf_op jit(solution)/shard_map/ppermute | solution.py:115
  114.7 0.1 add_convert_fusion.4
  114.9 1.9 %collective-permute-start.7 = (bf16[2,192,512]{2,1,0:T(8,128)(2,1)S(1)}, bf16[2,192,512]{2,1,0:T(8,128)(2,1)S(1)}, u32[]{:S(2)}, u32[]{:S(2)}) collective-permute-start(bf16[2,192,512]{2,1,0:T(8,128)(2,1)S(1)} %add_convert_fusion.4), channel_id=1, source_target_pairs={{0,96},{1,97},{2,98},{3,99},{4,100},{5,101},{6,102},{7,103},{8,104... | collective-permute-start | bytes 1179656 | tf_op jit(solution)/shard_map/ppermute | solution.py:115
  116.8 0.1 add_convert_fusion.1
  116.9 4.3 %collective-permute-start.14 = (bf16[2,192,512]{2,1,0:T(8,128)(2,1)S(1)}, bf16[2,192,512]{2,1,0:T(8,128)(2,1)S(1)}, u32[]{:S(2)}, u32[]{:S(2)}) collective-permute-start(bf16[2,192,512]{2,1,0:T(8,128)(2,1)S(1)} %add_convert_fusion.1), channel_id=1, source_target_pairs={{0,672},{1,673},{2,674},{3,675},{4,676},{5,677},{6,678},{7,679},{8... | collective-permute-start | bytes 1179656 | tf_op jit(solution)/shard_map/ppermute | solution.py:115
  121.2 6.7 %collective-permute-done.7 = bf16[2,192,512]{2,1,0:T(8,128)(2,1)S(1)} collective-permute-done((bf16[2,192,512]{2,1,0:T(8,128)(2,1)S(1)}, bf16[2,192,512]{2,1,0:T(8,128)(2,1)S(1)}, u32[]{:S(2)}, u32[]{:S(2)}) %collective-permute-start.7) | collective-permute-done | bytes 393248 | tf_op jit(solution)/shard_map/ppermute | solution.py:115
  127.9 0.1 add_convert_fusion.3.refs_0_
  128.1 3.6 %collective-permute-start.8 = (bf16[192,512]{1,0:T(8,128)(2,1)S(1)}, bf16[192,512]{1,0:T(8,128)(2,1)S(1)}, u32[]{:S(2)}, u32[]{:S(2)}) collective-permute-start(bf16[192,512]{1,0:T(8,128)(2,1)S(1)} %slice_bitcast_fusion.1), channel_id=1, source_target_pairs={{0,672},{1,673},{2,674},{3,675},{4,676},{5,677},{6,678},{7,679},{8... | collective-permute-start | bytes 589832 | tf_op jit(solution)/shard_map/ppermute | solution.py:115
  131.7 0.1 add_convert_fusion.refs_2_
  131.8 2.0 %collective-permute-start.15 = (bf16[192,512]{1,0:T(8,128)(2,1)S(1)}, bf16[192,512]{1,0:T(8,128)(2,1)S(1)}, u32[]{:S(2)}, u32[]{:S(2)}) collective-permute-start(bf16[192,512]{1,0:T(8,128)(2,1)S(1)} %slice_bitcast_fusion), channel_id=1, source_target_pairs={{0,96},{1,97},{2,98},{3,99},{4,100},{5,101},{6,102},{7,103},{8,104... | collective-permute-start | bytes 589832 | tf_op jit(solution)/shard_map/ppermute | solution.py:115
  133.8 4.4 %collective-permute-done.8.refs_1_ = bf16[192,512]{1,0:T(8,128)(2,1)S(1)} collective-permute-done((bf16[192,512]{1,0:T(8,128)(2,1)S(1)}, bf16[192,512]{1,0:T(8,128)(2,1)S(1)}, u32[]{:S(2)}, u32[]{:S(2)}) %collective-permute-start.8) | collective-permute-done | bytes 196640 | tf_op jit(solution)/shard_map/ppermute | solution.py:115
  138.2 0.4 collective-permute-done.15.refs_3_
  138.5 0.4 shard_map.93
  139.0 0.1 reshape.18
  139.1 39.7 %all_to_all.11 = bf16[96,4,512]{2,1,0:T(4,128)(2,1)S(1)} all-to-all(bf16[96,4,512]{2,1,0:T(4,128)(2,1)S(1)} %reshape.18), channel_id=1, replica_groups=mesh['etp'=8,'ep'=96] {'ep'}, dimensions={0} | all-to-all | bytes 786432 | tf_op jit(solution)/shard_map/all_to_all | solution.py:285
  178.7 0.1 reshape.19.refs_2_
  178.8 1.2 shard_map.94
  (19 shorter events, 0.1 us)
Async XLA Ops:
  0.6 45.0 %copy-start.2 = (bf16[1,192,4096]{2,1,0:T(8,128)(2,1)S(1)}, bf16[1,192,4096]{2,1,0:T(8,128)(2,1)}, u32[]{:S(2)}) copy-start(bf16[1,192,4096]{2,1,0:T(8,128)(2,1)} %param.13) | copy-start | bytes 4718596
  45.7 40.3 %copy-start = (bf16[1,4096,192]{1,2,0:T(8,128)(2,1)S(1)}, bf16[1,4096,192]{1,2,0:T(8,128)(2,1)}, u32[]{:S(2)}) copy-start(bf16[1,4096,192]{1,2,0:T(8,128)(2,1)} %param.11) | copy-start | bytes 4718596
  45.7 40.2 %copy-start.1 = (bf16[1,4096,192]{1,2,0:T(8,128)(2,1)S(1)}, bf16[1,4096,192]{1,2,0:T(8,128)(2,1)}, u32[]{:S(2)}) copy-start(bf16[1,4096,192]{1,2,0:T(8,128)(2,1)} %param.12) | copy-start | bytes 4718596
  46.1 8.9 %collective-permute-start = (bf16[192,512]{1,0:T(8,128)(2,1)S(1)}, bf16[192,512]{1,0:T(8,128)(2,1)S(1)}, u32[]{:S(2)}, u32[]{:S(2)}) collective-permute-start(bf16[192,512]{1,0:T(8,128)(2,1)S(1)} %get-tuple-element.20), channel_id=1, source_target_pairs={{0,672},{1,673},{2,674},{3,675},{4,676},{5,677},{6,678},{7,679},{8... | collective-permute-start | bytes 589832 | tf_op jit(solution)/shard_map/ppermute | solution.py:115
  51.3 6.4 %collective-permute-start.1 = (bf16[192,512]{1,0:T(8,128)(2,1)S(1)}, bf16[192,512]{1,0:T(8,128)(2,1)S(1)}, u32[]{:S(2)}, u32[]{:S(2)}) collective-permute-start(bf16[192,512]{1,0:T(8,128)(2,1)S(1)} %get-tuple-element.21), channel_id=1, source_target_pairs={{0,96},{1,97},{2,98},{3,99},{4,100},{5,101},{6,102},{7,103},{8,104... | collective-permute-start | bytes 589832 | tf_op jit(solution)/shard_map/ppermute | solution.py:115
  57.8 9.6 %collective-permute-start.2 = (bf16[2,192,512]{2,1,0:T(8,128)(2,1)S(1)}, bf16[2,192,512]{2,1,0:T(8,128)(2,1)S(1)}, u32[]{:S(2)}, u32[]{:S(2)}) collective-permute-start(bf16[2,192,512]{2,1,0:T(8,128)(2,1)S(1)} %pad_maximum_fusion.refs_0_), channel_id=1, source_target_pairs={{0,96},{1,97},{2,98},{3,99},{4,100},{5,101},{6,102},{7,103},{8,104... | collective-permute-start | bytes 1179656 | tf_op jit(solution)/shard_map/ppermute | solution.py:115
  60.1 11.0 %collective-permute-start.9 = (bf16[2,192,512]{2,1,0:T(8,128)(2,1)S(1)}, bf16[2,192,512]{2,1,0:T(8,128)(2,1)S(1)}, u32[]{:S(2)}, u32[]{:S(2)}) collective-permute-start(bf16[2,192,512]{2,1,0:T(8,128)(2,1)S(1)} %pad_maximum_fusion.1.refs_0_), channel_id=1, source_target_pairs={{0,672},{1,673},{2,674},{3,675},{4,676},{5,677},{6,678},{7,679},{8... | collective-permute-start | bytes 1179656 | tf_op jit(solution)/shard_map/ppermute | solution.py:115
  67.3 12.3 %collective-permute-start.3 = (bf16[2,192,512]{2,1,0:T(8,128)(2,1)S(1)}, bf16[2,192,512]{2,1,0:T(8,128)(2,1)S(1)}, u32[]{:S(2)}, u32[]{:S(2)}) collective-permute-start(bf16[2,192,512]{2,1,0:T(8,128)(2,1)S(1)} %collective-permute-done.2.refs_1_), channel_id=1, source_target_pairs={{0,672},{1,673},{2,674},{3,675},{4,676},{5,677},{6,678},{7,679},{8... | collective-permute-start | bytes 1179656 | tf_op jit(solution)/shard_map/ppermute | solution.py:115
  71.1 11.6 %collective-permute-start.10 = (bf16[2,192,512]{2,1,0:T(8,128)(2,1)S(1)}, bf16[2,192,512]{2,1,0:T(8,128)(2,1)S(1)}, u32[]{:S(2)}, u32[]{:S(2)}) collective-permute-start(bf16[2,192,512]{2,1,0:T(8,128)(2,1)S(1)} %collective-permute-done.9.refs_1_), channel_id=1, source_target_pairs={{0,96},{1,97},{2,98},{3,99},{4,100},{5,101},{6,102},{7,103},{8,104... | collective-permute-start | bytes 1179656 | tf_op jit(solution)/shard_map/ppermute | solution.py:115
  79.6 10.9 %collective-permute-start.4 = (bf16[2,192,512]{2,1,0:T(8,128)(2,1)S(1)}, bf16[2,192,512]{2,1,0:T(8,128)(2,1)S(1)}, u32[]{:S(2)}, u32[]{:S(2)}) collective-permute-start(bf16[2,192,512]{2,1,0:T(8,128)(2,1)S(1)} %collective-permute-done.3.refs_2_), channel_id=1, source_target_pairs={{0,96},{1,97},{2,98},{3,99},{4,100},{5,101},{6,102},{7,103},{8,104... | collective-permute-start | bytes 1179656 | tf_op jit(solution)/shard_map/ppermute | solution.py:115
  82.7 11.7 %collective-permute-start.11 = (bf16[2,192,512]{2,1,0:T(8,128)(2,1)S(1)}, bf16[2,192,512]{2,1,0:T(8,128)(2,1)S(1)}, u32[]{:S(2)}, u32[]{:S(2)}) collective-permute-start(bf16[2,192,512]{2,1,0:T(8,128)(2,1)S(1)} %collective-permute-done.10.refs_2_), channel_id=1, source_target_pairs={{0,672},{1,673},{2,674},{3,675},{4,676},{5,677},{6,678},{7,679},{8... | collective-permute-start | bytes 1179656 | tf_op jit(solution)/shard_map/ppermute | solution.py:115
  91.4 9.0 %collective-permute-start.5 = (bf16[2,192,512]{2,1,0:T(8,128)(2,1)S(1)}, bf16[2,192,512]{2,1,0:T(8,128)(2,1)S(1)}, u32[]{:S(2)}, u32[]{:S(2)}) collective-permute-start(bf16[2,192,512]{2,1,0:T(8,128)(2,1)S(1)} %get-tuple-element.28), channel_id=1, source_target_pairs={{0,96},{1,97},{2,98},{3,99},{4,100},{5,101},{6,102},{7,103},{8,104... | collective-permute-start | bytes 1179656 | tf_op jit(solution)/shard_map/ppermute | solution.py:115
  95.2 10.4 %collective-permute-start.12 = (bf16[2,192,512]{2,1,0:T(8,128)(2,1)S(1)}, bf16[2,192,512]{2,1,0:T(8,128)(2,1)S(1)}, u32[]{:S(2)}, u32[]{:S(2)}) collective-permute-start(bf16[2,192,512]{2,1,0:T(8,128)(2,1)S(1)} %get-tuple-element.37), channel_id=1, source_target_pairs={{0,672},{1,673},{2,674},{3,675},{4,676},{5,677},{6,678},{7,679},{8... | collective-permute-start | bytes 1179656 | tf_op jit(solution)/shard_map/ppermute | solution.py:115
  100.5 14.3 %collective-permute-start.6 = (bf16[2,192,512]{2,1,0:T(8,128)(2,1)S(1)}, bf16[2,192,512]{2,1,0:T(8,128)(2,1)S(1)}, u32[]{:S(2)}, u32[]{:S(2)}) collective-permute-start(bf16[2,192,512]{2,1,0:T(8,128)(2,1)S(1)} %add_convert_fusion.5), channel_id=1, source_target_pairs={{0,672},{1,673},{2,674},{3,675},{4,676},{5,677},{6,678},{7,679},{8... | collective-permute-start | bytes 1179656 | tf_op jit(solution)/shard_map/ppermute | solution.py:115
  105.7 11.1 %collective-permute-start.13 = (bf16[2,192,512]{2,1,0:T(8,128)(2,1)S(1)}, bf16[2,192,512]{2,1,0:T(8,128)(2,1)S(1)}, u32[]{:S(2)}, u32[]{:S(2)}) collective-permute-start(bf16[2,192,512]{2,1,0:T(8,128)(2,1)S(1)} %add_convert_fusion.2), channel_id=1, source_target_pairs={{0,96},{1,97},{2,98},{3,99},{4,100},{5,101},{6,102},{7,103},{8,104... | collective-permute-start | bytes 1179656 | tf_op jit(solution)/shard_map/ppermute | solution.py:115
  114.9 13.1 %collective-permute-start.7 = (bf16[2,192,512]{2,1,0:T(8,128)(2,1)S(1)}, bf16[2,192,512]{2,1,0:T(8,128)(2,1)S(1)}, u32[]{:S(2)}, u32[]{:S(2)}) collective-permute-start(bf16[2,192,512]{2,1,0:T(8,128)(2,1)S(1)} %add_convert_fusion.4), channel_id=1, source_target_pairs={{0,96},{1,97},{2,98},{3,99},{4,100},{5,101},{6,102},{7,103},{8,104... | collective-permute-start | bytes 1179656 | tf_op jit(solution)/shard_map/ppermute | solution.py:115
  116.9 14.7 %collective-permute-start.14 = (bf16[2,192,512]{2,1,0:T(8,128)(2,1)S(1)}, bf16[2,192,512]{2,1,0:T(8,128)(2,1)S(1)}, u32[]{:S(2)}, u32[]{:S(2)}) collective-permute-start(bf16[2,192,512]{2,1,0:T(8,128)(2,1)S(1)} %add_convert_fusion.1), channel_id=1, source_target_pairs={{0,672},{1,673},{2,674},{3,675},{4,676},{5,677},{6,678},{7,679},{8... | collective-permute-start | bytes 1179656 | tf_op jit(solution)/shard_map/ppermute | solution.py:115
  128.1 10.1 %collective-permute-start.8 = (bf16[192,512]{1,0:T(8,128)(2,1)S(1)}, bf16[192,512]{1,0:T(8,128)(2,1)S(1)}, u32[]{:S(2)}, u32[]{:S(2)}) collective-permute-start(bf16[192,512]{1,0:T(8,128)(2,1)S(1)} %slice_bitcast_fusion.1), channel_id=1, source_target_pairs={{0,672},{1,673},{2,674},{3,675},{4,676},{5,677},{6,678},{7,679},{8... | collective-permute-start | bytes 589832 | tf_op jit(solution)/shard_map/ppermute | solution.py:115
  131.8 6.7 %collective-permute-start.15 = (bf16[192,512]{1,0:T(8,128)(2,1)S(1)}, bf16[192,512]{1,0:T(8,128)(2,1)S(1)}, u32[]{:S(2)}, u32[]{:S(2)}) collective-permute-start(bf16[192,512]{1,0:T(8,128)(2,1)S(1)} %slice_bitcast_fusion), channel_id=1, source_target_pairs={{0,96},{1,97},{2,98},{3,99},{4,100},{5,101},{6,102},{7,103},{8,104... | collective-permute-start | bytes 589832 | tf_op jit(solution)/shard_map/ppermute | solution.py:115
  138.9 39.9 %copy-start.3 = (s32[16,8]{0,1:T(8,128)S(1)}, s32[16,8]{0,1:T(8,128)}, u32[]{:S(2)}) copy-start(s32[16,8]{0,1:T(8,128)} %param.8) | copy-start | bytes 1540
  139.0 39.9 %copy-start.4 = (f32[16,8]{0,1:T(8,128)S(1)}, f32[16,8]{0,1:T(8,128)}, u32[]{:S(2)}) copy-start(f32[16,8]{0,1:T(8,128)} %param.9) | copy-start | bytes 1540

commit v10 on v9

--- a/solution.py
+++ b/solution.py
@@ -228,8 +228,8 @@
         out_specs=[VMEM] * 2,
         compiler_params=pltpu.CompilerParams(vmem_limit_bytes=VMEM_LIMIT),
     )(recv, w_down[0])
-    token_next, grad_next = lax.optimization_barrier(
-        (exchange(token_rows, 0, 0), exchange(grad_rows, 0, 1))
+    grad_next, token_next = lax.optimization_barrier(
+        (exchange(grad_rows, 0, 1), exchange(token_rows, 0, 0))
     )
     token_held = [jnp.stack([token_rows, token_next])]
     grad_held = [jnp.stack([grad_rows, grad_next])]

time: 181 us -> 177 us (0.978)
  starting transfers between devices: 49.5 us -> 55.3 us
  blocking collectives: 80.9 us -> 75.7 us
  waiting for transfers between devices: 38.1 us -> 33.6 us
    ppermute x16, starting transfers between devices: 49.5 us -> 55.3 us  [exchange(): return lax.ppermute(value, ('etp', 'ep'), pairs)]
    all_to_all x1, blocking collectives: 39.7 us -> 34.4 us  [on_device(): lax.all_to_all(unsorted.reshape(owners, 2 * capacity, local_width), 'ep',...]
    ppermute x16, waiting for transfers between devices: 38.1 us -> 33.6 us  [exchange(): return lax.ppermute(value, ('etp', 'ep'), pairs)]
  transfers between devices with their start and end apart: 16 -> 16, of which waited for: 11 -> 10; matrix products, arithmetic and copies ran while one was open for 0% -> 0% of each run, Pallas kernels for 2% -> 2%
where the time goes in v10:
time: 177 us; the launch traced here: 176 us
  blocking collectives  75.7 us (43%)
  starting transfers between devices  55.3 us (31%)
  waiting for transfers between devices  33.6 us (19%)
  Pallas kernels  8.33 us (5%)
    ppermute x16, starting transfers between devices, exchange(): return lax.ppermute(value, ('etp', 'ep'), pairs)  55.3 us
    all_to_all x1, blocking collectives, on_device(): lax.all_to_all(send.reshape(owners, 2 * capacity, local_width), 'ep', spl...  41.3 us
    all_to_all x1, blocking collectives, on_device(): lax.all_to_all(unsorted.reshape(owners, 2 * capacity, local_width), 'ep',...  34.4 us
    ppermute x16, waiting for transfers between devices, exchange(): return lax.ppermute(value, ('etp', 'ep'), pairs)  33.6 us
    pallas_call x5, Pallas kernels, call(): pl.pallas_call(kernel, out_shape=shapes, in_specs=[VMEM] * len(operands),...  3.82 us
  transfers between devices with their start and end apart: 16, of which 10 were waited for; matrix products, arithmetic and copies ran while one was open for 0% of the time, Pallas kernels for 2%

profile of v10, /device:TPU:1, one launch (start us, length us, event | category | flops | bytes accessed | tf_op | source)
XLA Modules:
  0.0 176.2 jit_solution(5278899223899080419)
XLA Ops:
  0.6 2.5 %shard_map.86 = bf16[384,512]{1,0:T(8,128)(2,1)} custom-call(s32[8,16]{1,0:T(8,128)} %bitcast.31, f32[8,16]{1,0:T(8,128)} %bitcast.33, bf16[16,512]{1,0:T(8,128)(2,1)} %refs_2_.1, bf16[16,512]{1,0:T(8,128)(2,1)} %refs_3_.1), custom_call_target="tpu_custom_call" | custom-call | tf_op jit(solution)/shard_map/pallas_call | solution.py:211
  3.2 1.1 reshape.16
  4.3 41.3 %all_to_all.10 = bf16[96,4,512]{2,1,0:T(4,128)(2,1)S(1)} all-to-all(bf16[96,4,512]{2,1,0:T(4,128)(2,1)S(1)} %reshape.16), channel_id=1, replica_groups=mesh['etp'=8,'ep'=96] {'ep'}, dimensions={0} | all-to-all | bytes 786432 | tf_op jit(solution)/shard_map/all_to_all | solution.py:220
  45.6 0.1 reshape.17.refs_0_
  45.7 0.0 copy-start.1
  45.7 0.4 shard_map.87
  46.1 3.3 %collective-permute-start = (bf16[192,512]{1,0:T(8,128)(2,1)S(1)}, bf16[192,512]{1,0:T(8,128)(2,1)S(1)}, u32[]{:S(2)}, u32[]{:S(2)}) collective-permute-start(bf16[192,512]{1,0:T(8,128)(2,1)S(1)} %get-tuple-element.21), channel_id=1, source_target_pairs={{0,96},{1,97},{2,98},{3,99},{4,100},{5,101},{6,102},{7,103},{8,104... | collective-permute-start | bytes 589832 | tf_op jit(solution)/shard_map/ppermute | solution.py:115
  49.4 4.9 %collective-permute-start.1 = (bf16[192,512]{1,0:T(8,128)(2,1)S(1)}, bf16[192,512]{1,0:T(8,128)(2,1)S(1)}, u32[]{:S(2)}, u32[]{:S(2)}) collective-permute-start(bf16[192,512]{1,0:T(8,128)(2,1)S(1)} %get-tuple-element.20), channel_id=1, source_target_pairs={{0,672},{1,673},{2,674},{3,675},{4,676},{5,677},{6,678},{7,679},{8... | collective-permute-start | bytes 589832 | tf_op jit(solution)/shard_map/ppermute | solution.py:115
  54.3 3.4 %collective-permute-done.1 = bf16[192,512]{1,0:T(8,128)(2,1)S(1)} collective-permute-done((bf16[192,512]{1,0:T(8,128)(2,1)S(1)}, bf16[192,512]{1,0:T(8,128)(2,1)S(1)}, u32[]{:S(2)}, u32[]{:S(2)}) %collective-permute-start.1) | collective-permute-done | bytes 196640 | tf_op jit(solution)/shard_map/ppermute | solution.py:115
  57.7 1.9 %collective-permute-start.2 = (bf16[2,192,512]{2,1,0:T(8,128)(2,1)S(1)}, bf16[2,192,512]{2,1,0:T(8,128)(2,1)S(1)}, u32[]{:S(2)}, u32[]{:S(2)}) collective-permute-start(bf16[2,192,512]{2,1,0:T(8,128)(2,1)S(1)} %pad_maximum_fusion.refs_0_), channel_id=1, source_target_pairs={{0,96},{1,97},{2,98},{3,99},{4,100},{5,101},{6,102},{7,103},{8,104... | collective-permute-start | bytes 1179656 | tf_op jit(solution)/shard_map/ppermute | solution.py:115
  59.7 4.2 %collective-permute-start.9 = (bf16[2,192,512]{2,1,0:T(8,128)(2,1)S(1)}, bf16[2,192,512]{2,1,0:T(8,128)(2,1)S(1)}, u32[]{:S(2)}, u32[]{:S(2)}) collective-permute-start(bf16[2,192,512]{2,1,0:T(8,128)(2,1)S(1)} %pad_maximum_fusion.1.refs_0_), channel_id=1, source_target_pairs={{0,672},{1,673},{2,674},{3,675},{4,676},{5,677},{6,678},{7,679},{8... | collective-permute-start | bytes 1179656 | tf_op jit(solution)/shard_map/ppermute | solution.py:115
  63.9 3.9 %collective-permute-done.2.refs_1_ = bf16[2,192,512]{2,1,0:T(8,128)(2,1)S(1)} collective-permute-done((bf16[2,192,512]{2,1,0:T(8,128)(2,1)S(1)}, bf16[2,192,512]{2,1,0:T(8,128)(2,1)S(1)}, u32[]{:S(2)}, u32[]{:S(2)}) %collective-permute-start.2) | collective-permute-done | bytes 393248 | tf_op jit(solution)/shard_map/ppermute | solution.py:115
  67.8 3.7 %collective-permute-start.3 = (bf16[2,192,512]{2,1,0:T(8,128)(2,1)S(1)}, bf16[2,192,512]{2,1,0:T(8,128)(2,1)S(1)}, u32[]{:S(2)}, u32[]{:S(2)}) collective-permute-start(bf16[2,192,512]{2,1,0:T(8,128)(2,1)S(1)} %collective-permute-done.2.refs_1_), channel_id=1, source_target_pairs={{0,672},{1,673},{2,674},{3,675},{4,676},{5,677},{6,678},{7,679},{8... | collective-permute-start | bytes 1179656 | tf_op jit(solution)/shard_map/ppermute | solution.py:115
  71.5 1.9 %collective-permute-start.10 = (bf16[2,192,512]{2,1,0:T(8,128)(2,1)S(1)}, bf16[2,192,512]{2,1,0:T(8,128)(2,1)S(1)}, u32[]{:S(2)}, u32[]{:S(2)}) collective-permute-start(bf16[2,192,512]{2,1,0:T(8,128)(2,1)S(1)} %collective-permute-done.9.refs_1_), channel_id=1, source_target_pairs={{0,96},{1,97},{2,98},{3,99},{4,100},{5,101},{6,102},{7,103},{8,104... | collective-permute-start | bytes 1179656 | tf_op jit(solution)/shard_map/ppermute | solution.py:115
  73.4 5.4 %collective-permute-done.3.refs_2_ = bf16[2,192,512]{2,1,0:T(8,128)(2,1)S(1)} collective-permute-done((bf16[2,192,512]{2,1,0:T(8,128)(2,1)S(1)}, bf16[2,192,512]{2,1,0:T(8,128)(2,1)S(1)}, u32[]{:S(2)}, u32[]{:S(2)}) %collective-permute-start.3) | collective-permute-done | bytes 393248 | tf_op jit(solution)/shard_map/ppermute | solution.py:115
  78.8 3.6 %collective-permute-start.4 = (bf16[2,192,512]{2,1,0:T(8,128)(2,1)S(1)}, bf16[2,192,512]{2,1,0:T(8,128)(2,1)S(1)}, u32[]{:S(2)}, u32[]{:S(2)}) collective-permute-start(bf16[2,192,512]{2,1,0:T(8,128)(2,1)S(1)} %collective-permute-done.3.refs_2_), channel_id=1, source_target_pairs={{0,96},{1,97},{2,98},{3,99},{4,100},{5,101},{6,102},{7,103},{8,104... | collective-permute-start | bytes 1179656 | tf_op jit(solution)/shard_map/ppermute | solution.py:115
  82.4 4.2 %collective-permute-start.11 = (bf16[2,192,512]{2,1,0:T(8,128)(2,1)S(1)}, bf16[2,192,512]{2,1,0:T(8,128)(2,1)S(1)}, u32[]{:S(2)}, u32[]{:S(2)}) collective-permute-start(bf16[2,192,512]{2,1,0:T(8,128)(2,1)S(1)} %collective-permute-done.10.refs_2_), channel_id=1, source_target_pairs={{0,672},{1,673},{2,674},{3,675},{4,676},{5,677},{6,678},{7,679},{8... | collective-permute-start | bytes 1179656 | tf_op jit(solution)/shard_map/ppermute | solution.py:115
  86.7 0.8 shard_map.88
  87.5 2.9 %collective-permute-done.4.held = bf16[2,192,512]{2,1,0:T(8,128)(2,1)S(1)} collective-permute-done((bf16[2,192,512]{2,1,0:T(8,128)(2,1)S(1)}, bf16[2,192,512]{2,1,0:T(8,128)(2,1)S(1)}, u32[]{:S(2)}, u32[]{:S(2)}) %collective-permute-start.4) | collective-permute-done | bytes 393248 | tf_op jit(solution)/shard_map/ppermute | solution.py:115
  90.4 0.9 shard_map.89
  91.3 2.4 %collective-permute-start.5 = (bf16[2,192,512]{2,1,0:T(8,128)(2,1)S(1)}, bf16[2,192,512]{2,1,0:T(8,128)(2,1)S(1)}, u32[]{:S(2)}, u32[]{:S(2)}) collective-permute-start(bf16[2,192,512]{2,1,0:T(8,128)(2,1)S(1)} %get-tuple-element.28), channel_id=1, source_target_pairs={{0,96},{1,97},{2,98},{3,99},{4,100},{5,101},{6,102},{7,103},{8,104... | collective-permute-start | bytes 1179656 | tf_op jit(solution)/shard_map/ppermute | solution.py:115
  93.7 0.5 shard_map.90.grad_sum
  94.2 0.8 shard_map.91
  95.1 5.2 %collective-permute-start.12 = (bf16[2,192,512]{2,1,0:T(8,128)(2,1)S(1)}, bf16[2,192,512]{2,1,0:T(8,128)(2,1)S(1)}, u32[]{:S(2)}, u32[]{:S(2)}) collective-permute-start(bf16[2,192,512]{2,1,0:T(8,128)(2,1)S(1)} %get-tuple-element.37), channel_id=1, source_target_pairs={{0,672},{1,673},{2,674},{3,675},{4,676},{5,677},{6,678},{7,679},{8... | collective-permute-start | bytes 1179656 | tf_op jit(solution)/shard_map/ppermute | solution.py:115
  100.3 0.2 collective-permute-done.5
  100.5 0.1 add_convert_fusion.5
  100.6 4.8 %collective-permute-start.6 = (bf16[2,192,512]{2,1,0:T(8,128)(2,1)S(1)}, bf16[2,192,512]{2,1,0:T(8,128)(2,1)S(1)}, u32[]{:S(2)}, u32[]{:S(2)}) collective-permute-start(bf16[2,192,512]{2,1,0:T(8,128)(2,1)S(1)} %add_convert_fusion.5), channel_id=1, source_target_pairs={{0,672},{1,673},{2,674},{3,675},{4,676},{5,677},{6,678},{7,679},{8... | collective-permute-start | bytes 1179656 | tf_op jit(solution)/shard_map/ppermute | solution.py:115
  105.4 0.8 shard_map.92
  106.2 0.3 collective-permute-done.12
  106.6 0.1 add_convert_fusion.2
  106.7 2.1 %collective-permute-start.13 = (bf16[2,192,512]{2,1,0:T(8,128)(2,1)S(1)}, bf16[2,192,512]{2,1,0:T(8,128)(2,1)S(1)}, u32[]{:S(2)}, u32[]{:S(2)}) collective-permute-start(bf16[2,192,512]{2,1,0:T(8,128)(2,1)S(1)} %add_convert_fusion.2), channel_id=1, source_target_pairs={{0,96},{1,97},{2,98},{3,99},{4,100},{5,101},{6,102},{7,103},{8,104... | collective-permute-start | bytes 1179656 | tf_op jit(solution)/shard_map/ppermute | solution.py:115
  108.8 6.4 %collective-permute-done.6 = bf16[2,192,512]{2,1,0:T(8,128)(2,1)S(1)} collective-permute-done((bf16[2,192,512]{2,1,0:T(8,128)(2,1)S(1)}, bf16[2,192,512]{2,1,0:T(8,128)(2,1)S(1)}, u32[]{:S(2)}, u32[]{:S(2)}) %collective-permute-start.6) | collective-permute-done | bytes 393248 | tf_op jit(solution)/shard_map/ppermute | solution.py:115
  115.2 0.1 add_convert_fusion.4
  115.3 2.4 %collective-permute-start.7 = (bf16[2,192,512]{2,1,0:T(8,128)(2,1)S(1)}, bf16[2,192,512]{2,1,0:T(8,128)(2,1)S(1)}, u32[]{:S(2)}, u32[]{:S(2)}) collective-permute-start(bf16[2,192,512]{2,1,0:T(8,128)(2,1)S(1)} %add_convert_fusion.4), channel_id=1, source_target_pairs={{0,96},{1,97},{2,98},{3,99},{4,100},{5,101},{6,102},{7,103},{8,104... | collective-permute-start | bytes 1179656 | tf_op jit(solution)/shard_map/ppermute | solution.py:115
  117.7 0.1 add_convert_fusion.1
  117.8 4.1 %collective-permute-start.14 = (bf16[2,192,512]{2,1,0:T(8,128)(2,1)S(1)}, bf16[2,192,512]{2,1,0:T(8,128)(2,1)S(1)}, u32[]{:S(2)}, u32[]{:S(2)}) collective-permute-start(bf16[2,192,512]{2,1,0:T(8,128)(2,1)S(1)} %add_convert_fusion.1), channel_id=1, source_target_pairs={{0,672},{1,673},{2,674},{3,675},{4,676},{5,677},{6,678},{7,679},{8... | collective-permute-start | bytes 1179656 | tf_op jit(solution)/shard_map/ppermute | solution.py:115
  121.9 6.4 %collective-permute-done.7 = bf16[2,192,512]{2,1,0:T(8,128)(2,1)S(1)} collective-permute-done((bf16[2,192,512]{2,1,0:T(8,128)(2,1)S(1)}, bf16[2,192,512]{2,1,0:T(8,128)(2,1)S(1)}, u32[]{:S(2)}, u32[]{:S(2)}) %collective-permute-start.7) | collective-permute-done | bytes 393248 | tf_op jit(solution)/shard_map/ppermute | solution.py:115
  128.3 0.1 add_convert_fusion.3.refs_0_
  128.5 4.6 %collective-permute-start.8 = (bf16[192,512]{1,0:T(8,128)(2,1)S(1)}, bf16[192,512]{1,0:T(8,128)(2,1)S(1)}, u32[]{:S(2)}, u32[]{:S(2)}) collective-permute-start(bf16[192,512]{1,0:T(8,128)(2,1)S(1)} %slice_bitcast_fusion.1), channel_id=1, source_target_pairs={{0,672},{1,673},{2,674},{3,675},{4,676},{5,677},{6,678},{7,679},{8... | collective-permute-start | bytes 589832 | tf_op jit(solution)/shard_map/ppermute | solution.py:115
  133.1 0.1 add_convert_fusion.refs_2_
  133.2 1.9 %collective-permute-start.15 = (bf16[192,512]{1,0:T(8,128)(2,1)S(1)}, bf16[192,512]{1,0:T(8,128)(2,1)S(1)}, u32[]{:S(2)}, u32[]{:S(2)}) collective-permute-start(bf16[192,512]{1,0:T(8,128)(2,1)S(1)} %slice_bitcast_fusion), channel_id=1, source_target_pairs={{0,96},{1,97},{2,98},{3,99},{4,100},{5,101},{6,102},{7,103},{8,104... | collective-permute-start | bytes 589832 | tf_op jit(solution)/shard_map/ppermute | solution.py:115
  135.1 3.4 %collective-permute-done.8.refs_1_ = bf16[192,512]{1,0:T(8,128)(2,1)S(1)} collective-permute-done((bf16[192,512]{1,0:T(8,128)(2,1)S(1)}, bf16[192,512]{1,0:T(8,128)(2,1)S(1)}, u32[]{:S(2)}, u32[]{:S(2)}) %collective-permute-start.8) | collective-permute-done | bytes 196640 | tf_op jit(solution)/shard_map/ppermute | solution.py:115
  138.5 1.4 collective-permute-done.15.refs_3_
  139.9 0.4 shard_map.93
  140.3 0.1 reshape.18
  140.4 34.4 %all_to_all.11 = bf16[96,4,512]{2,1,0:T(4,128)(2,1)S(1)} all-to-all(bf16[96,4,512]{2,1,0:T(4,128)(2,1)S(1)} %reshape.18), channel_id=1, replica_groups=mesh['etp'=8,'ep'=96] {'ep'}, dimensions={0} | all-to-all | bytes 786432 | tf_op jit(solution)/shard_map/all_to_all | solution.py:285
  174.9 0.1 reshape.19.refs_2_
  175.0 1.2 shard_map.94
  (19 shorter events, 0.1 us)
Async XLA Ops:
  0.6 45.0 %copy-start.2 = (bf16[1,192,4096]{2,1,0:T(8,128)(2,1)S(1)}, bf16[1,192,4096]{2,1,0:T(8,128)(2,1)}, u32[]{:S(2)}) copy-start(bf16[1,192,4096]{2,1,0:T(8,128)(2,1)} %param.13) | copy-start | bytes 4718596
  45.7 41.0 %copy-start = (bf16[1,4096,192]{1,2,0:T(8,128)(2,1)S(1)}, bf16[1,4096,192]{1,2,0:T(8,128)(2,1)}, u32[]{:S(2)}) copy-start(bf16[1,4096,192]{1,2,0:T(8,128)(2,1)} %param.11) | copy-start | bytes 4718596
  45.7 41.0 %copy-start.1 = (bf16[1,4096,192]{1,2,0:T(8,128)(2,1)S(1)}, bf16[1,4096,192]{1,2,0:T(8,128)(2,1)}, u32[]{:S(2)}) copy-start(bf16[1,4096,192]{1,2,0:T(8,128)(2,1)} %param.12) | copy-start | bytes 4718596
  46.1 8.2 %collective-permute-start = (bf16[192,512]{1,0:T(8,128)(2,1)S(1)}, bf16[192,512]{1,0:T(8,128)(2,1)S(1)}, u32[]{:S(2)}, u32[]{:S(2)}) collective-permute-start(bf16[192,512]{1,0:T(8,128)(2,1)S(1)} %get-tuple-element.21), channel_id=1, source_target_pairs={{0,96},{1,97},{2,98},{3,99},{4,100},{5,101},{6,102},{7,103},{8,104... | collective-permute-start | bytes 589832 | tf_op jit(solution)/shard_map/ppermute | solution.py:115
  49.4 8.3 %collective-permute-start.1 = (bf16[192,512]{1,0:T(8,128)(2,1)S(1)}, bf16[192,512]{1,0:T(8,128)(2,1)S(1)}, u32[]{:S(2)}, u32[]{:S(2)}) collective-permute-start(bf16[192,512]{1,0:T(8,128)(2,1)S(1)} %get-tuple-element.20), channel_id=1, source_target_pairs={{0,672},{1,673},{2,674},{3,675},{4,676},{5,677},{6,678},{7,679},{8... | collective-permute-start | bytes 589832 | tf_op jit(solution)/shard_map/ppermute | solution.py:115
  57.7 10.1 %collective-permute-start.2 = (bf16[2,192,512]{2,1,0:T(8,128)(2,1)S(1)}, bf16[2,192,512]{2,1,0:T(8,128)(2,1)S(1)}, u32[]{:S(2)}, u32[]{:S(2)}) collective-permute-start(bf16[2,192,512]{2,1,0:T(8,128)(2,1)S(1)} %pad_maximum_fusion.refs_0_), channel_id=1, source_target_pairs={{0,96},{1,97},{2,98},{3,99},{4,100},{5,101},{6,102},{7,103},{8,104... | collective-permute-start | bytes 1179656 | tf_op jit(solution)/shard_map/ppermute | solution.py:115
  59.7 11.8 %collective-permute-start.9 = (bf16[2,192,512]{2,1,0:T(8,128)(2,1)S(1)}, bf16[2,192,512]{2,1,0:T(8,128)(2,1)S(1)}, u32[]{:S(2)}, u32[]{:S(2)}) collective-permute-start(bf16[2,192,512]{2,1,0:T(8,128)(2,1)S(1)} %pad_maximum_fusion.1.refs_0_), channel_id=1, source_target_pairs={{0,672},{1,673},{2,674},{3,675},{4,676},{5,677},{6,678},{7,679},{8... | collective-permute-start | bytes 1179656 | tf_op jit(solution)/shard_map/ppermute | solution.py:115
  67.8 11.0 %collective-permute-start.3 = (bf16[2,192,512]{2,1,0:T(8,128)(2,1)S(1)}, bf16[2,192,512]{2,1,0:T(8,128)(2,1)S(1)}, u32[]{:S(2)}, u32[]{:S(2)}) collective-permute-start(bf16[2,192,512]{2,1,0:T(8,128)(2,1)S(1)} %collective-permute-done.2.refs_1_), channel_id=1, source_target_pairs={{0,672},{1,673},{2,674},{3,675},{4,676},{5,677},{6,678},{7,679},{8... | collective-permute-start | bytes 1179656 | tf_op jit(solution)/shard_map/ppermute | solution.py:115
  71.5 10.9 %collective-permute-start.10 = (bf16[2,192,512]{2,1,0:T(8,128)(2,1)S(1)}, bf16[2,192,512]{2,1,0:T(8,128)(2,1)S(1)}, u32[]{:S(2)}, u32[]{:S(2)}) collective-permute-start(bf16[2,192,512]{2,1,0:T(8,128)(2,1)S(1)} %collective-permute-done.9.refs_1_), channel_id=1, source_target_pairs={{0,96},{1,97},{2,98},{3,99},{4,100},{5,101},{6,102},{7,103},{8,104... | collective-permute-start | bytes 1179656 | tf_op jit(solution)/shard_map/ppermute | solution.py:115
  78.8 11.6 %collective-permute-start.4 = (bf16[2,192,512]{2,1,0:T(8,128)(2,1)S(1)}, bf16[2,192,512]{2,1,0:T(8,128)(2,1)S(1)}, u32[]{:S(2)}, u32[]{:S(2)}) collective-permute-start(bf16[2,192,512]{2,1,0:T(8,128)(2,1)S(1)} %collective-permute-done.3.refs_2_), channel_id=1, source_target_pairs={{0,96},{1,97},{2,98},{3,99},{4,100},{5,101},{6,102},{7,103},{8,104... | collective-permute-start | bytes 1179656 | tf_op jit(solution)/shard_map/ppermute | solution.py:115
  82.4 11.8 %collective-permute-start.11 = (bf16[2,192,512]{2,1,0:T(8,128)(2,1)S(1)}, bf16[2,192,512]{2,1,0:T(8,128)(2,1)S(1)}, u32[]{:S(2)}, u32[]{:S(2)}) collective-permute-start(bf16[2,192,512]{2,1,0:T(8,128)(2,1)S(1)} %collective-permute-done.10.refs_2_), channel_id=1, source_target_pairs={{0,672},{1,673},{2,674},{3,675},{4,676},{5,677},{6,678},{7,679},{8... | collective-permute-start | bytes 1179656 | tf_op jit(solution)/shard_map/ppermute | solution.py:115
  91.3 9.2 %collective-permute-start.5 = (bf16[2,192,512]{2,1,0:T(8,128)(2,1)S(1)}, bf16[2,192,512]{2,1,0:T(8,128)(2,1)S(1)}, u32[]{:S(2)}, u32[]{:S(2)}) collective-permute-start(bf16[2,192,512]{2,1,0:T(8,128)(2,1)S(1)} %get-tuple-element.28), channel_id=1, source_target_pairs={{0,96},{1,97},{2,98},{3,99},{4,100},{5,101},{6,102},{7,103},{8,104... | collective-permute-start | bytes 1179656 | tf_op jit(solution)/shard_map/ppermute | solution.py:115
  95.1 11.5 %collective-permute-start.12 = (bf16[2,192,512]{2,1,0:T(8,128)(2,1)S(1)}, bf16[2,192,512]{2,1,0:T(8,128)(2,1)S(1)}, u32[]{:S(2)}, u32[]{:S(2)}) collective-permute-start(bf16[2,192,512]{2,1,0:T(8,128)(2,1)S(1)} %get-tuple-element.37), channel_id=1, source_target_pairs={{0,672},{1,673},{2,674},{3,675},{4,676},{5,677},{6,678},{7,679},{8... | collective-permute-start | bytes 1179656 | tf_op jit(solution)/shard_map/ppermute | solution.py:115
  100.6 14.6 %collective-permute-start.6 = (bf16[2,192,512]{2,1,0:T(8,128)(2,1)S(1)}, bf16[2,192,512]{2,1,0:T(8,128)(2,1)S(1)}, u32[]{:S(2)}, u32[]{:S(2)}) collective-permute-start(bf16[2,192,512]{2,1,0:T(8,128)(2,1)S(1)} %add_convert_fusion.5), channel_id=1, source_target_pairs={{0,672},{1,673},{2,674},{3,675},{4,676},{5,677},{6,678},{7,679},{8... | collective-permute-start | bytes 1179656 | tf_op jit(solution)/shard_map/ppermute | solution.py:115
  106.7 11.0 %collective-permute-start.13 = (bf16[2,192,512]{2,1,0:T(8,128)(2,1)S(1)}, bf16[2,192,512]{2,1,0:T(8,128)(2,1)S(1)}, u32[]{:S(2)}, u32[]{:S(2)}) collective-permute-start(bf16[2,192,512]{2,1,0:T(8,128)(2,1)S(1)} %add_convert_fusion.2), channel_id=1, source_target_pairs={{0,96},{1,97},{2,98},{3,99},{4,100},{5,101},{6,102},{7,103},{8,104... | collective-permute-start | bytes 1179656 | tf_op jit(solution)/shard_map/ppermute | solution.py:115
  115.3 13.0 %collective-permute-start.7 = (bf16[2,192,512]{2,1,0:T(8,128)(2,1)S(1)}, bf16[2,192,512]{2,1,0:T(8,128)(2,1)S(1)}, u32[]{:S(2)}, u32[]{:S(2)}) collective-permute-start(bf16[2,192,512]{2,1,0:T(8,128)(2,1)S(1)} %add_convert_fusion.4), channel_id=1, source_target_pairs={{0,96},{1,97},{2,98},{3,99},{4,100},{5,101},{6,102},{7,103},{8,104... | collective-permute-start | bytes 1179656 | tf_op jit(solution)/shard_map/ppermute | solution.py:115
  117.8 15.2 %collective-permute-start.14 = (bf16[2,192,512]{2,1,0:T(8,128)(2,1)S(1)}, bf16[2,192,512]{2,1,0:T(8,128)(2,1)S(1)}, u32[]{:S(2)}, u32[]{:S(2)}) collective-permute-start(bf16[2,192,512]{2,1,0:T(8,128)(2,1)S(1)} %add_convert_fusion.1), channel_id=1, source_target_pairs={{0,672},{1,673},{2,674},{3,675},{4,676},{5,677},{6,678},{7,679},{8... | collective-permute-start | bytes 1179656 | tf_op jit(solution)/shard_map/ppermute | solution.py:115
  128.5 10.1 %collective-permute-start.8 = (bf16[192,512]{1,0:T(8,128)(2,1)S(1)}, bf16[192,512]{1,0:T(8,128)(2,1)S(1)}, u32[]{:S(2)}, u32[]{:S(2)}) collective-permute-start(bf16[192,512]{1,0:T(8,128)(2,1)S(1)} %slice_bitcast_fusion.1), channel_id=1, source_target_pairs={{0,672},{1,673},{2,674},{3,675},{4,676},{5,677},{6,678},{7,679},{8... | collective-permute-start | bytes 589832 | tf_op jit(solution)/shard_map/ppermute | solution.py:115
  133.2 6.7 %collective-permute-start.15 = (bf16[192,512]{1,0:T(8,128)(2,1)S(1)}, bf16[192,512]{1,0:T(8,128)(2,1)S(1)}, u32[]{:S(2)}, u32[]{:S(2)}) collective-permute-start(bf16[192,512]{1,0:T(8,128)(2,1)S(1)} %slice_bitcast_fusion), channel_id=1, source_target_pairs={{0,96},{1,97},{2,98},{3,99},{4,100},{5,101},{6,102},{7,103},{8,104... | collective-permute-start | bytes 589832 | tf_op jit(solution)/shard_map/ppermute | solution.py:115
  140.3 34.7 %copy-start.3 = (s32[16,8]{0,1:T(8,128)S(1)}, s32[16,8]{0,1:T(8,128)}, u32[]{:S(2)}) copy-start(s32[16,8]{0,1:T(8,128)} %param.8) | copy-start | bytes 1540
  140.3 34.7 %copy-start.4 = (f32[16,8]{0,1:T(8,128)S(1)}, f32[16,8]{0,1:T(8,128)}, u32[]{:S(2)}) copy-start(f32[16,8]{0,1:T(8,128)} %param.9) | copy-start | bytes 1540
